TPU v7x, 32 devices: a whole 2x2x4 slice. The times are simulated.
32 devices in a mesh: dp: 4 (over y, x), tm: 8 (over z, core).
Axes of the slice: x: 2, y: 2, z: 4, core: 2. Of those that a mesh axis runs over, the one named last changes fastest.
Arguments:
- frames: bfloat16 [2, 8, 4096, 512], P(None, 'dp', 'tm'), may hold values from -6 to 6
- lengths: int32 [8], P('dp'), may hold values from 409 to 4096, as said below
- norm_gain: float32 [2, 512], replicated, may hold values from 0.5 to 1.5
- norm_bias: float32 [2, 512], replicated, may hold values from -1.75 to 1.75
- qkv_weight: bfloat16 [512, 1536], replicated, may hold values from -0.25 to 0.25
- qv_bias: float32 [2, 512], replicated, may hold values from -3 to 3
- out_weight: bfloat16 [512, 512], replicated, may hold values from -1 to 1
- out_bias: float32 [512], replicated, may hold values from -1.75 to 1.75
- up_weight: bfloat16 [512, 2048], replicated, may hold values from -0.25 to 0.25
- up_bias: float32 [2048], replicated, may hold values from -3 to 3
- down_weight: bfloat16 [2048, 512], replicated, may hold values from -0.125 to 0.125
- down_bias: float32 [512], replicated, may hold values from -1.75 to 1.75
- cotangent: bfloat16 [2, 8, 4096, 512], P(None, 'dp', 'tm'), may hold values from -6 to 6
Outputs:
- mixed_out: bfloat16 [2, 8, 4096, 512], P(None, 'dp', 'tm')
- frames_grad: bfloat16 [2, 8, 4096, 512], P(None, 'dp', 'tm')
- norm_gain_grad: float32 [2, 512], replicated
- norm_bias_grad: float32 [2, 512], replicated
- qkv_weight_grad: float32 [512, 1536], replicated
- qv_bias_grad: float32 [2, 512], replicated
- out_weight_grad: float32 [512, 512], replicated
- out_bias_grad: float32 [512], replicated
- up_weight_grad: float32 [512, 2048], replicated
- up_bias_grad: float32 [2048], replicated
- down_weight_grad: float32 [2048, 512], replicated
- down_bias_grad: float32 [512], replicated
Inputs may be any that keep to these rules, and one draw needn't show every extreme that they name: `lengths`: in each group of 2 utterances that share an index of dp, one utterance, drawn from the seed, is 4096 frames long.
All inputs are finite; a program needn't handle non-finite values.
Results may differ from a plain program's by a relative error of at most 0.018.
Values may be sent and summed in bfloat16 or wider, within the bound.
No kernel may reach another device: no remote copies, remote signals or barrier semaphores. Data moves between devices by JAX's collectives and lax.ppermute only.
A program may use at most 384 MiB of HBM per device.

v0:
```python
import jax
import jax.numpy as jnp
from jax import lax
from jax.sharding import PartitionSpec as P

HEADS = 8
SEG = 16
LEFT = 30
RC = 4
MEMS = 4


def shifted_2(value, axis, steps):
    count = lax.axis_size(axis)
    initial, last = (max(0, -steps), min(count, count - steps))
    return lax.ppermute(value, axis, [(source, source + steps) for source in range(initial, last)])


def layer_norm(values, norm_scale, norm_shift):
    center = values - jnp.mean(values, axis=-1, keepdims=True)
    spread = jnp.mean(center * center, axis=-1, keepdims=True)
    return center * lax.rsqrt(spread + 1e-05) * norm_scale + norm_shift


def exact_gelu(values):
    return jax.nn.gelu(values, approximate=False)


def dense(values, matrix):
    return jnp.einsum("...d,de->...e", values, matrix, preferred_element_type=jnp.float32)


def dense_back(grads, matrix):
    return jnp.einsum("...e,de->...d", grads, matrix, preferred_element_type=jnp.float32)


def weight_grad(values, grads):
    return jnp.einsum("...d,...e->de", values, grads, preferred_element_type=jnp.float32)


def bias_sum(values):
    return jnp.sum(values.astype(jnp.float32).reshape(-1, values.shape[-1]), axis=0)


def split_heads(values):
    return values.reshape(values.shape[:-1] + (HEADS, values.shape[-1] // HEADS))


def near_window(extended, segments):
    lead_blocks = -(-LEFT // SEG)
    rows_count = extended.shape[0]
    width = extended.shape[-1]
    blocks = extended.reshape(rows_count, lead_blocks + segments + 1, SEG, width)
    stacked = jnp.stack(
        [blocks[:, shift_index : shift_index + segments] for shift_index in range(lead_blocks + 2)],
        2,
    )
    flat = stacked.reshape(rows_count, segments, (lead_blocks + 2) * SEG, width)
    offset = lead_blocks * SEG - LEFT
    return flat[:, :, offset : offset + LEFT + SEG + RC]


def near_window_back(grads, segments):
    lead_blocks = -(-LEFT // SEG)
    rows_count = grads.shape[0]
    width = grads.shape[-1]
    offset = lead_blocks * SEG - LEFT
    padded = jnp.pad(grads, ((0, 0), (0, 0), (offset, SEG - RC), (0, 0)))
    blocks = padded.reshape(rows_count, segments, lead_blocks + 2, SEG, width)
    summed = jnp.zeros((rows_count, lead_blocks + segments + 1, SEG, width), jnp.float32)
    for shift_index in range(lead_blocks + 2):
        summed = summed + jnp.pad(
            blocks[:, :, shift_index],
            ((0, 0), (shift_index, lead_blocks + 1 - shift_index), (0, 0), (0, 0)),
        )
    return summed.reshape(rows_count, (lead_blocks + segments + 1) * SEG, width)


def masked_softmax(scores, key_mask):
    keep_mask = key_mask[:, :, None, None, :]
    shifted = jnp.where(keep_mask, scores, -1000000000.0)
    largest = jnp.max(shifted, axis=-1, keepdims=True)
    raised = jnp.exp(shifted - largest)
    return raised / jnp.sum(raised, axis=-1, keepdims=True)


def attend_forward(queries, keys_in, values_in, key_mask):
    scale_factor = (queries.shape[-1] // HEADS) ** (-0.5)
    scores = (
        jnp.einsum(
            "usqhe,uskhe->ushqk",
            split_heads(queries),
            split_heads(keys_in),
            preferred_element_type=jnp.float32,
        )
        * scale_factor
    )
    probs = masked_softmax(scores, key_mask)
    mixed = jnp.einsum(
        "ushqk,uskhe->usqhe",
        probs.astype(jnp.bfloat16),
        split_heads(values_in),
        preferred_element_type=jnp.float32,
    )
    return (mixed.reshape(queries.shape).astype(jnp.bfloat16), probs)


def attend_backward(grad_out, queries, keys_in, values_in, probs):
    scale_factor = (queries.shape[-1] // HEADS) ** (-0.5)
    heads_out = split_heads(grad_out)
    grad_probs = jnp.einsum(
        "usqhe,uskhe->ushqk", heads_out, split_heads(values_in), preferred_element_type=jnp.float32
    )
    grad_values = jnp.einsum(
        "ushqk,usqhe->uskhe",
        probs.astype(jnp.bfloat16),
        heads_out,
        preferred_element_type=jnp.float32,
    ).reshape(values_in.shape)
    grad_scores = probs * (grad_probs - jnp.sum(probs * grad_probs, axis=-1, keepdims=True))
    score_low = grad_scores.astype(jnp.bfloat16)
    grad_queries = (
        jnp.einsum(
            "ushqk,uskhe->usqhe",
            score_low,
            split_heads(keys_in),
            preferred_element_type=jnp.float32,
        ).reshape(queries.shape)
        * scale_factor
    )
    grad_keys = (
        jnp.einsum(
            "ushqk,usqhe->uskhe",
            score_low,
            split_heads(queries),
            preferred_element_type=jnp.float32,
        ).reshape(keys_in.shape)
        * scale_factor
    )
    return (grad_queries, grad_keys, grad_values)


def local(
    frames,
    lengths,
    norm_gain,
    norm_bias,
    qkv_weight,
    qv_bias,
    out_weight,
    out_bias,
    up_weight,
    up_bias,
    down_weight,
    down_bias,
    cotangent,
):
    micro_count, utterances, frames_dev, width = frames.shape
    segments = frames_dev // SEG
    position = lax.axis_index("tm")
    total_frames = frames_dev * lax.axis_size("tm")
    seg_ids = position * segments + jnp.arange(segments, dtype=jnp.int32)
    lead_blocks = -(-LEFT // SEG)
    own_start = lead_blocks * SEG
    window_ids = (
        seg_ids[:, None] * SEG - LEFT + jnp.arange(LEFT + SEG + RC, dtype=jnp.int32)[None, :]
    )
    inside = (window_ids >= 0) & (window_ids < total_frames)
    near_valid = inside[None] & (
        (window_ids[None] < lengths[:, None, None]) | (window_ids % SEG == 0)[None]
    )
    slots = jnp.arange(MEMS, dtype=jnp.int32)
    window_valid = jnp.broadcast_to(
        (seg_ids[:, None] - MEMS + slots[None, :] >= 0)[None], (utterances, segments, MEMS)
    )
    all_valid = jnp.concatenate([window_valid, near_valid], 2)
    reach = -(-MEMS // segments)
    base = reach * segments
    w_query = qkv_weight[:, :width]
    w_key = qkv_weight[:, width : 2 * width]
    w_value = qkv_weight[:, 2 * width :]
    front_rows = jnp.zeros((utterances, own_start - LEFT, width), jnp.bfloat16)
    back_rows = jnp.zeros((utterances, SEG - RC, width), jnp.bfloat16)

    def forward(inputs):
        normed, norm_one_back = jax.vjp(layer_norm, inputs, norm_gain[0], norm_bias[0])
        normed_low = normed.astype(jnp.bfloat16)
        projected = dense(normed_low, qkv_weight)
        queries = (projected[..., :width] + qv_bias[0]).astype(jnp.bfloat16)
        keys_flat = (
            projected[..., width : 2 * width]
            .astype(jnp.bfloat16)
            .reshape(utterances, frames_dev, width)
        )
        values_flat = (
            (projected[..., 2 * width :] + qv_bias[1])
            .astype(jnp.bfloat16)
            .reshape(utterances, frames_dev, width)
        )
        left_keys, left_values = shifted_2(
            (keys_flat[:, frames_dev - LEFT :], values_flat[:, frames_dev - LEFT :]), "tm", 1
        )
        right_keys, right_values = shifted_2((keys_flat[:, :RC], values_flat[:, :RC]), "tm", -1)
        near_keys = near_window(
            jnp.concatenate([front_rows, left_keys, keys_flat, right_keys, back_rows], 1), segments
        )
        near_values = near_window(
            jnp.concatenate([front_rows, left_values, values_flat, right_values, back_rows], 1),
            segments,
        )
        pooled_low = jnp.mean(normed, axis=2).astype(jnp.bfloat16)
        pooled_query = (dense(pooled_low, w_query) + qv_bias[0]).astype(jnp.bfloat16)
        summary, summary_probs = attend_forward(
            pooled_query[:, :, None], near_keys, near_values, near_valid
        )
        memory = (dense(summary[:, :, 0], out_weight) + out_bias).astype(jnp.bfloat16)
        pieces = [shifted_2(memory, "tm", 1)]
        bank = jnp.concatenate(pieces + [memory], 1)
        bank_proj = dense(bank, qkv_weight[:, width:])
        bank_keys = bank_proj[..., :width].astype(jnp.bfloat16)
        bank_values = (bank_proj[..., width:] + qv_bias[1]).astype(jnp.bfloat16)
        window_keys = jnp.stack(
            [
                bank_keys[:, base + seg_index - MEMS : base + seg_index]
                for seg_index in range(segments)
            ],
            1,
        )
        window_values = jnp.stack(
            [
                bank_values[:, base + seg_index - MEMS : base + seg_index]
                for seg_index in range(segments)
            ],
            1,
        )
        all_keys = jnp.concatenate([window_keys, near_keys], 2)
        all_values = jnp.concatenate([window_values, near_values], 2)
        attended, attend_probs = attend_forward(queries, all_keys, all_values, all_valid)
        mixed = inputs + dense(attended, out_weight) + out_bias
        normed_two, norm_two_back = jax.vjp(layer_norm, mixed, norm_gain[1], norm_bias[1])
        normed_two_low = normed_two.astype(jnp.bfloat16)
        upper = dense(normed_two_low, up_weight) + up_bias
        activated, gelu_back = jax.vjp(exact_gelu, upper)
        activated_low = activated.astype(jnp.bfloat16)
        result = mixed + dense(activated_low, down_weight) + down_bias
        saved = (
            norm_one_back,
            normed_low,
            queries,
            near_keys,
            near_values,
            pooled_low,
            pooled_query,
            summary,
            summary_probs,
            memory,
            all_keys,
            all_values,
            attended,
            attend_probs,
            norm_two_back,
            normed_two_low,
            gelu_back,
            activated_low,
        )
        return (result, saved)

    local_shape = (utterances, segments, SEG, width)
    outputs_list = []
    stored = []
    for micro_index in range(micro_count):
        result, saved = forward(frames[micro_index].reshape(local_shape).astype(jnp.float32))
        outputs_list.append(result.astype(jnp.bfloat16).reshape(utterances, frames_dev, width))
        stored.append(saved)
    totals = None
    input_grads = []
    for micro_index in range(micro_count):
        saved = forward(frames[micro_index].reshape(local_shape).astype(jnp.float32))[1]
        grad_result = cotangent[micro_index].reshape(local_shape)
        (
            backward_norm_one_back,
            backward_normed_low,
            backward_queries,
            backward_near_keys,
            backward_near_values,
            backward_pooled_low,
            backward_pooled_query,
            backward_summary,
            backward_summary_probs,
            backward_memory,
            backward_all_keys,
            backward_all_values,
            backward_attended,
            backward_attend_probs,
            backward_norm_two_back,
            backward_normed_two_low,
            backward_gelu_back,
            backward_activated_low,
        ) = saved
        grad_float = grad_result.astype(jnp.float32)
        down_grad = weight_grad(backward_activated_low, grad_result)
        down_bias_grad = bias_sum(grad_float)
        grad_upper = backward_gelu_back(dense_back(grad_result, down_weight))[0].astype(
            jnp.bfloat16
        )
        up_grad = weight_grad(backward_normed_two_low, grad_upper)
        up_bias_grad = bias_sum(grad_upper)
        mixed_norm, gain_two, shift_two = backward_norm_two_back(dense_back(grad_upper, up_weight))
        grad_mixed = grad_float + mixed_norm
        grad_branch = grad_mixed.astype(jnp.bfloat16)
        out_grad = weight_grad(backward_attended, grad_branch)
        out_bias_grad = bias_sum(grad_branch)
        grad_attended = dense_back(grad_branch, out_weight).astype(jnp.bfloat16)
        grad_queries, grad_all_keys, grad_all_values = attend_backward(
            grad_attended,
            backward_queries,
            backward_all_keys,
            backward_all_values,
            backward_attend_probs,
        )
        bank_key_grad = jnp.zeros((utterances, base + segments, width), jnp.float32)
        bank_value_grad = jnp.zeros((utterances, base + segments, width), jnp.float32)
        for backward_seg_index in range(segments):
            bank_key_grad = bank_key_grad.at[
                :, base + backward_seg_index - MEMS : base + backward_seg_index
            ].add(grad_all_keys[:, backward_seg_index, :MEMS])
            bank_value_grad = bank_value_grad.at[
                :, base + backward_seg_index - MEMS : base + backward_seg_index
            ].add(grad_all_values[:, backward_seg_index, :MEMS])
        memory_key_grad = bank_key_grad[:, base:]
        memory_value_grad = bank_value_grad[:, base:]
        lower = (reach - 1) * segments
        back_keys = shifted_2(
            bank_key_grad[:, lower : lower + segments].astype(jnp.bfloat16), "tm", -1
        ).astype(jnp.float32)
        back_values = shifted_2(
            bank_value_grad[:, lower : lower + segments].astype(jnp.bfloat16), "tm", -1
        ).astype(jnp.float32)
        memory_key_grad = memory_key_grad + back_keys
        memory_value_grad = memory_value_grad + back_values
        mem_key_low = memory_key_grad.astype(jnp.bfloat16)
        mem_value_low = memory_value_grad.astype(jnp.bfloat16)
        key_mem_grad = weight_grad(backward_memory, mem_key_low)
        value_mem_grad = weight_grad(backward_memory, mem_value_low)
        memory_grad = (dense_back(mem_key_low, w_key) + dense_back(mem_value_low, w_value)).astype(
            jnp.bfloat16
        )
        out_grad = out_grad + weight_grad(backward_summary[:, :, 0], memory_grad)
        out_bias_grad = out_bias_grad + bias_sum(memory_grad)
        grad_summary = dense_back(memory_grad, out_weight).astype(jnp.bfloat16)[:, :, None]
        grad_pooled_query, grad_near_keys, grad_near_values = attend_backward(
            grad_summary,
            backward_pooled_query[:, :, None],
            backward_near_keys,
            backward_near_values,
            backward_summary_probs,
        )
        ext_key_grad = near_window_back(grad_near_keys + grad_all_keys[:, :, MEMS:], segments)
        ext_value_grad = near_window_back(grad_near_values + grad_all_values[:, :, MEMS:], segments)
        pooled_grad_low = grad_pooled_query[:, :, 0].astype(jnp.bfloat16)
        query_pool_grad = weight_grad(backward_pooled_low, pooled_grad_low)
        grad_pooled = dense_back(pooled_grad_low, w_query)
        from_right_keys = shifted_2(
            ext_key_grad[:, own_start - LEFT : own_start].astype(jnp.bfloat16), "tm", -1
        ).astype(jnp.float32)
        from_right_values = shifted_2(
            ext_value_grad[:, own_start - LEFT : own_start].astype(jnp.bfloat16), "tm", -1
        ).astype(jnp.float32)
        tail_start = own_start + frames_dev
        from_left_keys = shifted_2(
            ext_key_grad[:, tail_start : tail_start + RC].astype(jnp.bfloat16), "tm", 1
        ).astype(jnp.float32)
        from_left_values = shifted_2(
            ext_value_grad[:, tail_start : tail_start + RC].astype(jnp.bfloat16), "tm", 1
        ).astype(jnp.float32)
        cache_pad = ((0, 0), (frames_dev - LEFT, 0), (0, 0))
        context_pad = ((0, 0), (0, frames_dev - RC), (0, 0))
        key_total = (
            ext_key_grad[:, own_start:tail_start]
            + jnp.pad(from_right_keys, cache_pad)
            + jnp.pad(from_left_keys, context_pad)
        )
        value_total = (
            ext_value_grad[:, own_start:tail_start]
            + jnp.pad(from_right_values, cache_pad)
            + jnp.pad(from_left_values, context_pad)
        )
        query_low = grad_queries.astype(jnp.bfloat16)
        key_low = key_total.astype(jnp.bfloat16).reshape(query_low.shape)
        value_low = value_total.astype(jnp.bfloat16).reshape(query_low.shape)
        grad_projected = jnp.concatenate([query_low, key_low, value_low], -1)
        qkv_grad = weight_grad(backward_normed_low, grad_projected) + jnp.concatenate(
            [query_pool_grad, key_mem_grad, value_mem_grad], 1
        )
        qv_bias_grad = jnp.stack(
            [
                bias_sum(query_low) + bias_sum(pooled_grad_low),
                bias_sum(value_low) + bias_sum(mem_value_low),
            ]
        )
        grad_normed = dense_back(grad_projected, qkv_weight) + grad_pooled[:, :, None] / SEG
        input_norm, gain_one, shift_one = backward_norm_one_back(grad_normed)
        grad_frames = (grad_mixed + input_norm).astype(jnp.bfloat16)
        grads = (
            jnp.stack([gain_one, gain_two]),
            jnp.stack([shift_one, shift_two]),
            qkv_grad,
            qv_bias_grad,
            out_grad,
            out_bias_grad,
            up_grad,
            up_bias_grad,
            down_grad,
            down_bias_grad,
        )
        grad_frames, grads = (grad_frames, grads)
        input_grads.append(grad_frames.reshape(utterances, frames_dev, width))
        totals = (
            grads
            if totals is None
            else tuple((total + grad_part for total, grad_part in zip(totals, grads)))
        )
    totals = lax.psum(
        (
            totals[0],
            totals[1],
            totals[2],
            totals[3],
            totals[4],
            totals[5],
            totals[6],
            totals[7],
            totals[8],
            totals[9],
        ),
        ("dp", "tm"),
    )
    return (
        jnp.stack(outputs_list),
        jnp.stack(input_grads),
        totals[0],
        totals[1],
        totals[2],
        totals[3],
        totals[4],
        totals[5],
        totals[6],
        totals[7],
        totals[8],
        totals[9],
    )


def solution(mesh):
    in_specs = (
        P(None, "dp", "tm", None),
        P("dp"),
        P(),
        P(),
        P(),
        P(),
        P(),
        P(),
        P(),
        P(),
        P(),
        P(),
        P(None, "dp", "tm", None),
    )
    out_specs = (
        P(None, "dp", "tm", None),
        P(None, "dp", "tm", None),
        P(),
        P(),
        P(),
        P(),
        P(),
        P(),
        P(),
        P(),
        P(),
        P(),
    )
    return jax.shard_map(local, mesh=mesh, in_specs=in_specs, out_specs=out_specs, check_vma=False)
```

profile of v0, /device:TPU:0, one launch (start us, length us, event | category | flops | bytes accessed | tf_op | source)
XLA Modules:
  0.0 1282.3 jit_solution(17530893411939426685)
XLA Ops:
  30.3 5.2 collective-permute-start.2
  66.8 5.6 concatenate.311
  76.1 5.6 concatenate.312
  86.8 9.3 reshape.4778
  96.1 6.9 fusion.24
  107.5 9.2 reshape.4775
  129.0 9.7 reshape.4782
  138.6 6.7 fusion.16
  157.3 5.0 fusion.28
  172.0 5.6 concatenate.317
  182.7 9.3 reshape.4779
  192.0 5.0 fusion.20
  203.3 6.0 pad_maximum_fusion.5
  209.3 9.7 reshape.4788
  221.2 6.0 pad_maximum_fusion.4
  227.2 9.5 reshape.4787
  236.7 7.6 fusion.40
  244.2 87.4 %fusion.285 = (f32[2,32,8,16]{3,2,1,0:T(8,128)S(1)}, f32[2,32,8,16,54]{4,3,2,1,0:T(8,128)S(1)}) fusion(f32[2,32,8,16,54]{4,3,2,1,0:T(8,128)S(1)} %fusion.40, pred[2,32,54]{2,1,0:T(8,128)(4,1)S(1)} %copy-done.246), kind=kOutput, calls=%fused_computation.1007 | output fusion | flops 2654261 | bytes 3575168 | tf_op jit(solution)/shard_map/sub | solution.py:83
  331.7 8.0 convert_bitcast_fusion.1
  356.4 9.9 reshape.4790
  366.3 7.5 fusion.32
  381.8 9.5 reshape.4789
  391.2 6.3 convert_bitcast_fusion
  409.2 10.1 convert_reduce_fusion.3
  419.3 42.3 %multiply_convert_fusion.1 = (bf16[2,32,16,2048]{3,2,1,0:T(8,128)(2,1)}, f32[2,32,16,2048]{3,2,1,0:T(8,128)}, bf16[2,32,16,2048]{3,2,1,0:T(8,128)(2,1)}, f32[2,32,16,2048]{3,2,1,0:T(8,128)S(1)}) fusion(f32[2,32,16,2048]{3,2,1,0:T(8,128)} %get-tuple-element.1824, f32[2048]{0:T(1024)S(1)} %copy-done.234, u32[2,16,2048]{2,1,0:T(8,128)S(1)} %get-tuple-element.1549, ...), kind=kLoop, calls=%fused_computation.38 | loop fusion | flops 287309824 | bytes 42999808 | tf_op jit(solution)/shard_map/convert_element_type | solution.py:244
  461.5 11.2 convert_reduce_fusion.5
  472.7 6.7 fusion.251
  479.5 8.5 convert_reduce_fusion.4
  508.3 8.1 multiply_reduce_fusion
  520.3 7.3 multiply_bitcast_fusion
  527.6 12.9 %copy.196 = f32[2,32,54,8,64]{4,3,1,2,0:T(8,128)} copy(f32[2,32,54,8,64]{4,2,3,1,0:T(8,128)} %multiply_bitcast_fusion) | data formatting | bytes 14155776 | tf_op jit(solution)/shard_map/mul | solution.py:132
  540.5 12.5 mul.536
  559.0 10.5 convolution_bitcast_fusion
  569.6 12.9 %copy.229 = f32[2,32,54,8,64]{4,3,1,2,0:T(8,128)} copy(f32[2,32,54,8,64]{4,2,3,1,0:T(8,128)} %convolution_bitcast_fusion) | data formatting | bytes 14155776 | tf_op jit(solution)/shard_map/ushqk,usqhe->uskhe/transpose | solution.py:114
  582.5 12.5 reshape.4692
  609.4 8.0 multiply_reduce_fusion.1
  621.2 7.5 multiply_bitcast_fusion.1
  628.7 12.9 %copy.118 = f32[2,32,54,8,64]{4,3,1,2,0:T(8,128)} copy(f32[2,32,54,8,64]{4,2,3,1,0:T(8,128)} %multiply_bitcast_fusion.1) | data formatting | bytes 14155776 | tf_op jit(solution)/shard_map/mul | solution.py:132
  641.6 12.5 mul.506
  659.9 10.3 convolution_bitcast_fusion.1
  670.2 12.9 %copy.151 = f32[2,32,54,8,64]{4,3,1,2,0:T(8,128)} copy(f32[2,32,54,8,64]{4,2,3,1,0:T(8,128)} %convolution_bitcast_fusion.1) | data formatting | bytes 14155776 | tf_op jit(solution)/shard_map/ushqk,usqhe->uskhe/transpose | solution.py:114
  683.2 12.9 %reshape.4620 = f32[2,32,54,512]{3,1,2,0:T(8,128)} reshape(f32[2,32,54,8,64]{4,3,1,2,0:T(8,128)} %copy.151) | data formatting | bytes 14155776 | tf_op jit(solution)/shard_map/reshape | solution.py:119
  702.2 7.2 convert_reduce_fusion.7
  709.5 7.2 convert_reduce_fusion.6
  799.1 7.5 fusion.18
  814.1 6.8 fusion.26
  830.3 7.5 multiply_bitcast_fusion.5
  837.8 11.9 mul.511
  849.6 6.5 slice_add_fusion.3
  865.0 7.5 multiply_bitcast_fusion.3
  872.5 12.1 mul.541
  884.6 6.4 slice_add_fusion.1
  905.0 5.6 collective-permute-start.13
  910.6 7.7 multiply_bitcast_fusion.4
  918.3 11.6 reshape.4656
  929.9 6.4 slice_add_fusion.2
  956.4 7.7 multiply_bitcast_fusion.2
  964.1 11.7 reshape.4728
  975.8 6.5 slice_add_fusion
  992.0 5.1 fusion.14
  1029.5 5.9 add_convert_fusion.6
  1042.4 5.4 multiply_reduce_fusion.8
  1054.1 43.5 %all-reduce.32 = (f32[2,512]{1,0:T(2,128)}, f32[2,512]{1,0:T(2,128)}, f32[2,512]{1,0:T(2,128)}, f32[512]{0:T(512)}, f32[2048]{0:T(1024)}, /*index=5*/f32[512]{0:T(512)}) all-reduce(f32[2,512]{1,0:T(2,128)S(1)} %maximum_add_fusion, f32[2,512]{1,0:T(2,128)S(1)} %maximum_add_fusion.1, ...), channel_id=1, replica_groups=mesh['dp'=4,'tm'=8] {'dp','tm'}, use_global_device_ids=true, to_apply=%region_34.35 | all-reduce | flops 6144 | bytes 49152 | tf_op jit(solution)/shard_map/psum | solution.py:423
  1102.0 162.4 %all-reduce.36.cloned.1.call-done = (f32[512,1536]{1,0:T(8,128)}, f32[512,512]{1,0:T(8,128)}, f32[512,2048]{1,0:T(8,128)}, f32[2048,512]{1,0:T(8,128)}) async-done(((f32[512,1536]{1,0:T(8,128)}, f32[512,512]{1,0:T(8,128)}, f32[512,2048]{1,0:T(8,128)}, f32[2048,512]{1,0:T(8,128)}), (f32[512,1536]{1,0:T(8,128)}, f32[512,512]{1,0:T(8,128)}, f32[512,2048]{1,0:T(8,128)}, ...) | async-done | bytes 12582928 | tf_op jit(solution)/shard_map/psum | solution.py:423
  (1150 shorter events, 419.1 us)
Async XLA Ops:
  7.2 399.5 %copy-start = (bf16[512,2048]{1,0:T(8,128)(2,1)S(1)}, bf16[512,2048]{1,0:T(8,128)(2,1)}, u32[]{:S(2)}) copy-start(bf16[512,2048]{1,0:T(8,128)(2,1)} %param.277) | copy-start | bytes 6291460
  7.2 1257.2 %all-reduce.36.cloned.1.call-start = ((), (), s32[]{:S(2)}) async-start(), calls=%async_computation | async-start | bytes 25165824 | tf_op jit(solution)/shard_map/psum | solution.py:423
  12.3 30.2 %copy-start.137 = (f32[2,32,16]{2,1,0:T(8,128)}, f32[2,32,16]{2,1,0:T(8,128)S(1)}, u32[]{:S(2)}) copy-start(f32[2,32,16]{2,1,0:T(8,128)S(1)} %div.149) | copy-start | bytes 12292
  14.8 27.8 %copy-start.130 = (f32[2,32,16]{2,1,0:T(8,128)}, f32[2,32,16]{2,1,0:T(8,128)S(1)}, u32[]{:S(2)}) copy-start(f32[2,32,16]{2,1,0:T(8,128)S(1)} %div.159) | copy-start | bytes 12292
  14.9 27.6 %copy-start.139 = (f32[2,32,16]{2,1,0:T(8,128)}, f32[2,32,16]{2,1,0:T(8,128)S(1)}, u32[]{:S(2)}) copy-start(f32[2,32,16]{2,1,0:T(8,128)S(1)} %rsqrt.44) | copy-start | bytes 12292
  14.9 27.6 %copy-start.229 = (f32[1,512]{1,0:T(1,128)}, f32[1,512]{1,0:T(1,128)S(1)}, u32[]{:S(2)}) copy-start(f32[1,512]{1,0:T(1,128)S(1)} %get-tuple-element.1797) | copy-start | bytes 6148
  15.0 27.6 %copy-start.242 = (f32[1,512]{1,0:T(1,128)}, f32[1,512]{1,0:T(1,128)S(1)}, u32[]{:S(2)}) copy-start(f32[1,512]{1,0:T(1,128)S(1)} %get-tuple-element.1799) | copy-start | bytes 6148
  15.0 457.8 %copy-start.227 = (f32[1,512]{1,0:T(1,128)}, f32[1,512]{1,0:T(1,128)S(1)}, u32[]{:S(2)}) copy-start(f32[1,512]{1,0:T(1,128)S(1)} %get-tuple-element.1798) | copy-start | bytes 6148
  15.6 27.0 %copy-start.132 = (f32[2,32,16]{2,1,0:T(8,128)}, f32[2,32,16]{2,1,0:T(8,128)S(1)}, u32[]{:S(2)}) copy-start(f32[2,32,16]{2,1,0:T(8,128)S(1)} %rsqrt.46) | copy-start | bytes 12292
  24.3 26.3 %copy-start.63 = (bf16[2,32,16,512]{3,2,1,0:T(8,128)(2,1)}, bf16[2,32,16,512]{3,2,1,0:T(8,128)(2,1)S(1)}, u32[]{:S(2)}) copy-start(bf16[2,32,16,512]{3,2,1,0:T(8,128)(2,1)S(1)} %get-tuple-element.1764) | copy-start | bytes 3145732
  25.0 37.5 %collective-permute-start = (bf16[2,30,512]{2,1,0:T(8,128)(2,1)}, bf16[2,30,512]{2,1,0:T(8,128)(2,1)}, u32[]{:S(2)}, u32[]{:S(2)}) collective-permute-start(bf16[2,30,512]{2,1,0:T(8,128)(2,1)} %slice.4848), channel_id=1, source_target_pairs={{0,1},{1,2},{2,3},{3,4},{4,5},{5,6},{6,7},{8,9},{9,10},{10,11},{11... | collective-permute-start | bytes 184328 | tf_op jit(solution)/shard_map/ppermute | solution.py:16
  28.1 33.1 %collective-permute-start.1 = (bf16[2,4,512]{2,1,0:T(4,128)(2,1)S(1)}, bf16[2,4,512]{2,1,0:T(4,128)(2,1)S(1)}, u32[]{:S(2)}, u32[]{:S(2)}) collective-permute-start(bf16[2,4,512]{2,1,0:T(4,128)(2,1)S(1)} %slice.4849), channel_id=1, source_target_pairs={{1,0},{2,1},{3,2},{4,3},{5,4},{6,5},{7,6},{9,8},{10,9},{11,10},{12... | collective-permute-start | bytes 24584 | tf_op jit(solution)/shard_map/ppermute | solution.py:16
  30.3 45.9 %collective-permute-start.2 = (bf16[2,30,512]{2,1,0:T(8,128)(2,1)}, bf16[2,30,512]{2,1,0:T(8,128)(2,1)}, u32[]{:S(2)}, u32[]{:S(2)}) collective-permute-start(bf16[2,30,512]{2,1,0:T(8,128)(2,1)} %slice.4856), channel_id=1, source_target_pairs={{0,1},{1,2},{2,3},{3,4},{4,5},{5,6},{6,7},{8,9},{9,10},{10,11},{11... | collective-permute-start | bytes 184328 | tf_op jit(solution)/shard_map/ppermute | solution.py:16
  36.1 38.5 %collective-permute-start.3 = (bf16[2,4,512]{2,1,0:T(4,128)(2,1)}, bf16[2,4,512]{2,1,0:T(4,128)(2,1)}, u32[]{:S(2)}, u32[]{:S(2)}) collective-permute-start(bf16[2,4,512]{2,1,0:T(4,128)(2,1)} %slice.4857), channel_id=1, source_target_pairs={{1,0},{2,1},{3,2},{4,3},{5,4},{6,5},{7,6},{9,8},{10,9},{11,10},{12... | collective-permute-start | bytes 24584 | tf_op jit(solution)/shard_map/ppermute | solution.py:16
  38.3 80.8 %collective-permute-start.7 = (bf16[2,30,512]{2,1,0:T(8,128)(2,1)}, bf16[2,30,512]{2,1,0:T(8,128)(2,1)}, u32[]{:S(2)}, u32[]{:S(2)}) collective-permute-start(bf16[2,30,512]{2,1,0:T(8,128)(2,1)} %slice.4938), channel_id=1, source_target_pairs={{0,1},{1,2},{2,3},{3,4},{4,5},{5,6},{6,7},{8,9},{9,10},{10,11},{11... | collective-permute-start | bytes 184328 | tf_op jit(solution)/shard_map/ppermute | solution.py:16
  49.2 103.1 %copy-start.111 = (pred[2,32,50]{1,2,0:T(8,128)(4,1)}, pred[2,32,50]{1,2,0:T(8,128)(4,1)S(1)}, u32[]{:S(2)}) copy-start(pred[2,32,50]{1,2,0:T(8,128)(4,1)S(1)} %copy.84) | copy-start | bytes 9604
  61.2 57.8 %collective-permute-start.8 = (bf16[2,4,512]{2,1,0:T(4,128)(2,1)S(1)}, bf16[2,4,512]{2,1,0:T(4,128)(2,1)S(1)}, u32[]{:S(2)}, u32[]{:S(2)}) collective-permute-start(bf16[2,4,512]{2,1,0:T(4,128)(2,1)S(1)} %slice.4939), channel_id=1, source_target_pairs={{1,0},{2,1},{3,2},{4,3},{5,4},{6,5},{7,6},{9,8},{10,9},{11,10},{12... | collective-permute-start | bytes 24584 | tf_op jit(solution)/shard_map/ppermute | solution.py:16
  62.5 109.5 %collective-permute-start.5 = (bf16[2,30,512]{2,1,0:T(8,128)(2,1)}, bf16[2,30,512]{2,1,0:T(8,128)(2,1)}, u32[]{:S(2)}, u32[]{:S(2)}) collective-permute-start(bf16[2,30,512]{2,1,0:T(8,128)(2,1)} %slice.4930), channel_id=1, source_target_pairs={{0,1},{1,2},{2,3},{3,4},{4,5},{5,6},{6,7},{8,9},{9,10},{10,11},{11... | collective-permute-start | bytes 184328 | tf_op jit(solution)/shard_map/ppermute | solution.py:16
  74.6 97.4 %collective-permute-start.6 = (bf16[2,4,512]{2,1,0:T(4,128)(2,1)}, bf16[2,4,512]{2,1,0:T(4,128)(2,1)}, u32[]{:S(2)}, u32[]{:S(2)}) collective-permute-start(bf16[2,4,512]{2,1,0:T(4,128)(2,1)} %slice.4931), channel_id=1, source_target_pairs={{1,0},{2,1},{3,2},{4,3},{5,4},{6,5},{7,6},{9,8},{10,9},{11,10},{12... | collective-permute-start | bytes 24584 | tf_op jit(solution)/shard_map/ppermute | solution.py:16
  165.8 35.4 %copy-start.95 = (bf16[2,32,512]{2,1,0:T(8,128)(2,1)}, bf16[2,32,512]{2,1,0:T(8,128)(2,1)S(1)}, u32[]{:S(2)}) copy-start(bf16[2,32,512]{2,1,0:T(8,128)(2,1)S(1)} %fusion.135) | copy-start | bytes 196612
  165.8 35.4 %collective-permute-start.4 = (bf16[2,32,512]{2,1,0:T(8,128)(2,1)S(1)}, bf16[2,32,512]{2,1,0:T(8,128)(2,1)}, u32[]{:S(2)}, u32[]{:S(2)}) collective-permute-start(bf16[2,32,512]{2,1,0:T(8,128)(2,1)S(1)} %fusion.135), channel_id=1, source_target_pairs={{0,1},{1,2},{2,3},{3,4},{4,5},{5,6},{6,7},{8,9},{9,10},{10,11},{11... | collective-permute-start | bytes 196616 | tf_op jit(solution)/shard_map/ppermute | solution.py:16
  197.4 21.6 %collective-permute-start.9 = (bf16[2,32,512]{2,1,0:T(8,128)(2,1)S(1)}, bf16[2,32,512]{2,1,0:T(8,128)(2,1)}, u32[]{:S(2)}, u32[]{:S(2)}) collective-permute-start(bf16[2,32,512]{2,1,0:T(8,128)(2,1)S(1)} %fusion.137), channel_id=1, source_target_pairs={{0,1},{1,2},{2,3},{3,4},{4,5},{5,6},{6,7},{8,9},{9,10},{10,11},{11... | collective-permute-start | bytes 196616 | tf_op jit(solution)/shard_map/ppermute | solution.py:16
  406.3 90.1 %copy-start.11 = (f32[2,32,16,512]{3,2,1,0:T(8,128)}, f32[2,32,16,512]{3,2,1,0:T(8,128)S(1)}, u32[]{:S(2)}) copy-start(f32[2,32,16,512]{3,2,1,0:T(8,128)S(1)} %get-tuple-element.1823) | copy-start | bytes 6291460
  419.3 42.3 %copy-start.47 = (bf16[1,2,512,512]{3,2,1,0:T(8,128)(2,1)S(1)}, bf16[1,2,512,512]{3,2,1,0:T(8,128)(2,1)}, u32[]{:S(2)}) copy-start(bf16[1,2,512,512]{3,2,1,0:T(8,128)(2,1)} %get-tuple-element.1765) | copy-start | bytes 3145732
  721.6 23.7 %copy-start.178 = (f32[2,1,4,512]{3,1,2,0:T(1,128)S(1)}, f32[2,1,4,512]{3,1,2,0:T(1,128)}, u32[]{:S(2)}) copy-start(f32[2,1,4,512]{3,1,2,0:T(1,128)} %get-tuple-element.1732) | copy-start | bytes 49156
  721.6 23.9 %copy-start.177 = (f32[2,1,4,512]{3,1,2,0:T(1,128)S(1)}, f32[2,1,4,512]{3,1,2,0:T(1,128)}, u32[]{:S(2)}) copy-start(f32[2,1,4,512]{3,1,2,0:T(1,128)} %get-tuple-element.1731) | copy-start | bytes 49156
  721.7 23.9 %copy-start.176 = (f32[2,1,4,512]{3,1,2,0:T(1,128)S(1)}, f32[2,1,4,512]{3,1,2,0:T(1,128)}, u32[]{:S(2)}) copy-start(f32[2,1,4,512]{3,1,2,0:T(1,128)} %get-tuple-element.1730) | copy-start | bytes 49156
  721.7 24.9 %copy-start.175 = (f32[2,1,4,512]{3,1,2,0:T(1,128)S(1)}, f32[2,1,4,512]{3,1,2,0:T(1,128)}, u32[]{:S(2)}) copy-start(f32[2,1,4,512]{3,1,2,0:T(1,128)} %get-tuple-element.1729) | copy-start | bytes 49156
  726.4 33.3 %copy-start.174 = (f32[2,1,4,512]{3,1,2,0:T(1,128)S(1)}, f32[2,1,4,512]{3,1,2,0:T(1,128)}, u32[]{:S(2)}) copy-start(f32[2,1,4,512]{3,1,2,0:T(1,128)} %get-tuple-element.1651) | copy-start | bytes 49156
  726.6 33.1 %copy-start.173 = (f32[2,1,4,512]{3,1,2,0:T(1,128)S(1)}, f32[2,1,4,512]{3,1,2,0:T(1,128)}, u32[]{:S(2)}) copy-start(f32[2,1,4,512]{3,1,2,0:T(1,128)} %get-tuple-element.1650) | copy-start | bytes 49156
  726.9 33.0 %copy-start.172 = (f32[2,1,4,512]{3,1,2,0:T(1,128)S(1)}, f32[2,1,4,512]{3,1,2,0:T(1,128)}, u32[]{:S(2)}) copy-start(f32[2,1,4,512]{3,1,2,0:T(1,128)} %get-tuple-element.1649) | copy-start | bytes 49156
  726.9 33.3 %copy-start.171 = (f32[2,1,4,512]{3,1,2,0:T(1,128)S(1)}, f32[2,1,4,512]{3,1,2,0:T(1,128)}, u32[]{:S(2)}) copy-start(f32[2,1,4,512]{3,1,2,0:T(1,128)} %get-tuple-element.1648) | copy-start | bytes 49156
  727.1 33.3 %copy-start.170 = (f32[2,1,4,512]{3,1,2,0:T(1,128)S(1)}, f32[2,1,4,512]{3,1,2,0:T(1,128)}, u32[]{:S(2)}) copy-start(f32[2,1,4,512]{3,1,2,0:T(1,128)} %get-tuple-element.1647) | copy-start | bytes 49156
  727.4 33.0 %copy-start.169 = (f32[2,1,4,512]{3,1,2,0:T(1,128)S(1)}, f32[2,1,4,512]{3,1,2,0:T(1,128)}, u32[]{:S(2)}) copy-start(f32[2,1,4,512]{3,1,2,0:T(1,128)} %get-tuple-element.1646) | copy-start | bytes 49156
  727.6 33.0 %copy-start.168 = (f32[2,1,4,512]{3,1,2,0:T(1,128)S(1)}, f32[2,1,4,512]{3,1,2,0:T(1,128)}, u32[]{:S(2)}) copy-start(f32[2,1,4,512]{3,1,2,0:T(1,128)} %get-tuple-element.1645) | copy-start | bytes 49156
  727.7 33.3 %copy-start.167 = (f32[2,1,4,512]{3,1,2,0:T(1,128)S(1)}, f32[2,1,4,512]{3,1,2,0:T(1,128)}, u32[]{:S(2)}) copy-start(f32[2,1,4,512]{3,1,2,0:T(1,128)} %get-tuple-element.1644) | copy-start | bytes 49156
  727.9 33.3 %copy-start.166 = (f32[2,1,4,512]{3,1,2,0:T(1,128)S(1)}, f32[2,1,4,512]{3,1,2,0:T(1,128)}, u32[]{:S(2)}) copy-start(f32[2,1,4,512]{3,1,2,0:T(1,128)} %get-tuple-element.1643) | copy-start | bytes 49156
  728.1 33.0 %copy-start.165 = (f32[2,1,4,512]{3,1,2,0:T(1,128)S(1)}, f32[2,1,4,512]{3,1,2,0:T(1,128)}, u32[]{:S(2)}) copy-start(f32[2,1,4,512]{3,1,2,0:T(1,128)} %get-tuple-element.1642) | copy-start | bytes 49156
  728.4 33.0 %copy-start.164 = (f32[2,1,4,512]{3,1,2,0:T(1,128)S(1)}, f32[2,1,4,512]{3,1,2,0:T(1,128)}, u32[]{:S(2)}) copy-start(f32[2,1,4,512]{3,1,2,0:T(1,128)} %get-tuple-element.1641) | copy-start | bytes 49156
  728.4 33.3 %copy-start.163 = (f32[2,1,4,512]{3,1,2,0:T(1,128)S(1)}, f32[2,1,4,512]{3,1,2,0:T(1,128)}, u32[]{:S(2)}) copy-start(f32[2,1,4,512]{3,1,2,0:T(1,128)} %get-tuple-element.1640) | copy-start | bytes 49156
  728.6 33.3 %copy-start.162 = (f32[2,1,4,512]{3,1,2,0:T(1,128)S(1)}, f32[2,1,4,512]{3,1,2,0:T(1,128)}, u32[]{:S(2)}) copy-start(f32[2,1,4,512]{3,1,2,0:T(1,128)} %get-tuple-element.1639) | copy-start | bytes 49156
  729.5 32.4 %copy-start.161 = (f32[2,1,4,512]{3,1,2,0:T(1,128)S(1)}, f32[2,1,4,512]{3,1,2,0:T(1,128)}, u32[]{:S(2)}) copy-start(f32[2,1,4,512]{3,1,2,0:T(1,128)} %get-tuple-element.1638) | copy-start | bytes 49156
  729.7 32.5 %copy-start.160 = (f32[2,1,4,512]{3,1,2,0:T(1,128)S(1)}, f32[2,1,4,512]{3,1,2,0:T(1,128)}, u32[]{:S(2)}) copy-start(f32[2,1,4,512]{3,1,2,0:T(1,128)} %get-tuple-element.1637) | copy-start | bytes 49156
  730.4 66.7 %collective-permute-start.16 = (bf16[2,32,512]{2,1,0:T(8,128)(2,1)}, bf16[2,32,512]{2,1,0:T(8,128)(2,1)S(1)}, u32[]{:S(2)}, u32[]{:S(2)}) collective-permute-start(bf16[2,32,512]{2,1,0:T(8,128)(2,1)} %slice.6018), channel_id=1, source_target_pairs={{1,0},{2,1},{3,2},{4,3},{5,4},{6,5},{7,6},{9,8},{10,9},{11,10},{12... | collective-permute-start | bytes 196616 | tf_op jit(solution)/shard_map/ppermute | solution.py:16
  742.8 23.9 %copy-start.207 = (f32[2,1,4,512]{3,1,2,0:T(1,128)S(1)}, f32[2,1,4,512]{3,1,2,0:T(1,128)}, u32[]{:S(2)}) copy-start(f32[2,1,4,512]{3,1,2,0:T(1,128)} %get-tuple-element.1688) | copy-start | bytes 49156
  742.8 23.9 %copy-start.206 = (f32[2,1,4,512]{3,1,2,0:T(1,128)S(1)}, f32[2,1,4,512]{3,1,2,0:T(1,128)}, u32[]{:S(2)}) copy-start(f32[2,1,4,512]{3,1,2,0:T(1,128)} %get-tuple-element.1687) | copy-start | bytes 49156
  743.1 23.9 %copy-start.205 = (f32[2,1,4,512]{3,1,2,0:T(1,128)S(1)}, f32[2,1,4,512]{3,1,2,0:T(1,128)}, u32[]{:S(2)}) copy-start(f32[2,1,4,512]{3,1,2,0:T(1,128)} %get-tuple-element.1686) | copy-start | bytes 49156
  743.1 24.1 %copy-start.204 = (f32[2,1,4,512]{3,1,2,0:T(1,128)S(1)}, f32[2,1,4,512]{3,1,2,0:T(1,128)}, u32[]{:S(2)}) copy-start(f32[2,1,4,512]{3,1,2,0:T(1,128)} %get-tuple-element.1685) | copy-start | bytes 49156
  743.4 24.1 %copy-start.159 = (f32[2,1,4,512]{3,1,2,0:T(1,128)S(1)}, f32[2,1,4,512]{3,1,2,0:T(1,128)}, u32[]{:S(2)}) copy-start(f32[2,1,4,512]{3,1,2,0:T(1,128)} %get-tuple-element.1683) | copy-start | bytes 49156
  743.7 23.9 %copy-start.158 = (f32[2,1,4,512]{3,1,2,0:T(1,128)S(1)}, f32[2,1,4,512]{3,1,2,0:T(1,128)}, u32[]{:S(2)}) copy-start(f32[2,1,4,512]{3,1,2,0:T(1,128)} %get-tuple-element.1682) | copy-start | bytes 49156
  743.9 23.8 %copy-start.157 = (f32[2,1,4,512]{3,1,2,0:T(1,128)S(1)}, f32[2,1,4,512]{3,1,2,0:T(1,128)}, u32[]{:S(2)}) copy-start(f32[2,1,4,512]{3,1,2,0:T(1,128)} %get-tuple-element.1681) | copy-start | bytes 49156
  747.4 47.6 %collective-permute-start.17 = (bf16[2,32,512]{2,1,0:T(8,128)(2,1)}, bf16[2,32,512]{2,1,0:T(8,128)(2,1)}, u32[]{:S(2)}, u32[]{:S(2)}) collective-permute-start(bf16[2,32,512]{2,1,0:T(8,128)(2,1)} %slice.6017), channel_id=1, source_target_pairs={{1,0},{2,1},{3,2},{4,3},{5,4},{6,5},{7,6},{9,8},{10,9},{11,10},{12... | collective-permute-start | bytes 196616 | tf_op jit(solution)/shard_map/ppermute | solution.py:16
  763.9 48.2 %collective-permute-start.10 = (bf16[2,32,512]{2,1,0:T(8,128)(2,1)}, bf16[2,32,512]{2,1,0:T(8,128)(2,1)S(1)}, u32[]{:S(2)}, u32[]{:S(2)}) collective-permute-start(bf16[2,32,512]{2,1,0:T(8,128)(2,1)} %slice.6020), channel_id=1, source_target_pairs={{1,0},{2,1},{3,2},{4,3},{5,4},{6,5},{7,6},{9,8},{10,9},{11,10},{12... | collective-permute-start | bytes 196616 | tf_op jit(solution)/shard_map/ppermute | solution.py:16
  781.1 25.5 %collective-permute-start.11 = (bf16[2,32,512]{2,1,0:T(8,128)(2,1)}, bf16[2,32,512]{2,1,0:T(8,128)(2,1)}, u32[]{:S(2)}, u32[]{:S(2)}) collective-permute-start(bf16[2,32,512]{2,1,0:T(8,128)(2,1)} %slice.6019), channel_id=1, source_target_pairs={{1,0},{2,1},{3,2},{4,3},{5,4},{6,5},{7,6},{9,8},{10,9},{11,10},{12... | collective-permute-start | bytes 196616 | tf_op jit(solution)/shard_map/ppermute | solution.py:16
  903.7 108.8 %collective-permute-start.12 = (bf16[2,30,512]{2,1,0:T(8,128)(2,1)}, bf16[2,30,512]{2,1,0:T(8,128)(2,1)}, u32[]{:S(2)}, u32[]{:S(2)}) collective-permute-start(bf16[2,30,512]{2,1,0:T(8,128)(2,1)} %slice.5145), channel_id=1, source_target_pairs={{1,0},{2,1},{3,2},{4,3},{5,4},{6,5},{7,6},{9,8},{10,9},{11,10},{12... | collective-permute-start | bytes 184328 | tf_op jit(solution)/shard_map/ppermute | solution.py:16
  905.0 103.9 %collective-permute-start.13 = (bf16[2,4,512]{2,1,0:T(4,128)(2,1)S(1)}, bf16[2,4,512]{2,1,0:T(4,128)(2,1)S(1)}, u32[]{:S(2)}, u32[]{:S(2)}) collective-permute-start(bf16[2,4,512]{2,1,0:T(4,128)(2,1)S(1)} %slice.5146), channel_id=1, source_target_pairs={{0,1},{1,2},{2,3},{3,4},{4,5},{5,6},{6,7},{8,9},{9,10},{10,11},{11... | collective-permute-start | bytes 24584 | tf_op jit(solution)/shard_map/ppermute | solution.py:16
  944.5 74.1 %collective-permute-start.14 = (bf16[2,30,512]{2,1,0:T(8,128)(2,1)}, bf16[2,30,512]{2,1,0:T(8,128)(2,1)}, u32[]{:S(2)}, u32[]{:S(2)}) collective-permute-start(bf16[2,30,512]{2,1,0:T(8,128)(2,1)} %slice.5153), channel_id=1, source_target_pairs={{1,0},{2,1},{3,2},{4,3},{5,4},{6,5},{7,6},{9,8},{10,9},{11,10},{12... | collective-permute-start | bytes 184328 | tf_op jit(solution)/shard_map/ppermute | solution.py:16
  954.2 67.8 %collective-permute-start.18 = (bf16[2,30,512]{2,1,0:T(8,128)(2,1)}, bf16[2,30,512]{2,1,0:T(8,128)(2,1)}, u32[]{:S(2)}, u32[]{:S(2)}) collective-permute-start(bf16[2,30,512]{2,1,0:T(8,128)(2,1)} %slice.5289), channel_id=1, source_target_pairs={{1,0},{2,1},{3,2},{4,3},{5,4},{6,5},{7,6},{9,8},{10,9},{11,10},{12... | collective-permute-start | bytes 184328 | tf_op jit(solution)/shard_map/ppermute | solution.py:16
  1004.0 11.1 collective-permute-start.15
  1008.9 13.0 %collective-permute-start.19 = (bf16[2,4,512]{2,1,0:T(4,128)(2,1)S(1)}, bf16[2,4,512]{2,1,0:T(4,128)(2,1)S(1)}, u32[]{:S(2)}, u32[]{:S(2)}) collective-permute-start(bf16[2,4,512]{2,1,0:T(4,128)(2,1)S(1)} %slice.5290), channel_id=1, source_target_pairs={{0,1},{1,2},{2,3},{3,4},{4,5},{5,6},{6,7},{8,9},{9,10},{10,11},{11... | collective-permute-start | bytes 24584 | tf_op jit(solution)/shard_map/ppermute | solution.py:16
  1012.6 10.6 collective-permute-start.20
  1015.1 8.1 collective-permute-start.21
  1050.3 47.3 %copy-start.46 = (bf16[1,2,512,512]{3,2,1,0:T(8,128)(2,1)S(1)}, bf16[1,2,512,512]{3,2,1,0:T(8,128)(2,1)}, u32[]{:S(2)}) copy-start(bf16[1,2,512,512]{3,2,1,0:T(8,128)(2,1)} %get-tuple-element.1766) | copy-start | bytes 3145732
  1050.3 47.3 %copy-start.142 = (f32[2,32,16]{2,1,0:T(8,128)S(1)}, f32[2,32,16]{2,1,0:T(8,128)}, u32[]{:S(2)}) copy-start(f32[2,32,16]{2,1,0:T(8,128)} %copy-done.141) | copy-start | bytes 12292
  (220 other events, 1649.0 us)
Sparse Core Ops, SparseCore 0:
  1029.0 235.3 all-reduce.35
where the time goes:
time: 1300 us; the launch traced here: 1280 us
  local copies, waits for them, and re-layouts  436 us (34%)
  other arithmetic  297 us (23%)
  matrix products  264 us (20%)
  waiting for transfers between devices  162 us (12%)
  starting transfers between devices  58 us (4%)
  blocking collectives  43.5 us (3%)
  between operations  20.4 us (2%)
    psum x1, waiting for transfers between devices, local(): lax.psum((totals[0], totals[1], totals[2], totals[3], totals[4], totals[5...  162 us
    sub x2, other arithmetic, masked_softmax(): raised = jnp.exp(shifted - largest)  90.8 us
    reshape x12, local copies, waits for them, and re-layouts, split_heads(): values.reshape(values.shape[:-1] + (HEADS, values.shape[-1] // HEADS))  87.9 us
    mul x6, local copies, waits for them, and re-layouts, attend_backward(): jnp.einsum('ushqk,usqhe->uskhe', score_low, split_heads(queries), preferr...  74.8 us
    ppermute x22, starting transfers between devices, shifted_2(): lax.ppermute(value, axis, [(source, source + steps) for source in range(i...  58 us
    reshape x4, local copies, waits for them, and re-layouts, attend_backward(): grad_values = jnp.einsum('ushqk,usqhe->uskhe', probs.astype(jnp.bfloat16)...  48.7 us
    dot_general x16, matrix products, dense_back(): jnp.einsum('...e,de->...d', grads, matrix, preferred_element_type=jnp.flo...  44.6 us
    psum x1, blocking collectives, local(): lax.psum((totals[0], totals[1], totals[2], totals[3], totals[4], totals[5...  43.5 us
  transfers between devices with their start and end apart: 23, of which 1 were waited for; matrix products, arithmetic and copies ran while one was open for 28% of the time, Pallas kernels for 0%

commit v1 on v0

v1 whole, which is shorter than its diff:
```python
import functools

import jax
import jax.numpy as jnp
import numpy as np
from jax import lax
from jax.experimental import pallas as pl
from jax.experimental.pallas import tpu as pltpu
from jax.sharding import PartitionSpec as P

HEADS = 8
SEG = 16
LEFT = 30
RC = 4
MEMS = 4
D = 512
HD = D // HEADS
GROUP = 4
GQ = GROUP * SEG
NEAR = 112
MEMK = 16
KEYS = MEMK + NEAR
HL = 96
HR = 16
HALO = HL + HR
OWN0 = HL - 32
SCALE = HD**-0.5
NEG = -1000000000.0
MB = 1024 * 1024

f32 = jnp.float32
bf16 = jnp.bfloat16


def dot(a, b):
    return lax.dot_general(a, b, (((1,), (0,)), ((), ())), preferred_element_type=f32)


def dot_nt(a, b):
    return lax.dot_general(a, b, (((1,), (1,)), ((), ())), preferred_element_type=f32)


def dot_tn(a, b):
    return lax.dot_general(a, b, (((0,), (0,)), ((), ())), preferred_element_type=f32)


def normalize(x):
    center = x - jnp.mean(x, axis=-1, keepdims=True)
    spread = jnp.mean(center * center, axis=-1, keepdims=True)
    r = lax.rsqrt(spread + 1e-05)
    return center * r, r


def norm_back(grad_y, n, r, gain):
    d = grad_y * gain
    return r * (d - jnp.mean(d, axis=-1, keepdims=True) - n * jnp.mean(d * n, axis=-1, keepdims=True))


def col_sum(v):
    return jnp.sum(v, axis=0, keepdims=True)


def row_blocks(rows, most):
    size = max(d for d in range(16, most + 1, 16) if rows % d == 0)
    return [slice(r0, r0 + size) for r0 in range(0, rows, size)]


def fold_rows(v, op=jnp.sum):
    return op(v.reshape(-1, 8, v.shape[-1]), axis=0)


def block_diag(rows, masks):
    return jnp.concatenate([rows * m for m in masks], 0)


def pick_heads(r, rows):
    lane = lax.broadcasted_iota(jnp.int32, (rows, 128), 1)
    return jnp.where(lane < HD, r[:rows], r[rows:])


def valid_frames(f, total, length):
    return (f >= 0) & (f < total) & ((f < length) | ((f & (SEG - 1)) == 0))


def softmax_rows(s):
    m = jnp.max(s, axis=0, keepdims=True)
    e = jnp.exp(s - m)
    return e * (1.0 / jnp.sum(e, axis=0, keepdims=True))


def const_spec(shape):
    zeros = (0,) * len(shape)
    return pl.BlockSpec(shape, lambda r: zeros, pipeline_mode=pl.Buffered(1))


def row_spec(shape):
    zeros = (0,) * len(shape)
    return pl.BlockSpec((1,) + shape, lambda r: (r,) + zeros)


def in_vmem(shape, dtype):
    return pltpu.VMEM(shape, dtype)


def smem_spec():
    return pl.BlockSpec(memory_space=pltpu.SMEM)


def params(mb=60):
    return pltpu.CompilerParams(dimension_semantics=("arbitrary",), vmem_limit_bytes=mb * MB)


def cost():
    return pl.CostEstimate(flops=1000000, bytes_accessed=100000, transcendentals=0)


def own_kernel(
    x_ref,
    gain_ref,
    bias_ref,
    w_ref,
    qvb_ref,
    pool_ref,
    q_ref,
    k_ref,
    v_ref,
    nt_ref,
    ns_ref,
    pooled_ref,
    pq_ref,
    low_s,
    n_s,
):
    t = x_ref.shape[1]
    for rows in row_blocks(t, 32):
        n, _ = normalize(x_ref[0, rows].astype(f32))
        low_s[rows] = (n * gain_ref[0:1] + bias_ref[0:1]).astype(bf16)
        n_s[rows] = n.astype(bf16)
    low = low_s[...]
    q_ref[0] = ((dot(low, w_ref[:, :D]) + qvb_ref[0:1]) * SCALE).astype(bf16)
    for rows in row_blocks(t, 128):
        nt_ref[0, :, rows] = n_s[rows].T
    k_ref[0, HL : HL + t] = dot(low, w_ref[:, D : 2 * D]).astype(bf16)
    v_ref[0, HL : HL + t] = (dot(low, w_ref[:, 2 * D :]) + qvb_ref[1:2]).astype(bf16)
    ns_ref[0] = dot(pool_ref[...], n_s[...])
    pooled = (dot(pool_ref[...], low) * (1.0 / SEG)).astype(bf16)
    pooled_ref[0] = pooled
    pq_ref[0] = ((dot(pooled, w_ref[:, :D]) + qvb_ref[0:1]) * SCALE).astype(bf16)


def near_mask(keys, lanes, seg_mask, seg0, frame0, position, total, length):
    f = lax.broadcasted_iota(jnp.int32, (keys, lanes), 0) + frame0
    seg = (lax.broadcasted_iota(jnp.int32, (keys, lanes), 1) & seg_mask) + seg0
    start = seg * SEG
    ok = (f >= start - LEFT) & (f < start + (SEG + RC))
    return ok & valid_frames(f + position, total, length)


def memory_kernel(
    groups,
    total,
    utts,
    len_ref,
    xl_ref,
    xr_ref,
    pq_ref,
    gain_ref,
    bias_ref,
    w_ref,
    qvb_ref,
    ow_ref,
    ob_ref,
    poolh_ref,
    expand_ref,
    hm8_ref,
    kin_ref,
    vin_ref,
    q_ref,
    hm4_ref,
    inside_ref,
    kext_ref,
    vext_ref,
    mkg_hbm,
    mvg_hbm,
    summary_hbm,
    memory_hbm,
    ps_hbm,
    p_ref,
    att_ref,
    k_s,
    v_s,
    score_s,
    prob_s,
    mkg_ref,
    mvg_ref,
    summary_ref,
    memory_ref,
    ps_ref,
    in_sem,
    out_sem,
    early_sem,
):
    step = pl.program_id(0)
    early_refs = (mkg_hbm, mvg_hbm, summary_hbm, memory_hbm, ps_hbm)

    @pl.when(step == pl.num_programs(0) - 1)
    def _():
        for value, out, sem in zip((mkg_ref, mvg_ref, summary_ref, memory_ref, ps_ref), early_refs, range(5)):
            pltpu.make_async_copy(value, out, early_sem.at[sem]).wait()

    @pl.when(step == 0)
    def _():
        memory_step(
            total,
            utts,
            len_ref,
            xl_ref,
            xr_ref,
            pq_ref,
            gain_ref,
            bias_ref,
            w_ref,
            qvb_ref,
            ow_ref,
            ob_ref,
            poolh_ref,
            expand_ref,
            hm8_ref,
            kin_ref,
            vin_ref,
            kext_ref,
            vext_ref,
            mkg_ref,
            mvg_ref,
            summary_ref,
            memory_ref,
            ps_ref,
            k_s,
            v_s,
            score_s,
            prob_s,
            in_sem,
            out_sem,
            early_refs,
            early_sem,
        )

    @pl.when(step > 0)
    def _():
        row = step - 1
        attend_step(
            groups,
            total,
            len_ref[lax.rem(row, utts)],
            q_ref,
            k_s.at[pl.ds(row, 1)],
            v_s.at[pl.ds(row, 1)],
            mkg_ref.at[pl.ds(row, 1)],
            mvg_ref.at[pl.ds(row, 1)],
            hm4_ref,
            inside_ref,
            p_ref,
            att_ref,
        )


def memory_step(
    total,
    utts,
    len_ref,
    xl_ref,
    xr_ref,
    pq_ref,
    gain_ref,
    bias_ref,
    w_ref,
    qvb_ref,
    ow_ref,
    ob_ref,
    poolh_ref,
    expand_ref,
    hm8_ref,
    kin_ref,
    vin_ref,
    kext_ref,
    vext_ref,
    mkg_ref,
    mvg_ref,
    summary_ref,
    memory_ref,
    ps_ref,
    k_s,
    v_s,
    score_s,
    prob_s,
    in_sem,
    out_sem,
    early_refs,
    early_sem,
):
    rows, ext, _ = k_s.shape
    t = ext - HALO
    sp = pq_ref.shape[1]
    own_keys = ext - OWN0
    loads = [pltpu.make_async_copy(kin_ref, k_s, in_sem.at[0]), pltpu.make_async_copy(vin_ref, v_s, in_sem.at[1])]
    for load in loads:
        load.start()
    position = lax.axis_index("tm") * t
    halo = [xl_ref[...].reshape(rows * HL, D), xr_ref[...].reshape(rows * HR, D)]
    n, _ = normalize(jnp.concatenate(halo, 0).astype(f32))
    low = (n * gain_ref[0:1] + bias_ref[0:1]).astype(bf16)
    kh = dot(low, w_ref[:, D : 2 * D]).astype(bf16)
    vh = (dot(low, w_ref[:, 2 * D :]) + qvb_ref[1:2]).astype(bf16)
    pooled = [dot(poolh_ref[...], low[r * HL : (r + 1) * HL]) * (1.0 / SEG) for r in range(rows)]
    pooled = jnp.concatenate(pooled, 0).astype(bf16)
    pqh = ((dot(pooled, w_ref[:, :D]) + qvb_ref[0:1]) * SCALE).astype(bf16)
    for load in loads:
        load.wait()
    for scratch, value in ((k_s, kh), (v_s, vh)):
        for r in range(rows):
            scratch[r, :HL] = value[r * HL : (r + 1) * HL]
            scratch[r, HL + t :] = value[rows * HL + r * HR : rows * HL + (r + 1) * HR]
    stores = []
    for i, (scratch, out) in enumerate(((k_s, kext_ref), (v_s, vext_ref))):
        for j, part in enumerate((pl.ds(0, HL), pl.ds(HL + t, HR))):
            stores.append(pltpu.make_async_copy(scratch.at[:, part], out.at[:, part], out_sem.at[2 * i + j]))
    for store in stores:
        store.start()
    masks8 = [hm8_ref[h : h + 1] for h in range(HEADS)]
    jobs = []
    for r in range(rows):
        jobs.append((r, slice(0, HALO), 16, -16, -HL))
        jobs.append((r, slice(OWN0, ext), sp, 0, -32))
    sums = []
    for step in range(len(jobs) + 2):
        if step < len(jobs):
            r, keys, count, _, _ = jobs[step]
            pq = pqh[r * 16 : (r + 1) * 16] if step % 2 == 0 else pq_ref[r]
            score_s[step % 4, : keys.stop - keys.start, : HEADS * count] = dot_nt(k_s[r, keys], block_diag(pq, masks8))
        if 1 <= step <= len(jobs):
            r, keys, count, seg0, frame0 = jobs[step - 1]
            score, prob = score_s.at[(step - 1) % 4], prob_s.at[(step - 1) % 4]
            blocks = row_blocks(keys.stop - keys.start, 128)
            for l0 in range(0, HEADS * count, 128):
                lanes = slice(l0, l0 + 128)
                most = None
                for block in blocks:
                    shape = (block.stop - block.start, 128)
                    mask = near_mask(*shape, count - 1, seg0, frame0 + block.start, position, total, len_ref[r % utts])
                    value = jnp.where(mask, score[block, lanes], NEG)
                    score[block, lanes] = value
                    value = fold_rows(value, jnp.max)
                    most = value if most is None else jnp.maximum(most, value)
                most = jnp.max(most, axis=0, keepdims=True)
                weight = 0.0
                for block in blocks:
                    value = jnp.exp(score[block, lanes] - most)
                    score[block, lanes] = value
                    weight += fold_rows(value)
                weight = 1.0 / col_sum(weight)
                for block in blocks:
                    value = (score[block, lanes] * weight).astype(bf16)
                    prob[block, lanes] = value
                    if step % 2 == 0:
                        ps_ref[r, block, lanes] = value
        if step >= 2:
            r, keys, count, _, _ = jobs[step - 2]
            prob = prob_s[(step - 2) % 4, : keys.stop - keys.start, : HEADS * count]
            o = dot_tn(prob, v_s[r, keys])
            o = [
                pick_heads(o[2 * j * count : (2 * j + 2) * count, 128 * j : 128 * j + 128], count)
                for j in range(HEADS // 2)
            ]
            sums.append(jnp.concatenate(o, 1).astype(bf16))
            if step % 2:
                summary_ref[r] = sums[-1]
    memory = (dot(jnp.concatenate(sums, 0), ow_ref[...]) + ob_ref[...]).astype(bf16)
    mk = dot(memory, w_ref[:, D : 2 * D]).astype(bf16)
    mv = (dot(memory, w_ref[:, 2 * D :]) + qvb_ref[1:2]).astype(bf16)
    both = jnp.concatenate([mk, mv], 1)
    for r in range(rows):
        here = slice(r * (16 + sp), (r + 1) * (16 + sp))
        memory_ref[r] = memory[here][16:]
        spread = dot(expand_ref[...], both[here]).astype(bf16)
        mkg_ref[r] = spread[:, :D]
        mvg_ref[r] = spread[:, D:]
    for value, out, sem in zip((mkg_ref, mvg_ref, summary_ref, memory_ref, ps_ref), early_refs, range(5)):
        pltpu.make_async_copy(value, out, early_sem.at[sem]).start()
    for store in stores:
        store.wait()


def group_keys(ref, mem_ref, g):
    k0 = g * GQ + OWN0
    return jnp.concatenate([mem_ref[0, g * MEMK : (g + 1) * MEMK], ref[0, k0 : k0 + NEAR]], 0)


def attend_step(
    groups, total, length, q_ref, kext_ref, vext_ref, mkg_ref, mvg_ref, hm4_ref, inside_ref, p_ref, att_ref
):
    position = lax.axis_index("tm") * q_ref.shape[1]
    masks4 = [hm4_ref[h : h + 1] for h in range(4)]
    slot = lax.broadcasted_iota(jnp.int32, (KEYS, 128), 0)
    inside = inside_ref[...] > 0.5
    scores, probs = {}, {}
    for step in range(groups + 2):
        if step < groups:
            g = step
            q = q_ref[0, g * GQ : (g + 1) * GQ]
            kc = group_keys(kext_ref, mkg_ref, g)
            for quad in range(2):
                c0 = 256 * quad
                scores[g, quad] = dot_nt(kc[:, c0 : c0 + 256], block_diag(q[:, c0 : c0 + 256], masks4))
        if 1 <= step <= groups:
            g = step - 1
            f = jnp.where(slot < MEMK, (slot + (g * GROUP - MEMS)) * SEG, slot + (g * GQ - 32 - MEMK)) + position
            keep = inside & valid_frames(f, total, length)
            for pair in range(HEADS // 2):
                cp = 128 * pair
                s = scores[g, pair // 2][:, 128 * (pair % 2) : 128 * (pair % 2) + 128]
                probs[g, pair] = softmax_rows(jnp.where(keep, s, NEG)).astype(bf16)
                p_ref[0, g, :, cp : cp + 128] = probs[g, pair]
        if step >= 2:
            g = step - 2
            vc = group_keys(vext_ref, mvg_ref, g)
            for pair in range(HEADS // 2):
                cp = 128 * pair
                r = dot_tn(probs[g, pair], vc[:, cp : cp + 128])
                att_ref[0, g * GQ : (g + 1) * GQ, cp : cp + 128] = pick_heads(r, GQ).astype(bf16)


def split_halves(bit_ref, keep_ref, send_ref, cols, src_ref):
    half = D // 2

    @pl.when(bit_ref[0] == 0)
    def _():
        keep_ref[:, cols] = src_ref[:half].astype(bf16)
        send_ref[:, cols] = src_ref[half:].astype(bf16)

    @pl.when(bit_ref[0] != 0)
    def _():
        keep_ref[:, cols] = src_ref[half:].astype(bf16)
        send_ref[:, cols] = src_ref[:half].astype(bf16)


def gelu_both(v):
    e = jnp.exp2(v * v * (-0.5 * 1.4426950408889634))
    t = pl.reciprocal(1.0 + jnp.abs(v) * (0.3275911 * 0.5**0.5), approx=True)
    e, t, v = e.astype(bf16), t.astype(bf16), v.astype(bf16)
    poly = 0.5 * -1.453152027 + t * (0.5 * 1.061405429)
    poly = 0.5 * 1.421413741 + t * poly
    poly = 0.5 * -0.284496736 + t * poly
    poly = 0.5 * 0.254829592 + t * poly
    tail = t * poly * e
    phi = jnp.where(v >= 0, 1 - tail, tail)
    return v * phi, phi + v * (e * 0.3989422804014327)


def ff_kernel(
    tiles,
    bit_ref,
    x_ref,
    c_ref,
    att_ref,
    gain_ref,
    bias_ref,
    ow_ref,
    ob_ref,
    uw_ref,
    ub_ref,
    dw_ref,
    db_ref,
    out_ref,
    gmix_ref,
    gatt_ref,
    keep_ref,
    send_ref,
    outg_ref,
    vec_ref,
    upb_ref,
    n_s,
    r_s,
    n2_s,
    n2t_s,
    ct_s,
    up0_s,
    up1_s,
    da0_s,
    da1_s,
    act0_s,
    act1_s,
    dup0_s,
    dup1_s,
    acc_s,
    gy_s,
    upg_s,
    dng_s,
):
    step = pl.program_id(0)
    ff = uw_ref.shape[1]
    wide = ff // tiles
    up_s, da_s, act_s, dup_s = (up0_s, up1_s), (da0_s, da1_s), (act0_s, act1_s), (dup0_s, dup1_s)

    @pl.when(step == 0)
    def _():
        upg_s[...] = jnp.zeros_like(upg_s)
        dng_s[...] = jnp.zeros_like(dng_s)
        outg_ref[...] = jnp.zeros_like(outg_ref)
        vec_ref[...] = jnp.zeros_like(vec_ref)
        upb_ref[...] = jnp.zeros_like(upb_ref)

    gy_s[...] = x_ref[...].astype(f32) + dot(att_ref[...], ow_ref[...]) + ob_ref[...]
    for rows in row_blocks(x_ref.shape[0], 32):
        mixed = gy_s[rows]
        n, r = normalize(mixed)
        n_s[rows] = n
        r_s[rows] = jnp.broadcast_to(r, (mixed.shape[0], 128))
        n2_s[rows] = (n * gain_ref[1:2] + bias_ref[1:2]).astype(bf16)
        acc_s[rows] = mixed + db_ref[...]
    for rows in row_blocks(x_ref.shape[0], 128):
        n2t_s[:D, rows] = n2_s[rows].T
        ct_s[:, rows] = c_ref[rows].T
    n2t_s[D:] = jnp.ones((16, x_ref.shape[0]), bf16)

    tb = x_ref.shape[0]
    chunk = min(512, tb)

    def gelu_rows(i, few):
        half = slice((i % 2) * wide, (i % 2 + 1) * wide)
        act, slope = gelu_both(up_s[i % 2][few])
        act_s[i // 2 % 2][few, half] = act
        dup_s[i // 2 % 2][few, half] = slope * da_s[i % 2][few]

    for j in range(tiles + 2):
        pieces = row_blocks(tb, 64) if 1 <= j <= tiles else []

        def some(count):
            for few in pieces[:count]:
                gelu_rows(j - 1, few)
            del pieces[:count]

        for r0 in range(0, tb, chunk):
            rows = slice(r0, r0 + chunk)
            if j < tiles:
                cols = slice(j * wide, (j + 1) * wide)
                up_s[j % 2][rows] = dot(n2_s[rows], uw_ref[:, cols]) + ub_ref[:, cols]
                some(3)
                da_s[j % 2][rows] = dot_nt(c_ref[rows], dw_ref[cols, :]).astype(bf16)
            some(3)
            if j >= 2 and j % 2:
                i = j - 2
                both = slice((i - 1) * wide, (i + 1) * wide)
                acc_s[rows] += dot(act_s[i // 2 % 2][rows], dw_ref[both, :])
                back = dot_nt(dup_s[i // 2 % 2][rows], uw_ref[:, both])
                gy_s[rows] = back if i == 1 else gy_s[rows] + back
        some(len(pieces))
        if j >= 2:
            i = j - 2
            cols = slice(i * wide, (i + 1) * wide)
            half = slice((i % 2) * wide, (i % 2 + 1) * wide)
            grad = dot(n2t_s[...], dup_s[i // 2 % 2][:, half])
            upg_s[:, cols] += grad[:D]
            upb_ref[:, cols] += grad[D : D + 1]
            dng_s[:, cols] += dot(ct_s[...], act_s[i // 2 % 2][:, half])

    sums = [0.0] * 4
    for rows in row_blocks(x_ref.shape[0], 32):
        out_ref[rows] = acc_s[rows].astype(bf16)
        n = n_s[rows]
        cf = c_ref[rows].astype(f32)
        gy = gy_s[rows]
        gmix = cf + norm_back(gy, n, r_s[rows, 0:1], gain_ref[1:2])
        gmix_ref[rows] = gmix.astype(bf16)
        sums = [a + fold_rows(b) for a, b in zip(sums, (gy * n, gy, gmix, cf))]
    branch = gmix_ref[...]
    gatt_ref[...] = dot_nt(branch, ow_ref[...]).astype(bf16)
    outg_ref[...] += dot_tn(att_ref[...], branch)
    for i, value in enumerate(sums):
        vec_ref[i : i + 1] += col_sum(value)

    @pl.when(step == pl.num_programs(0) - 1)
    def _():
        split_halves(bit_ref, keep_ref, send_ref, slice(0, ff), upg_s)
        split_halves(bit_ref, keep_ref, send_ref, slice(ff, 2 * ff), dng_s)


def attend_back_kernel(
    g0,
    g1,
    q_ref,
    kext_ref,
    vext_ref,
    mkg_ref,
    mvg_ref,
    p_ref,
    g_ref,
    hm4_ref,
    dq_ref,
    dk_ref,
    dv_ref,
    dm_ref,
    first_ref,
    dk_s,
    dv_s,
):
    dk_s[...] = jnp.zeros_like(dk_s)
    dv_s[...] = jnp.zeros_like(dv_s)
    masks4 = [hm4_ref[h : h + 1] for h in range(4)]
    count = g1 - g0
    grads, backs = {}, {}
    for step in range(count + 2):
        if step < count:
            g = step
            go = g_ref[0, (g0 + g) * GQ : (g0 + g + 1) * GQ]
            vc = group_keys(vext_ref, mvg_ref, g0 + g)
            for quad in range(2):
                cols = slice(256 * quad, 256 * quad + 256)
                grads[g, quad] = dot_nt(vc[:, cols], block_diag(go[:, cols], masks4))
        if 1 <= step <= count:
            g = step - 1
            for pair in range(HEADS // 2):
                half = slice(128 * (pair % 2), 128 * (pair % 2) + 128)
                p = p_ref[0, g0 + g, :, 128 * pair : 128 * pair + 128].astype(f32)
                pdp = p * grads[g, pair // 2][:, half]
                backs[g, pair] = (pdp - p * col_sum(pdp)).astype(bf16)
        if step >= 2:
            g = step - 2
            here = slice(g * GQ, (g + 1) * GQ)
            near = slice(g * GQ, g * GQ + NEAR)
            mem = slice(g * MEMK, (g + 1) * MEMK)
            there = slice((g0 + g) * GQ, (g0 + g + 1) * GQ)
            q = q_ref[0, there]
            go = g_ref[0, there]
            kc = group_keys(kext_ref, mkg_ref, g0 + g)
            for quad in range(2):
                c0 = 256 * quad
                cols = slice(c0, c0 + 256)
                dv_cols = slice(D + c0, D + c0 + 256)
                ds = jnp.concatenate([backs[g, 2 * quad], backs[g, 2 * quad + 1]], 1)
                dv = dot(p_ref[0, g0 + g, :, cols], block_diag(go[:, cols], masks4))
                dk = dot(ds, block_diag(q[:, cols], masks4))
                dm_ref[0, mem, cols] = dk[:MEMK].astype(bf16)
                dm_ref[0, mem, dv_cols] = dv[:MEMK].astype(bf16)
                if g0 + g == 0:
                    first_ref[0, :, cols] = dk[:MEMK].astype(bf16)
                    first_ref[0, :, dv_cols] = dv[:MEMK].astype(bf16)
                dk_s[near, cols] += dk[MEMK:]
                dv_s[near, cols] += dv[MEMK:]
                for pair in range(2):
                    cp = c0 + 128 * pair
                    r = dot_tn(backs[g, 2 * quad + pair], kc[:, cp : cp + 128])
                    dq_ref[0, here, cp : cp + 128] = (pick_heads(r, GQ) * SCALE).astype(bf16)
    dk_ref[0] = dk_s[...].astype(bf16)
    dv_ref[0] = dv_s[...].astype(bf16)
    if g0:
        first_ref[...] = jnp.zeros_like(first_ref)


def memory_back_kernel(parts, *refs):
    count = len(parts)
    dm_refs, main_hbm = refs[:count], refs[count : 3 * count]
    (
        recv_ref,
        fold_ref,
        place_ref,
        w_ref,
        ow_ref,
        hm8_ref,
        pq_ref,
        kext_hbm,
        vext_hbm,
        ps_hbm,
        dko_hbm,
        dvo_hbm,
        left_ref,
        right_ref,
        gpq_ref,
        dmo_ref,
        gm_ref,
        k_s,
        v_s,
        ps_s,
        dp_s,
        ds_s,
        dk_s,
        dv_s,
        dko_s,
        dvo_s,
        *main_s,
        in_sems,
        out_sems,
    ) = refs[3 * count :]
    rows, sp, _ = pq_ref.shape
    t = dko_s.shape[1]
    own = pl.ds(OWN0, k_s.shape[1])
    loads = []
    for r in range(rows):
        pairs = [(vext_hbm.at[r, own], v_s.at[r]), (ps_hbm.at[r], ps_s.at[r]), (kext_hbm.at[r, own], k_s.at[r])]
        pairs += [(src.at[r], held.at[r]) for src, held in zip(main_hbm, main_s)]
        loads.append([pltpu.make_async_copy(src, dst, in_sems.at[r, i]) for i, (src, dst) in enumerate(pairs)])
    for row in loads:
        for load in row:
            load.start()
    stores = []
    for r in range(rows):
        pairs = ((dko_s.at[r], dko_hbm.at[r]), (dvo_s.at[r], dvo_hbm.at[r]))
        stores.append([pltpu.make_async_copy(src, dst, out_sems.at[r, i]) for i, (src, dst) in enumerate(pairs)])
    masks8 = [hm8_ref[h : h + 1] for h in range(HEADS)]

    def fold(r):
        got = dot(fold_ref[...], jnp.concatenate([ref[r] for ref in dm_refs], 0))
        return (got + dot(place_ref[...], recv_ref[r])).astype(bf16)

    dm = jnp.concatenate([fold(r) for r in range(rows)], 0)
    gm = dot_nt(dm, w_ref[:, D:]).astype(bf16)
    gs = dot_nt(gm, ow_ref[...]).astype(bf16)
    for r in range(rows):
        dmo_ref[r] = dm[r * sp : (r + 1) * sp]
        gm_ref[r] = gm[r * sp : (r + 1) * sp]
    gbd = {}
    blocks = row_blocks(dp_s.shape[1], 128)
    for step in range(rows + 2):
        if step < rows:
            loads[step][0].wait()
        if 1 <= step <= rows:
            loads[step - 1][1].wait()
        if step >= 2:
            for load in loads[step - 2][2:]:
                load.wait()
        if step < rows:
            r = step
            gbd[r] = block_diag(gs[r * sp : (r + 1) * sp], masks8)
            dp_s[r] = dot_nt(v_s[r], gbd[r])
        if 1 <= step <= rows:
            r = step - 1
            for l0 in range(0, HEADS * sp, 128):
                lanes = slice(l0, l0 + 128)
                weight = 0.0
                for block in blocks:
                    pdp = ps_s[r, block, lanes].astype(f32) * dp_s[r, block, lanes]
                    dp_s[r, block, lanes] = pdp
                    weight += fold_rows(pdp)
                weight = col_sum(weight)
                for block in blocks:
                    p = ps_s[r, block, lanes].astype(f32)
                    ds_s[r, block, lanes] = (dp_s[r, block, lanes] - p * weight).astype(bf16)
        if step >= 2:
            r = step - 2
            ds = ds_s[r]
            dq = dot_tn(ds, k_s[r])
            dq = [
                pick_heads(dq[2 * j * sp : (2 * j + 2) * sp, 128 * j : 128 * j + 128], sp)
                for j in range(HEADS // 2)
            ]
            gpq_ref[r] = (jnp.concatenate(dq, 1) * SCALE).astype(bf16)
            for left, right, sum_s, held, out_s, cols in (
                (ds, block_diag(pq_ref[r], masks8), dk_s, main_s[:count], dko_s, slice(0, D)),
                (ps_s[r], gbd[r], dv_s, main_s[count:], dvo_s, slice(D, 2 * D)),
            ):
                sum_s[r] = dot(left, right)
                for (g0, _), main in zip(parts, held):
                    sum_s[r, g0 * GQ : g0 * GQ + main.shape[1]] += main[r].astype(f32)
                left_ref[r, :, cols] = sum_s[r, :32].astype(bf16)
                out_s[r] = sum_s[r, 32 : 32 + t].astype(bf16)
                right_ref[r, :, cols] = sum_s[r, 32 + t :].astype(bf16)
            for store in stores[r]:
                store.start()
    for row in stores:
        for store in row:
            store.wait()


def query_weights_kernel(count, nt_ref, ns_ref, *refs):
    dq_refs = refs[:count]
    gpq_ref, w_ref, acc_ref, sum_ref = refs[count:]

    @pl.when(pl.program_id(0) == 0)
    def _():
        acc_ref[...] = jnp.zeros_like(acc_ref)
        sum_ref[...] = jnp.zeros_like(sum_ref)

    dq = jnp.concatenate([ref[0] for ref in dq_refs], 0)
    acc_ref[...] += dot(nt_ref[0], dq)
    gp = dot_nt(gpq_ref[0], w_ref[...]) * (1.0 / SEG)
    sum_ref[0:1] += col_sum(gp * ns_ref[0])
    sum_ref[1:2] += col_sum(gp) * SEG
    sum_ref[2:3] += col_sum(dq.astype(f32))


def shared_frames(main, from_left, from_right):
    t = main.shape[0]
    first = (main[:HR].astype(f32) + from_left.astype(f32)).astype(bf16)
    last = (main[t - 32 :].astype(f32) + from_right.astype(f32)).astype(bf16)
    return jnp.concatenate([first, main[HR : t - 32], last], 0)


def key_weights_kernel(
    nt_ref,
    dk_ref,
    dv_ref,
    fr_ref,
    fl_ref,
    gain_ref,
    bias_ref,
    sum_ref,
    pooled_ref,
    gpq_ref,
    memory_ref,
    dm_ref,
    summary_ref,
    gm_ref,
    vec_ref,
    upb_ref,
    w_hbm,
    accq_hbm,
    outg_hbm,
    bit_ref,
    keep_ref,
    send_ref,
    acc_s,
    cs_s,
    grads_s,
    norm_s,
    w_ref,
    accq_ref,
    outg_ref,
    sems,
):
    row = pl.program_id(0)
    late = ((w_hbm, w_ref), (accq_hbm, accq_ref), (outg_hbm, outg_ref))
    loads = [pltpu.make_async_copy(src, dst, sems.at[i]) for i, (src, dst) in enumerate(late)]

    @pl.when(row == 0)
    def _():
        for load in loads:
            load.start()
        acc_s[...] = jnp.zeros_like(acc_s)
        cs_s[...] = jnp.zeros_like(cs_s)

    for ref, cols in ((dk_ref, slice(0, D)), (dv_ref, slice(D, 2 * D))):
        d = shared_frames(ref[0], fl_ref[0, :, cols], fr_ref[0, :, cols])
        acc_s[:, cols] += dot(nt_ref[0], d)
        cs_s[:, cols] += col_sum(d.astype(f32))

    @pl.when(row == pl.num_programs(0) - 1)
    def _():
        for load in loads:
            load.wait()
        sums = sum_ref[...]
        norm = jnp.concatenate([gain_ref[0:1], bias_ref[0:1], jnp.zeros((126, D), f32)], 0).T
        norm_s[0] = jnp.broadcast_to(norm[:, 0:1], (D, 128))
        norm_s[1] = jnp.broadcast_to(norm[:, 1:2], (D, 128))
        norm_s[2:] = jnp.zeros((2, D, 128), f32)
        for part, (acc_ref, cs, left, right) in enumerate(
            (
                (accq_ref, sums[2:3], pooled_ref[...], gpq_ref[...]),
                (acc_s.at[:, :D], cs_s[:, :D], memory_ref[...], dm_ref[:, :D]),
                (acc_s.at[:, D:], cs_s[:, D:], memory_ref[...], dm_ref[:, D:]),
            )
        ):
            cols = slice(part * D, (part + 1) * D)
            grads_s[...] = dot_tn(left, right)
            for block in row_blocks(D, 128):
                for c0 in range(0, D, 128):
                    lanes = slice(c0, c0 + 128)
                    acc = acc_ref[block, lanes]
                    w = w_ref[block, part * D + c0 : part * D + c0 + 128].astype(f32)
                    grads_s[block, lanes] += acc * norm_s[0, block] + norm_s[1, block] * cs[:, lanes]
                    norm_s[2, block] += w * acc
                    norm_s[3, block] += w * cs[:, lanes]
            split_halves(bit_ref, keep_ref, send_ref, cols, grads_s)
        grads_s[...] = outg_ref[...] + dot_tn(summary_ref[...], gm_ref[...])
        split_halves(bit_ref, keep_ref, send_ref, slice(3 * D, 4 * D), grads_s)
        v = vec_ref[...]
        vectors = [sums[0:1], sums[1:2], v[0:1], v[1:2]]
        vectors += [sums[2:3] + col_sum(gpq_ref[...].astype(f32)), cs_s[:, D:] + col_sum(dm_ref[:, D:].astype(f32))]
        vectors += [v[2:3] + col_sum(gm_ref[...].astype(f32)), v[3:4]]
        hidden = [upb_ref[:, i * D : (i + 1) * D] for i in range(upb_ref.shape[1] // D)]
        packed = vectors + hidden + [jnp.zeros((128 - len(vectors) - len(hidden), D), f32)]
        columns = jnp.concatenate(packed, 0).T
        lane = lax.broadcasted_iota(jnp.int32, columns.shape, 1)
        gain_col = jnp.sum(norm_s[2], axis=-1, keepdims=True)
        bias_col = jnp.sum(norm_s[3], axis=-1, keepdims=True)
        columns += jnp.where(lane == 0, gain_col, jnp.where(lane == 1, bias_col, 0.0))
        grads_s[:, :128] = columns
        split_halves(bit_ref, keep_ref, send_ref, slice(4 * D, 4 * D + 128), grads_s.at[:, :128])


def own_frames_kernel(count, x_ref, *refs):
    dq_refs = refs[:count]
    dk_ref, dv_ref, fr_ref, fl_ref, gpq_ref, gmix_ref, gain_ref, w_ref, fg_ref, gy_s = refs[count:]
    t = x_ref.shape[1]
    gp = (dot_nt(gpq_ref[0], w_ref[:, :D]) * (1.0 / SEG))[: t // SEG]
    spread = jnp.broadcast_to(gp[:, None, :], (t // SEG, SEG, D)).reshape(t, D)
    dq = jnp.concatenate([ref[0] for ref in dq_refs], 0)
    dk = shared_frames(dk_ref[0], fl_ref[0, :, :D], fr_ref[0, :, :D])
    dv = shared_frames(dv_ref[0], fl_ref[0, :, D:], fr_ref[0, :, D:])
    gy_s[...] = (
        dot_nt(dq, w_ref[:, :D]) + dot_nt(dk, w_ref[:, D : 2 * D]) + dot_nt(dv, w_ref[:, 2 * D :]) + spread
    )
    for rows in row_blocks(t, 32):
        n, r = normalize(x_ref[0, rows].astype(f32))
        fg_ref[0, rows] = (gmix_ref[0, rows].astype(f32) + norm_back(gy_s[rows], n, r, gain_ref[0:1])).astype(bf16)


def halves(bit_ref, mine_ref, other_ref, cols):
    first = jnp.where(bit_ref[0] == 0, mine_ref[:, cols], other_ref[:, cols])
    second = jnp.where(bit_ref[0] == 0, other_ref[:, cols], mine_ref[:, cols])
    return jnp.concatenate([first, second], 0).astype(f32)


def unpack_ff_kernel(bit_ref, mine_u, other_u, mine_d, other_d, up_ref, down_ref):
    up_ref[...] = halves(bit_ref, mine_u, other_u, slice(None))
    down_ref[...] = halves(bit_ref, mine_d, other_d, slice(None)).T


def unpack_own_kernel(side_ref, part_ref, qkv_ref, out_ref):
    step = pl.program_id(0)

    @pl.when(step < 3)
    def _():
        qkv_ref[...] = part_ref[...].astype(f32)

    @pl.when(step == 3)
    def _():
        out_ref[...] = part_ref[...].astype(f32)


def unpack_rest_kernel(
    side_ref,
    part_ref,
    mine_v,
    other_v,
    qkv_in,
    out_in,
    qkv_ref,
    out_ref,
    gain_ref,
    bias_ref,
    qvb_ref,
    outb_ref,
    upb_ref,
    downb_ref,
):
    unpack_own_kernel(side_ref, part_ref, qkv_ref, out_ref)

    @pl.when(pl.program_id(0) == 0)
    def _():
        second = side_ref[0] == 1
        first = jnp.where(second, mine_v[...], other_v[...])
        last = jnp.where(second, other_v[...], mine_v[...])
        v = jnp.concatenate([first, last], 0).astype(f32).T
        gain_ref[0:1], gain_ref[1:2] = v[0:1], v[2:3]
        bias_ref[0:1], bias_ref[1:2] = v[1:2], v[3:4]
        qvb_ref[...] = v[4:6]
        outb_ref[...] = v[6:7]
        downb_ref[...] = v[7:8]
        for i in range(upb_ref.shape[1] // D):
            upb_ref[:, i * D : (i + 1) * D] = v[8 + i : 9 + i]


def shifted(value, axis, steps):
    count = lax.axis_size(axis)
    first, last = max(0, -steps), min(count, count - steps)
    return lax.ppermute(value, axis, [(source, source + steps) for source in range(first, last)])


class Exchange:
    def __init__(self):
        self.count_dp, self.count_tm = lax.axis_size("dp"), lax.axis_size("tm")
        dp, tm = lax.axis_index("dp"), lax.axis_index("tm")
        dp_bits = [(1 << b, 0) for b in range(self.count_dp.bit_length() - 1)]
        tm_bits = [(0, 1 << b) for b in range(self.count_tm.bit_length() - 1)]
        self.steps = [([tm_bits[0]], [tm_bits[0]])]
        self.steps += [([a], [b]) for a, b in zip(dp_bits, reversed(dp_bits))]
        self.steps += [(tm_bits[i : i + 2],) * 2 for i in range(1, len(tm_bits), 2)]
        self.digits = []
        for step in self.steps:
            digit = [0, 0]
            for parity in range(2):
                for f_dp, f_tm in step[parity]:
                    one = ((dp & f_dp) + (tm & f_tm) != 0).astype(jnp.int32)
                    digit[parity] = digit[parity] * 2 + one
            self.digits.append(jnp.where((tm & 1) == 0, digit[0], digit[1]))

    def radix(self, index):
        return 1 << len(self.steps[index][0])

    def send(self, part, index, flip=1):
        pairs = []
        for d in range(self.count_dp):
            for t in range(self.count_tm):
                to_d, to_t = d, t
                bits = self.steps[index][t & 1]
                for i, (f_dp, f_tm) in enumerate(bits):
                    if flip >> (len(bits) - 1 - i) & 1:
                        to_d, to_t = to_d ^ f_dp, to_t ^ f_tm
                pairs.append((d * self.count_tm + t, to_d * self.count_tm + to_t))
        return lax.ppermute(part, ("dp", "tm"), pairs)

    def total(self, terms):
        return sum(term.astype(f32) for term in terms).astype(bf16)

    def part(self, terms, index, flip):
        rows = terms[0].shape[0] // self.radix(index)
        start = (self.digits[index] ^ flip) * rows
        return [lax.dynamic_slice_in_dim(term, start, rows) for term in terms]

    def scatter(self, terms, index, sends=None):
        if sends is None:
            sends = [self.total(self.part(terms, index, flip)) for flip in range(1, self.radix(index))]
            terms = self.part(terms, index, 0)
        return terms, [self.send(value, index, flip + 1) for flip, value in enumerate(sends)]

    def gather(self, value, index):
        return [self.send(value, index, flip) for flip in range(1, self.radix(index))]

    def join(self, value, others, index):
        pieces = [value] + others
        out = jnp.concatenate(pieces, 0)
        for digit in range(1, len(pieces)):
            order = [pieces[place ^ digit] for place in range(len(pieces))]
            out = jnp.where(self.digits[index] == digit, jnp.concatenate(order, 0), out)
        return out


class Running:
    def __init__(self, exchange, keep, send):
        self.exchange = exchange
        self.steps = len(exchange.steps)
        self.last = 2 * self.steps - 1
        self.phase = 0
        self.terms, self.arriving = exchange.scatter([keep], 0, [send])
        self.value = None

    def index(self):
        return min(self.phase, self.last - self.phase)

    def beside(self, result):
        self.arriving, _ = lax.optimization_barrier((self.arriving, result))

    def before(self, operand):
        self.arriving, operand = lax.optimization_barrier((self.arriving, operand))
        return operand

    def advance(self):
        if self.phase < self.steps:
            self.terms = self.terms + self.arriving
        else:
            self.value = self.exchange.join(self.value, self.arriving, self.index())
        self.phase += 1
        if self.phase < self.steps:
            self.terms, self.arriving = self.exchange.scatter(self.terms, self.phase)
        else:
            if self.phase == self.steps:
                self.value = self.exchange.total(self.terms)
            self.arriving = self.exchange.gather(self.value, self.index())

    def along(self, result, operand):
        if self.phase < self.last:
            self.beside(result)
            operand = self.before(operand)
            self.advance()
        return operand


def sds(shape, dtype):
    return jax.ShapeDtypeStruct(shape, dtype)


def local(
    frames,
    lengths,
    norm_gain,
    norm_bias,
    qkv_weight,
    qv_bias,
    out_weight,
    out_bias,
    up_weight,
    up_bias,
    down_weight,
    down_bias,
    cotangent,
):
    micro, utts, t, _ = frames.shape
    rows = micro * utts
    segments = t // SEG
    sp = -(-segments // 16) * 16
    groups = t // GQ
    ext = HL + t + HR
    own_keys = ext - OWN0
    ff = up_weight.shape[1]
    tokens = rows * t
    total = t * lax.axis_size("tm")
    x = frames.reshape(rows, t, D)
    c = cotangent.reshape(rows, t, D)
    ob = out_bias.reshape(1, D)
    ub = up_bias.reshape(1, ff)
    db = down_bias.reshape(1, D)
    exchange = Exchange()
    steps = len(exchange.steps)
    bit = exchange.digits[0].reshape(1)

    pool = np.zeros((sp, t), np.float32)
    for s in range(segments):
        pool[s, s * SEG : (s + 1) * SEG] = 1
    poolh = np.zeros((16, HL), np.float32)
    for s in range(HL // SEG):
        poolh[16 - HL // SEG + s, s * SEG : (s + 1) * SEG] = 1
    expand = np.zeros((groups * MEMK, 16 + sp), np.float32)
    fold = np.zeros((sp, groups * MEMK), np.float32)
    for g in range(groups):
        for j in range(2 * MEMS - 1):
            seg = GROUP * g - MEMS + j
            expand[g * MEMK + j, 16 + seg] = 1
            if seg >= 0:
                fold[seg, g * MEMK + j] = 1
    place = np.zeros((sp, 16), np.float32)
    for j in range(MEMS):
        place[segments - MEMS + j, j] = 1
    hm8 = (np.arange(D)[None, :] // HD == np.arange(HEADS)[:, None]).astype(np.float32)
    hm4 = np.zeros((8, 256), np.float32)
    hm4[:4] = hm8[:4, :256]
    inside = np.zeros((KEYS, 128), np.float32)
    for lane in range(128):
        s = lane % GQ // SEG
        inside[s : s + MEMS, lane] = 1
        first = MEMK + 32 + s * SEG - LEFT
        inside[first : first + LEFT + SEG + RC, lane] = 1
    pool, poolh, expand, fold, place, hm8, hm4 = (
        jnp.asarray(v, bf16) for v in (pool, poolh, expand, fold, place, hm8, hm4)
    )
    inside = jnp.asarray(inside)

    pieces = []
    hop, need = 1, HL
    while need > 0:
        take = min(t, need)
        pieces.insert(0, shifted(x[:, t - take :], "tm", hop))
        need -= take
        hop += 1
    xl = jnp.concatenate(pieces, 1)
    xr = shifted(x[:, :HR], "tm", -1)

    q, k, v, nt, ns, pooled, pq = pl.pallas_call(
        own_kernel,
        grid=(rows,),
        in_specs=[
            row_spec((t, D)),
            const_spec((2, D)),
            const_spec((2, D)),
            const_spec((D, 3 * D)),
            const_spec((2, D)),
            const_spec((sp, t)),
        ],
        out_specs=[
            row_spec((t, D)),
            row_spec((ext, D)),
            row_spec((ext, D)),
            row_spec((D, t)),
            row_spec((sp, D)),
            row_spec((sp, D)),
            row_spec((sp, D)),
        ],
        out_shape=[
            sds((rows, t, D), bf16),
            sds((rows, ext, D), bf16),
            sds((rows, ext, D), bf16),
            sds((rows, D, t), bf16),
            sds((rows, sp, D), f32),
            sds((rows, sp, D), bf16),
            sds((rows, sp, D), bf16),
        ],
        scratch_shapes=[pltpu.VMEM((t, D), bf16), pltpu.VMEM((t, D), bf16)],
        compiler_params=params(),
        cost_estimate=cost(),
        name="own",
    )(x, norm_gain, norm_bias, qkv_weight, qv_bias, pool)

    any_spec = pl.BlockSpec(memory_space=pl.ANY)
    after_first = lambda r: (jnp.maximum(r - 1, 0), 0, 0)
    kext, vext, mkg, mvg, summary, memory, ps, p, attended = pl.pallas_call(
        functools.partial(memory_kernel, groups, total, utts),
        grid=(1 + rows,),
        in_specs=[
            smem_spec(),
            const_spec((rows, HL, D)),
            const_spec((rows, HR, D)),
            const_spec((rows, sp, D)),
            const_spec((2, D)),
            const_spec((2, D)),
            const_spec((D, 3 * D)),
            const_spec((2, D)),
            const_spec((D, D)),
            const_spec((1, D)),
            const_spec((16, HL)),
            const_spec((groups * MEMK, 16 + sp)),
            const_spec((HEADS, D)),
            any_spec,
            any_spec,
            pl.BlockSpec((1, t, D), after_first),
            const_spec((8, 256)),
            const_spec((KEYS, 128)),
        ],
        out_specs=[any_spec] * 7
        + [
            pl.BlockSpec((1, groups, KEYS, HEADS * GQ), lambda r: (jnp.maximum(r - 1, 0), 0, 0, 0)),
            pl.BlockSpec((1, t, D), after_first),
        ],
        out_shape=[
            sds((rows, ext, D), bf16),
            sds((rows, ext, D), bf16),
            sds((rows, groups * MEMK, D), bf16),
            sds((rows, groups * MEMK, D), bf16),
            sds((rows, sp, D), bf16),
            sds((rows, sp, D), bf16),
            sds((rows, own_keys, HEADS * sp), bf16),
            sds((rows, groups, KEYS, HEADS * GQ), bf16),
            sds((rows, t, D), bf16),
        ],
        scratch_shapes=[
            pltpu.VMEM((rows, ext, D), bf16),
            pltpu.VMEM((rows, ext, D), bf16),
            pltpu.VMEM((4, max(own_keys, HALO), HEADS * sp), f32),
            pltpu.VMEM((4, max(own_keys, HALO), HEADS * sp), bf16),
            pltpu.VMEM((rows, groups * MEMK, D), bf16),
            pltpu.VMEM((rows, groups * MEMK, D), bf16),
            pltpu.VMEM((rows, sp, D), bf16),
            pltpu.VMEM((rows, sp, D), bf16),
            pltpu.VMEM((rows, own_keys, HEADS * sp), bf16),
            pltpu.SemaphoreType.DMA((2,)),
            pltpu.SemaphoreType.DMA((4,)),
            pltpu.SemaphoreType.DMA((5,)),
        ],
        input_output_aliases={13: 0, 14: 1},
        compiler_params=params(),
        cost_estimate=cost(),
        name="attend",
    )(
        lengths,
        xl,
        xr,
        pq,
        norm_gain,
        norm_bias,
        qkv_weight,
        qv_bias,
        out_weight,
        ob,
        poolh,
        expand,
        hm8,
        k,
        v,
        q,
        hm4,
        inside,
    )

    tb = min(512, tokens)
    tiles = 8
    wide = ff // tiles
    token_spec = pl.BlockSpec((tb, D), lambda i: (i, 0))
    out, gmix, gatt, ff_keep, ff_send, outg, vec, upb = pl.pallas_call(
        functools.partial(ff_kernel, tiles),
        grid=(tokens // tb,),
        in_specs=[
            smem_spec(),
            token_spec,
            token_spec,
            token_spec,
            const_spec((2, D)),
            const_spec((2, D)),
            const_spec((D, D)),
            const_spec((1, D)),
            const_spec((D, ff)),
            const_spec((1, ff)),
            const_spec((ff, D)),
            const_spec((1, D)),
        ],
        out_specs=[
            token_spec,
            token_spec,
            token_spec,
            const_spec((D // 2, 2 * ff)),
            const_spec((D // 2, 2 * ff)),
            const_spec((D, D)),
            const_spec((8, D)),
            const_spec((1, ff)),
        ],
        out_shape=[
            sds((tokens, D), bf16),
            sds((tokens, D), bf16),
            sds((tokens, D), bf16),
            sds((D // 2, 2 * ff), bf16),
            sds((D // 2, 2 * ff), bf16),
            sds((D, D), f32),
            sds((8, D), f32),
            sds((1, ff), f32),
        ],
        scratch_shapes=[
            pltpu.VMEM((tb, D), f32),
            pltpu.VMEM((tb, 128), f32),
            pltpu.VMEM((tb, D), bf16),
            pltpu.VMEM((D + 16, tb), bf16),
            pltpu.VMEM((D, tb), bf16),
            pltpu.VMEM((tb, wide), f32),
            pltpu.VMEM((tb, wide), f32),
            pltpu.VMEM((tb, wide), bf16),
            pltpu.VMEM((tb, wide), bf16),
            pltpu.VMEM((tb, 2 * wide), bf16),
            pltpu.VMEM((tb, 2 * wide), bf16),
            pltpu.VMEM((tb, 2 * wide), bf16),
            pltpu.VMEM((tb, 2 * wide), bf16),
            pltpu.VMEM((tb, D), f32),
            pltpu.VMEM((tb, D), f32),
            pltpu.VMEM((D, ff), f32),
            pltpu.VMEM((D, ff), f32),
        ],
        compiler_params=params(),
        cost_estimate=cost(),
        name="feed_forward",
    )(
        bit,
        x.reshape(tokens, D),
        c.reshape(tokens, D),
        attended.reshape(tokens, D),
        norm_gain,
        norm_bias,
        out_weight,
        ob,
        up_weight,
        ub,
        down_weight,
        db,
    )
    gatt = gatt.reshape(rows, t, D)

    ff_sum = Running(exchange, ff_keep, ff_send)

    cut = groups * 3 // 8
    parts = [(0, cut), (cut, groups)] if cut else [(0, groups)]
    dqs, dks, dvs, dms = [], [], [], []
    for g0, g1 in parts:
        near = (g1 - g0) * GQ + NEAR - GQ
        if g0:
            gatt = ff_sum.along(dq, gatt)
        held = groups // 2 if g1 <= groups // 2 else groups
        dq, dk, dv, dm, first = pl.pallas_call(
            functools.partial(attend_back_kernel, g0, g1),
            grid=(rows,),
            in_specs=[
                row_spec((held * GQ, D)),
                row_spec((ext, D)),
                row_spec((ext, D)),
                row_spec((groups * MEMK, D)),
                row_spec((groups * MEMK, D)),
                row_spec((held, KEYS, HEADS * GQ)),
                row_spec((held * GQ, D)),
                const_spec((8, 256)),
            ],
            out_specs=[
                row_spec(((g1 - g0) * GQ, D)),
                row_spec((near, D)),
                row_spec((near, D)),
                row_spec(((g1 - g0) * MEMK, 2 * D)),
                row_spec((MEMK, 2 * D)),
            ],
            out_shape=[
                sds((rows, (g1 - g0) * GQ, D), bf16),
                sds((rows, near, D), bf16),
                sds((rows, near, D), bf16),
                sds((rows, (g1 - g0) * MEMK, 2 * D), bf16),
                sds((rows, MEMK, 2 * D), bf16),
            ],
            scratch_shapes=[pltpu.VMEM((near, D), f32), pltpu.VMEM((near, D), f32)],
            compiler_params=params(),
            cost_estimate=cost(),
            name="attend_back",
        )(q, kext, vext, mkg, mvg, p, gatt, hm4)
        for group, value in zip((dqs, dks, dvs, dms), (dq, dk, dv, dm)):
            group.append(value)
        if g0 == 0:
            recv = shifted(first, "tm", -1)

    recv = ff_sum.along(dq, recv)
    dko, dvo, left, right, gpq, dm, gm = pl.pallas_call(
        functools.partial(memory_back_kernel, parts),
        grid=(1,),
        in_specs=[const_spec(v.shape) for v in dms]
        + [any_spec] * (2 * len(parts))
        + [
            const_spec((rows, MEMK, 2 * D)),
            const_spec((sp, groups * MEMK)),
            const_spec((sp, MEMK)),
            const_spec((D, 3 * D)),
            const_spec((D, D)),
            const_spec((HEADS, D)),
            const_spec((rows, sp, D)),
            any_spec,
            any_spec,
            any_spec,
        ],
        out_specs=[
            any_spec,
            any_spec,
            const_spec((rows, 32, 2 * D)),
            const_spec((rows, HR, 2 * D)),
            const_spec((rows, sp, D)),
            const_spec((rows, sp, 2 * D)),
            const_spec((rows, sp, D)),
        ],
        out_shape=[
            sds((rows, t, D), bf16),
            sds((rows, t, D), bf16),
            sds((rows, 32, 2 * D), bf16),
            sds((rows, HR, 2 * D), bf16),
            sds((rows, sp, D), bf16),
            sds((rows, sp, 2 * D), bf16),
            sds((rows, sp, D), bf16),
        ],
        scratch_shapes=[
            pltpu.VMEM((rows, own_keys, D), bf16),
            pltpu.VMEM((rows, own_keys, D), bf16),
            pltpu.VMEM((rows, own_keys, HEADS * sp), bf16),
            pltpu.VMEM((rows, own_keys, HEADS * sp), f32),
            pltpu.VMEM((rows, own_keys, HEADS * sp), bf16),
            pltpu.VMEM((rows, own_keys, D), f32),
            pltpu.VMEM((rows, own_keys, D), f32),
            pltpu.VMEM((rows, t, D), bf16),
            pltpu.VMEM((rows, t, D), bf16),
        ]
        + [pltpu.VMEM(v.shape, bf16) for v in dks + dvs]
        + [pltpu.SemaphoreType.DMA((rows, 3 + 2 * len(parts))), pltpu.SemaphoreType.DMA((rows, 2))],
        compiler_params=params(),
        cost_estimate=cost(),
        name="memory_back",
    )(*dms, *dks, *dvs, recv, fold, place, qkv_weight, out_weight, hm8, pq, kext, vext, ps)

    from_right = shifted(left, "tm", -1)
    from_left = shifted(right, "tm", 1)
    gpq = ff_sum.along(gpq, gpq)
    dq_specs = [row_spec(v.shape[1:]) for v in dqs]
    accq, sums = pl.pallas_call(
        functools.partial(query_weights_kernel, len(dqs)),
        grid=(rows,),
        in_specs=[row_spec((D, t)), row_spec((sp, D))] + dq_specs + [row_spec((sp, D)), const_spec((D, D))],
        out_specs=[const_spec((D, D)), const_spec((8, D))],
        out_shape=[sds((D, D), f32), sds((8, D), f32)],
        compiler_params=params(),
        cost_estimate=cost(),
        name="query_weights",
    )(nt, ns, *dqs, gpq, qkv_weight)

    sums = ff_sum.along(sums, sums)
    keep, send = pl.pallas_call(
        key_weights_kernel,
        grid=(rows,),
        in_specs=[
            row_spec((D, t)),
            row_spec((t, D)),
            row_spec((t, D)),
            row_spec((32, 2 * D)),
            row_spec((HR, 2 * D)),
            const_spec((2, D)),
            const_spec((2, D)),
            const_spec((8, D)),
            const_spec((rows * sp, D)),
            const_spec((rows * sp, D)),
            const_spec((rows * sp, D)),
            const_spec((rows * sp, 2 * D)),
            const_spec((rows * sp, D)),
            const_spec((rows * sp, D)),
            const_spec((8, D)),
            const_spec((1, ff)),
            any_spec,
            any_spec,
            any_spec,
            smem_spec(),
        ],
        out_specs=[pl.BlockSpec(memory_space=pltpu.VMEM)] * 2,
        out_shape=[in_vmem((D // 2, 4 * D + 128), bf16)] * 2,
        scratch_shapes=[
            pltpu.VMEM((D, 2 * D), f32),
            pltpu.VMEM((1, 2 * D), f32),
            pltpu.VMEM((D, D), f32),
            pltpu.VMEM((4, D, 128), f32),
            pltpu.VMEM((D, 3 * D), bf16),
            pltpu.VMEM((D, D), f32),
            pltpu.VMEM((D, D), f32),
            pltpu.SemaphoreType.DMA((3,)),
        ],
        compiler_params=params(56),
        cost_estimate=cost(),
        name="key_weights",
    )(
        nt,
        dko,
        dvo,
        from_right,
        from_left,
        norm_gain,
        norm_bias,
        sums,
        pooled.reshape(rows * sp, D),
        gpq.reshape(rows * sp, D),
        memory.reshape(rows * sp, D),
        dm.reshape(rows * sp, 2 * D),
        summary.reshape(rows * sp, D),
        gm.reshape(rows * sp, D),
        vec,
        upb,
        qkv_weight,
        accq,
        outg,
        bit,
    )
    ff_sum.beside(send)
    send = ff_sum.before(send)
    rest = Running(exchange, keep, send)
    gpq = rest.before(gpq)
    fg = pl.pallas_call(
        functools.partial(own_frames_kernel, len(dqs)),
        grid=(rows,),
        in_specs=[row_spec((t, D))]
        + dq_specs
        + [
            row_spec((t, D)),
            row_spec((t, D)),
            row_spec((32, 2 * D)),
            row_spec((HR, 2 * D)),
            row_spec((sp, D)),
            row_spec((t, D)),
            const_spec((2, D)),
            const_spec((D, 3 * D)),
        ],
        out_specs=row_spec((t, D)),
        out_shape=sds((rows, t, D), bf16),
        scratch_shapes=[pltpu.VMEM((t, D), f32)],
        compiler_params=params(56),
        cost_estimate=cost(),
        name="own_frames",
    )(x, *dqs, dko, dvo, from_right, from_left, gpq, gmix.reshape(rows, t, D), norm_gain, qkv_weight)
    turns = [steps - 2, steps - 1, steps + 1] if ff_sum.last - ff_sum.phase <= 3 else list(range(1, 2 * steps - 1))
    while rest.phase < rest.last:
        if rest.phase == 1:
            rest.beside(fg)
        if rest.phase in turns and ff_sum.phase < ff_sum.last:
            ff_sum.arriving, rest.arriving = lax.optimization_barrier((ff_sum.arriving, rest.arriving))
            ff_sum.advance()
        if rest.phase == rest.last - 1:
            blocks = ff // D
            half = D // 2
            up_sum, down_sum = pl.pallas_call(
                unpack_ff_kernel,
                grid=(blocks,),
                in_specs=[smem_spec()]
                + [pl.BlockSpec((half, D), lambda i: (0, i))] * 2
                + [pl.BlockSpec((half, D), lambda i: (0, i + blocks))] * 2,
                out_specs=[pl.BlockSpec((D, D), lambda i: (0, i)), pl.BlockSpec((D, D), lambda i: (i, 0))],
                out_shape=[sds((D, ff), f32), sds((ff, D), f32)],
                compiler_params=params(28),
                cost_estimate=cost(),
                name="unpack_feed_forward",
            )(bit, ff_sum.value, ff_sum.arriving[0], ff_sum.value, ff_sum.arriving[0])
            rest.beside(up_sum)
        rest.advance()
    grads, other = rest.value, rest.arriving[0]
    half = D // 2
    part_spec = pl.BlockSpec((half, D), lambda i, side: (0, i))
    vector_spec = pl.BlockSpec((half, 128), lambda i, side: (0, 4 * D // 128), pipeline_mode=pl.Buffered(1))
    big_specs = [
        pl.BlockSpec((half, D), lambda i, side: (side[0], jnp.minimum(i, 2))),
        pl.BlockSpec((half, D), lambda i, side: (side[0], 0)),
    ]
    big_shapes = [sds((D, 3 * D), f32), sds((D, D), f32)]
    qkv_sum, out_sum = pl.pallas_call(
        unpack_own_kernel,
        grid_spec=pltpu.PrefetchScalarGridSpec(
            num_scalar_prefetch=1, grid=(4,), in_specs=[part_spec], out_specs=big_specs
        ),
        out_shape=big_shapes,
        compiler_params=params(28),
        cost_estimate=cost(),
        name="unpack_own",
    )(bit, grads)
    small_shapes = [(2, D), (2, D), (2, D), (1, D), (1, ff), (1, D)]
    other, qkv_sum = lax.optimization_barrier((other, qkv_sum))
    qkv_sum, out_sum, gain_sum, bias_sum, qvb_sum, outb_sum, upb_sum, downb_sum = pl.pallas_call(
        unpack_rest_kernel,
        grid_spec=pltpu.PrefetchScalarGridSpec(
            num_scalar_prefetch=1,
            grid=(4,),
            in_specs=[part_spec, vector_spec, vector_spec, any_spec, any_spec],
            out_specs=big_specs
            + [pl.BlockSpec(v, lambda i, side: (0, 0), pipeline_mode=pl.Buffered(1)) for v in small_shapes],
        ),
        out_shape=big_shapes + [sds(v, f32) for v in small_shapes],
        input_output_aliases={4: 0, 5: 1},
        compiler_params=params(28),
        cost_estimate=cost(),
        name="unpack_rest",
    )(1 - bit, other, grads, other, qkv_sum, out_sum)
    return (
        out.reshape(micro, utts, t, D),
        fg.reshape(micro, utts, t, D),
        gain_sum,
        bias_sum,
        qkv_sum,
        qvb_sum,
        out_sum,
        outb_sum.reshape(D),
        up_sum,
        upb_sum.reshape(ff),
        down_sum,
        downb_sum.reshape(D),
    )


def solution(mesh):
    spread = P(None, "dp", "tm", None)
    in_specs = (spread, P("dp")) + (P(),) * 10 + (spread,)
    out_specs = (spread, spread) + (P(),) * 10
    return jax.shard_map(local, mesh=mesh, in_specs=in_specs, out_specs=out_specs, check_vma=False)
```

time: 1300 us -> 216 us (0.17); the launches traced: 1280 us -> 215 us
  local copies, waits for them, and re-layouts: 436 us -> 4.1 us
  other arithmetic: 297 us -> 9.95 us
  matrix products: 264 us -> 0 us
  waiting for transfers between devices: 162 us -> 32 us
  Pallas kernels: 0 us -> 129 us
  blocking collectives: 43.5 us -> 0 us
  between operations: 20.4 us -> 1.2 us
  starting transfers between devices: 58 us -> 38.9 us
    dot_general x66 -> x0, matrix products: 264 us -> none  [the longest x16 44.6 us: dense_back(): jnp.einsum('...e,de->...d', grads, matrix, preferred_element_type=jnp.flo...]
    psum x1 -> x0, waiting for transfers between devices: 162 us -> none  [local(): lax.psum((totals[0], totals[1], totals[2], totals[3], totals[4], totals[5...]
    reshape x16 -> x0, local copies, waits for them, and re-layouts: 137 us -> none  [the longest x12 87.9 us: split_heads(): values.reshape(values.shape[:-1] + (HEADS, values.shape[-1] // HEADS))]
    pallas_call x0 -> x12, Pallas kernels: none -> 129 us  [the longest x1 41.7 us: local(): pl.pallas_call(functools.partial(ff_kernel, tiles), grid=(tokens // tb,),...]
    sub x3 -> x0, other arithmetic: 90.8 us -> none  [the longest x2 90.8 us: masked_softmax(): raised = jnp.exp(shifted - largest)]
    mul x6 -> x0, local copies, waits for them, and re-layouts: 74.8 us -> none  [attend_backward(): jnp.einsum('ushqk,usqhe->uskhe', score_low, split_heads(queries), preferr...]
    slice x38 -> x2, local copies, waits for them, and re-layouts: 55.1 us -> 1.88 us  [the longest x1 1.03 us: local(): pieces.insert(0, shifted(x[:, t - take:], 'tm', hop))]
    convert_element_type x12 -> x8, other arithmetic: 60.7 us -> 8.68 us  [total(): return sum((term.astype(f32) for term in terms)).astype(bf16)]
  transfers between devices with their start and end apart: 23 -> 29, of which waited for: 1 -> 15; matrix products, arithmetic and copies ran while one was open for 28% -> 2% of each run, Pallas kernels for 0% -> 32%
where the time goes in v1:
time: 216 us; the launch traced here: 215 us
  Pallas kernels  129 us (60%)
  starting transfers between devices  38.9 us (18%)
  waiting for transfers between devices  32 us (15%)
  other arithmetic  9.95 us (5%)
  local copies, waits for them, and re-layouts  4.1 us (2%)
    pallas_call x1, Pallas kernels, local(): pl.pallas_call(functools.partial(ff_kernel, tiles), grid=(tokens // tb,),...  41.7 us
    ppermute x24, waiting for transfers between devices, send(): return lax.ppermute(part, ('dp', 'tm'), pairs)  32 us
    ppermute x24, starting transfers between devices, send(): return lax.ppermute(part, ('dp', 'tm'), pairs)  29.7 us
    pallas_call x2, Pallas kernels, local(): pl.pallas_call(functools.partial(attend_back_kernel, g0, g1), grid=(rows,...  18.6 us
    pallas_call x1, Pallas kernels, local(): pl.pallas_call(functools.partial(memory_kernel, groups, total, utts), gri...  16.4 us
    pallas_call x1, Pallas kernels, local(): pl.pallas_call(functools.partial(own_frames_kernel, len(dqs)), grid=(rows...  10 us
    pallas_call x1, Pallas kernels, local(): pl.pallas_call(functools.partial(memory_back_kernel, parts), grid=(1,), i...  10 us
    pallas_call x1, Pallas kernels, local(): pl.pallas_call(own_kernel, grid=(rows,), in_specs=[row_spec((t, D)), cons...  9.34 us
  transfers between devices with their start and end apart: 29, of which 15 were waited for; matrix products, arithmetic and copies ran while one was open for 2% of the time, Pallas kernels for 32%

profile of v1, /device:TPU:0, one launch (start us, length us, event | category | flops | bytes accessed | tf_op | source)
XLA Modules:
  0.0 214.9 jit_solution(18243732195015441725)
XLA Ops:
  0.6 1.0 slice.8
  1.7 2.4 %collective-permute-start = (bf16[4,96,512]{2,1,0:T(8,128)(2,1)S(1)}, bf16[4,96,512]{2,1,0:T(8,128)(2,1)S(1)}, u32[]{:S(2)}, u32[]{:S(2)}) collective-permute-start(bf16[4,96,512]{2,1,0:T(8,128)(2,1)S(1)} %slice.8), channel_id=1, source_target_pairs={{0,1},{1,2},{2,3},{3,4},{4,5},{5,6},{6,7},{8,9},{9,10},{10,11},{11... | collective-permute-start | bytes 1179656 | tf_op jit(solution)/shard_map/ppermute | solution.py:965
  4.1 0.8 slice.9
  4.9 1.3 collective-permute-start.1
  6.2 9.3 %own.1 = (bf16[4,512,512]{2,1,0:T(8,128)(2,1)}, bf16[4,624,512]{2,1,0:T(8,128)(2,1)}, bf16[4,624,512]{2,1,0:T(8,128)(2,1)}, bf16[4,512,512]{2,1,0:T(8,128)(2,1)}...) custom-call(bf16[4,512,512]{2,1,0:T(8,128)(2,1)} %bitcast.23, f32[2,512]{1,0:T(2,128)} %refs_8_.2, ...), custom_call_target="tpu_custom_call" | custom-call | flops 1000000 | bytes 100000 | tf_op jit(solution)/shard_map/own/pallas_call | solution.py:1146
  15.6 0.6 copy-done.13
  16.3 16.4 %attend.1 = (bf16[4,624,512]{2,1,0:T(8,128)(2,1)}, bf16[4,624,512]{2,1,0:T(8,128)(2,1)}, bf16[4,128,512]{2,1,0:T(8,128)(2,1)}, bf16[4,128,512]{2,1,0:T(8,128)(2,...) custom-call(s32[2]{0:T(128)} %len_ref.1, ...), custom_call_target="tpu_custom_call", output_to_operand_aliasing={{0}: (13, {}), {1}: (14, {})} | custom-call | flops 1000000 | bytes 100000 | tf_op jit(solution)/shard_map/attend/pallas_call | solution.py:1183
  32.8 41.7 %feed_forward.1 = (bf16[2048,512]{1,0:T(8,128)(2,1)}, bf16[2048,512]{1,0:T(8,128)(2,1)}, bf16[2048,512]{1,0:T(8,128)(2,1)}, bf16[256,4096]{1,0:T(8,128)(2,1)}, b...) custom-call(s32[1]{0:T(128)} %bitcast.bit_ref.side_ref, ...), custom_call_target="tpu_custom_call" | custom-call | flops 1000000 | bytes 100000 | tf_op jit(solution)/shard_map/feed_forward/pallas_call | solution.py:1265
  74.5 3.3 %collective-permute-start.2 = (bf16[256,4096]{1,0:T(8,128)(2,1)}, bf16[256,4096]{1,0:T(8,128)(2,1)}, u32[]{:S(2)}, u32[]{:S(2)}) collective-permute-start(bf16[256,4096]{1,0:T(8,128)(2,1)} %get-tuple-element.120), channel_id=1, source_target_pairs={{0,1},{1,0},{2,3},{3,2},{4,5},{5,4},{6,7},{7,6},{8,9},{9,8},{10,11... | collective-permute-start | bytes 6291464 | tf_op jit(solution)/shard_map/ppermute | solution.py:999
  77.8 7.9 %attend_back.2 = (bf16[4,192,512]{2,1,0:T(8,128)(2,1)}, bf16[4,240,512]{2,1,0:T(8,128)(2,1)}, bf16[4,240,512]{2,1,0:T(8,128)(2,1)}, bf16[4,48,1024]{2,1,0:T(8,128)(2,1)}, bf16[4,16,1024]{2,1,0:T(8,128)(2,1)}) custom-call(bf16[4,512,512]{2,1,0:T(8,128)(2,1)} %get-tuple-element.110.q_ref, bf16[4,624,512]{2,1,0:T(8,128)(2,1)} %get-tuple-element.113.kext_ref.refs_13_, ...), custom_call_target="tpu_custom_call" | custom-call | flops 1000000 | bytes 100000 | tf_op jit(solution)/shard_map/attend_back/pallas_call | solution.py:1350
  85.8 1.5 add_convert_fusion
  87.3 1.6 collective-permute-start.3
  88.9 1.3 collective-permute-start.4
  90.2 10.7 %attend_back.3 = (bf16[4,320,512]{2,1,0:T(8,128)(2,1)}, bf16[4,368,512]{2,1,0:T(8,128)(2,1)}, bf16[4,368,512]{2,1,0:T(8,128)(2,1)}, bf16[4,80,1024]{2,1,0:T(8,128)(2,1)}, bf16[4,16,1024]{2,1,0:T(8,128)(2,1)}) custom-call(bf16[4,512,512]{2,1,0:T(8,128)(2,1)} %get-tuple-element.110.q_ref, bf16[4,624,512]{2,1,0:T(8,128)(2,1)} %get-tuple-element.113.kext_ref.refs_13_, ...), custom_call_target="tpu_custom_call" | custom-call | flops 1000000 | bytes 100000 | tf_op jit(solution)/shard_map/attend_back/pallas_call | solution.py:1350
  100.9 1.4 collective-permute-done.3
  102.3 1.6 add_convert_fusion.2
  103.9 1.6 collective-permute-start.7
  105.5 10.0 %memory_back.1 = (bf16[4,512,512]{2,1,0:T(8,128)(2,1)}, bf16[4,512,512]{2,1,0:T(8,128)(2,1)}, bf16[4,32,1024]{2,1,0:T(8,128)(2,1)}, bf16[4,16,1024]{2,1,0:T(8,12...) custom-call(bf16[4,48,1024]{2,1,0:T(8,128)(2,1)} %get-tuple-element.124.refs_0_, ...), custom_call_target="tpu_custom_call" | custom-call | flops 1000000 | bytes 100000 | tf_op jit(solution)/shard_map/memory_back/pallas_call | solution.py:1388
  115.5 1.8 add_convert_fusion.5
  117.3 2.8 %collective-permute-start.8 = (bf16[16,4096]{1,0:T(8,128)(2,1)S(1)}, bf16[16,4096]{1,0:T(8,128)(2,1)S(1)}, u32[]{:S(2)}, u32[]{:S(2)}) collective-permute-start(bf16[16,4096]{1,0:T(8,128)(2,1)S(1)} %get-tuple-element.204), channel_id=1, source_target_pairs={{0,4},{1,5},{2,6},{3,7},{4,0},{5,1},{6,2},{7,3},{8,12},{9,13},{10,... | collective-permute-start | bytes 393224 | tf_op jit(solution)/shard_map/ppermute | solution.py:999
  120.0 1.6 collective-permute-start.9
  121.7 1.3 collective-permute-start.5
  123.0 3.0 %collective-permute-start.6 = (bf16[4,16,1024]{2,1,0:T(8,128)(2,1)}, bf16[4,16,1024]{2,1,0:T(8,128)(2,1)S(1)}, u32[]{:S(2)}, u32[]{:S(2)}) collective-permute-start(bf16[4,16,1024]{2,1,0:T(8,128)(2,1)} %get-tuple-element.139), channel_id=1, source_target_pairs={{0,1},{1,2},{2,3},{3,4},{4,5},{5,6},{6,7},{8,9},{9,10},{10,11},{11... | collective-permute-start | bytes 393224 | tf_op jit(solution)/shard_map/ppermute | solution.py:965
  126.1 5.7 %query_weights.1 = (f32[512,512]{1,0:T(8,128)}, f32[8,512]{1,0:T(8,128)}) custom-call(bf16[4,512,512]{2,1,0:T(8,128)(2,1)} %get-tuple-element.144.nt_ref, f32[4,32,512]{2,1,0:T(8,128)} %get-tuple-element.145.ns_ref, bf16[4,192,512]{2,1,0:T(8,128)(2,1)} %get-tuple-element.119.refs_0_, bf16[4,320,512]{2,1,0:T(8,128)(2,1)} %get-tuple-element.123.refs_1_, ...), custom_call_target="tpu_custom_call" | custom-call | flops 1000000 | bytes 100000 | tf_op jit(solution)/shard_map/query_weights/pallas_call | solution.py:1445
  131.8 1.2 add_convert_fusion.4
  133.0 2.8 %collective-permute-start.11 = (bf16[16,4096]{1,0:T(8,128)(2,1)S(1)}, bf16[16,4096]{1,0:T(8,128)(2,1)S(1)}, u32[]{:S(2)}, u32[]{:S(2)}) collective-permute-start(bf16[16,4096]{1,0:T(8,128)(2,1)S(1)} %add_convert_fusion.4), channel_id=1, source_target_pairs={{0,4},{1,5},{2,6},{3,7},{4,0},{5,1},{6,2},{7,3},{8,12},{9,13},{10,... | collective-permute-start | bytes 393224 | tf_op jit(solution)/shard_map/ppermute | solution.py:999
  135.8 1.6 collective-permute-start.12
  137.5 0.6 copy-done.4
  138.2 8.4 %key_weights.1 = (bf16[256,2176]{1,0:T(8,128)(2,1)S(1)}, bf16[256,2176]{1,0:T(8,128)(2,1)S(1)}) custom-call(bf16[4,512,512]{2,1,0:T(8,128)(2,1)} %get-tuple-element.144.nt_ref, bf16[4,512,512]{2,1,0:T(8,128)(2,1)} %get-tuple-element.136.dk_ref.refs_2_, bf16[4,512,512]{2,1,0:T(8,128)(2,1)} %get-tuple-element.137.dv_ref.refs_3_, ...), custom_call_target="tpu_custom_call" | custom-call | flops 1000000 | bytes 100000 | tf_op jit(solution)/shard_map/key_weights/pallas_call | solution.py:1457
  146.6 0.5 collective-permute-done.12
  147.2 2.7 %collective-permute-done.14 = bf16[256,2176]{1,0:T(8,128)(2,1)S(1)} collective-permute-done((bf16[256,2176]{1,0:T(8,128)(2,1)S(1)}, bf16[256,2176]{1,0:T(8,128)(2,1)S(1)}, u32[]{:S(2)}, u32[]{:S(2)}) %collective-permute-start.14) | collective-permute-done | bytes 1114144 | tf_op jit(solution)/shard_map/ppermute | solution.py:999
  150.0 1.6 collective-permute-start.15
  151.6 10.0 %own_frames.1 = bf16[4,512,512]{2,1,0:T(8,128)(2,1)} custom-call(bf16[4,512,512]{2,1,0:T(8,128)(2,1)} %bitcast.25, bf16[4,192,512]{2,1,0:T(8,128)(2,1)} %get-tuple-element.119.refs_0_, bf16[4,320,512]{2,1,0:T(8,128)(2,1)} %get-tuple-element.123.refs_1_, bf16[4,512,512]{2,1,0:T(8,128)(2,1)} %get-tuple-element.136.dk_ref.refs_2_, ...), custom_call_target="tpu_custom_call" | custom-call | flops 1000000 | bytes 100000 | tf_op jit(solution)/shard_map/own_frames/pallas_call | solution.py:1523
  161.9 0.4 collective-permute-start.16
  162.3 6.2 %collective-permute-done.16 = bf16[64,2176]{1,0:T(8,128)(2,1)S(1)} collective-permute-done((bf16[64,2176]{1,0:T(8,128)(2,1)S(1)}, bf16[64,2176]{1,0:T(8,128)(2,1)S(1)}, u32[]{:S(2)}, u32[]{:S(2)}) %collective-permute-start.16) | collective-permute-done | bytes 278560 | tf_op jit(solution)/shard_map/ppermute | solution.py:999
  168.7 0.4 collective-permute-start.17
  169.1 1.2 add_convert_fusion.9
  170.3 2.9 %collective-permute-start.18 = (bf16[16,2176]{1,0:T(8,128)(2,1)S(1)}, bf16[16,2176]{1,0:T(8,128)(2,1)S(1)}, u32[]{:S(2)}, u32[]{:S(2)}) collective-permute-start(bf16[16,2176]{1,0:T(8,128)(2,1)S(1)} %get-tuple-element.207), channel_id=1, source_target_pairs={{0,4},{1,5},{2,6},{3,7},{4,0},{5,1},{6,2},{7,3},{8,12},{9,13},{10,... | collective-permute-start | bytes 208904 | tf_op jit(solution)/shard_map/ppermute | solution.py:999
  173.2 1.0 collective-permute-start.19
  174.2 0.6 collective-permute-start.20
  174.8 0.9 collective-permute-done.18
  175.7 2.6 %collective-permute-done.19 = bf16[16,2176]{1,0:T(8,128)(2,1)S(1)} collective-permute-done((bf16[16,2176]{1,0:T(8,128)(2,1)S(1)}, bf16[16,2176]{1,0:T(8,128)(2,1)S(1)}, u32[]{:S(2)}, u32[]{:S(2)}) %collective-permute-start.19) | collective-permute-done | bytes 69664 | tf_op jit(solution)/shard_map/ppermute | solution.py:999
  178.3 2.0 collective-permute-done.20
  180.4 0.6 copy-done.11
  181.2 0.6 collective-permute-start.21
  181.9 1.1 add_convert_fusion.8
  183.0 0.8 collective-permute-start.24
  183.7 1.0 collective-permute-start.23
  184.7 2.7 %collective-permute-start.22 = (bf16[16,2176]{1,0:T(8,128)(2,1)S(1)}, bf16[16,2176]{1,0:T(8,128)(2,1)S(1)}, u32[]{:S(2)}, u32[]{:S(2)}) collective-permute-start(bf16[16,2176]{1,0:T(8,128)(2,1)S(1)} %add_convert_fusion.8), channel_id=1, source_target_pairs={{0,6},{1,7},{2,4},{3,5},{4,2},{5,3},{6,0},{7,1},{8,14},{9,15},{10,... | collective-permute-start | bytes 208904 | tf_op jit(solution)/shard_map/ppermute | solution.py:999
  187.4 1.7 collective-permute-done.24
  189.2 0.4 collective-permute-done.23
  189.5 1.3 collective-permute-done.22
  190.9 1.4 collective-permute-start.25
  192.3 5.2 %collective-permute-done.25 = bf16[64,2176]{1,0:T(8,128)(2,1)S(1)} collective-permute-done((bf16[64,2176]{1,0:T(8,128)(2,1)S(1)}, bf16[64,2176]{1,0:T(8,128)(2,1)S(1)}, u32[]{:S(2)}, u32[]{:S(2)}) %collective-permute-start.25) | collective-permute-done | bytes 278560 | tf_op jit(solution)/shard_map/ppermute | solution.py:999
  197.5 1.5 collective-permute-done.21
  199.1 0.5 maximum_select_fusion.mine_u.mine_d
  199.7 0.6 collective-permute-start.26
  200.4 3.4 %collective-permute-done.27.other_u.other_d = bf16[256,4096]{1,0:T(8,128)(2,1)S(1)} collective-permute-done((bf16[256,4096]{1,0:T(8,128)(2,1)S(1)}, bf16[256,4096]{1,0:T(8,128)(2,1)S(1)}, u32[]{:S(2)}, u32[]{:S(2)}) %collective-permute-start.27) | collective-permute-done | bytes 2097184 | tf_op jit(solution)/shard_map/ppermute | solution.py:999
  203.8 4.0 %unpack_feed_forward.1 = (f32[512,2048]{1,0:T(8,128)}, f32[2048,512]{1,0:T(8,128)}) custom-call(s32[1]{0:T(128)} %bitcast.bit_ref.side_ref, bf16[256,4096]{1,0:T(8,128)(2,1)S(1)} %maximum_select_fusion.mine_u.mine_d, bf16[256,4096]{1,0:T(8,128)(2,1)S(1)} %collective-permute-done.27.other_u.other_d, bf16[256,4096]{1,0:T(8,128)(2,1)S(1)} %maximum_select_fusion.mine_u.mine_d, ...), custom_call_target="tpu_custom_call" | custom-call | flops 1000000 | bytes 100000 | tf_op jit(solution)/shard_map/unpack_feed_forward/pallas_call | solution.py:1555
  207.8 1.5 collective-permute-done.26
  209.3 0.2 maximum_select_fusion.1.part_ref.mine_v
  209.7 2.1 unpack_own.1
  211.8 0.6 collective-permute-done.28.part_ref.other_v
  212.4 2.3 %unpack_rest.1 = (f32[512,1536]{1,0:T(8,128)}, f32[512,512]{1,0:T(8,128)}, f32[2,512]{1,0:T(2,128)}, f32[2,512]{1,0:T(2,128)}, f32[2,512]{1,0:T(2,128)}, /*index...) custom-call(s32[1]{0:T(128)S(6)} %sub.3.side_ref, ...), custom_call_target="tpu_custom_call", output_to_operand_aliasing={{0}: (4, {}), {1}: (5, {})} | custom-call | flops 1000000 | bytes 100000 | tf_op jit(solution)/shard_map/unpack_rest/pallas_call | solution.py:1590
  (52 shorter events, 1.7 us)
Async XLA Ops:
  1.7 13.9 %collective-permute-start = (bf16[4,96,512]{2,1,0:T(8,128)(2,1)S(1)}, bf16[4,96,512]{2,1,0:T(8,128)(2,1)S(1)}, u32[]{:S(2)}, u32[]{:S(2)}) collective-permute-start(bf16[4,96,512]{2,1,0:T(8,128)(2,1)S(1)} %slice.8), channel_id=1, source_target_pairs={{0,1},{1,2},{2,3},{3,4},{4,5},{5,6},{6,7},{8,9},{9,10},{10,11},{11... | collective-permute-start | bytes 1179656 | tf_op jit(solution)/shard_map/ppermute | solution.py:965
  4.9 10.6 %collective-permute-start.1 = (bf16[4,16,512]{2,1,0:T(8,128)(2,1)S(1)}, bf16[4,16,512]{2,1,0:T(8,128)(2,1)S(1)}, u32[]{:S(2)}, u32[]{:S(2)}) collective-permute-start(bf16[4,16,512]{2,1,0:T(8,128)(2,1)S(1)} %slice.9), channel_id=1, source_target_pairs={{1,0},{2,1},{3,2},{4,3},{5,4},{6,5},{7,6},{9,8},{10,9},{11,10},{12... | collective-permute-start | bytes 196616 | tf_op jit(solution)/shard_map/ppermute | solution.py:965
  15.6 0.6 copy-start.13
  15.6 0.7 copy-start.5
  74.5 11.3 %collective-permute-start.2 = (bf16[256,4096]{1,0:T(8,128)(2,1)}, bf16[256,4096]{1,0:T(8,128)(2,1)}, u32[]{:S(2)}, u32[]{:S(2)}) collective-permute-start(bf16[256,4096]{1,0:T(8,128)(2,1)} %get-tuple-element.120), channel_id=1, source_target_pairs={{0,1},{1,0},{2,3},{3,2},{4,5},{5,4},{6,7},{7,6},{8,9},{9,8},{10,11... | collective-permute-start | bytes 6291464 | tf_op jit(solution)/shard_map/ppermute | solution.py:999
  77.8 8.0 %copy-start = (bf16[256,4096]{1,0:T(8,128)(2,1)S(1)}, bf16[256,4096]{1,0:T(8,128)(2,1)}, u32[]{:S(2)}) copy-start(bf16[256,4096]{1,0:T(8,128)(2,1)} %get-tuple-element.130) | copy-start | bytes 6291460
  85.8 3.1 %copy-start.14 = (bf16[4,16,1024]{2,1,0:T(8,128)(2,1)S(1)}, bf16[4,16,1024]{2,1,0:T(8,128)(2,1)}, u32[]{:S(2)}) copy-start(bf16[4,16,1024]{2,1,0:T(8,128)(2,1)} %get-tuple-element.133) | copy-start | bytes 393220
  87.3 15.0 %collective-permute-start.3 = (bf16[128,4096]{1,0:T(8,128)(2,1)S(1)}, bf16[128,4096]{1,0:T(8,128)(2,1)}, u32[]{:S(2)}, u32[]{:S(2)}) collective-permute-start(bf16[128,4096]{1,0:T(8,128)(2,1)S(1)} %add_convert_fusion), channel_id=1, source_target_pairs={{0,8},{1,17},{2,10},{3,19},{4,12},{5,21},{6,14},{7,23},{8,0},{9,25... | collective-permute-start | bytes 3145736 | tf_op jit(solution)/shard_map/ppermute | solution.py:999
  88.9 13.4 %collective-permute-start.4 = (bf16[4,16,1024]{2,1,0:T(8,128)(2,1)S(1)}, bf16[4,16,1024]{2,1,0:T(8,128)(2,1)S(1)}, u32[]{:S(2)}, u32[]{:S(2)}) collective-permute-start(bf16[4,16,1024]{2,1,0:T(8,128)(2,1)S(1)} %copy-done.14), channel_id=1, source_target_pairs={{1,0},{2,1},{3,2},{4,3},{5,4},{6,5},{7,6},{9,8},{10,9},{11,10},{12... | collective-permute-start | bytes 393224 | tf_op jit(solution)/shard_map/ppermute | solution.py:965
  102.3 3.2 %copy-start.6 = (bf16[4,16,1024]{2,1,0:T(8,128)(2,1)}, bf16[4,16,1024]{2,1,0:T(8,128)(2,1)S(1)}, u32[]{:S(2)}) copy-start(bf16[4,16,1024]{2,1,0:T(8,128)(2,1)S(1)} %collective-permute-done.4.refs_6_) | copy-start | bytes 393220
  103.9 11.6 %collective-permute-start.7 = (bf16[64,4096]{1,0:T(8,128)(2,1)S(1)}, bf16[64,4096]{1,0:T(8,128)(2,1)S(1)}, u32[]{:S(2)}, u32[]{:S(2)}) collective-permute-start(bf16[64,4096]{1,0:T(8,128)(2,1)S(1)} %add_convert_fusion.2), channel_id=1, source_target_pairs={{0,16},{1,9},{2,18},{3,11},{4,20},{5,13},{6,22},{7,15},{8,24},{9,1... | collective-permute-start | bytes 1572872 | tf_op jit(solution)/shard_map/ppermute | solution.py:999
  117.3 14.5 %collective-permute-start.8 = (bf16[16,4096]{1,0:T(8,128)(2,1)S(1)}, bf16[16,4096]{1,0:T(8,128)(2,1)S(1)}, u32[]{:S(2)}, u32[]{:S(2)}) collective-permute-start(bf16[16,4096]{1,0:T(8,128)(2,1)S(1)} %get-tuple-element.204), channel_id=1, source_target_pairs={{0,4},{1,5},{2,6},{3,7},{4,0},{5,1},{6,2},{7,3},{8,12},{9,13},{10,... | collective-permute-start | bytes 393224 | tf_op jit(solution)/shard_map/ppermute | solution.py:999
  120.0 11.7 %collective-permute-start.9 = (bf16[16,4096]{1,0:T(8,128)(2,1)S(1)}, bf16[16,4096]{1,0:T(8,128)(2,1)S(1)}, u32[]{:S(2)}, u32[]{:S(2)}) collective-permute-start(bf16[16,4096]{1,0:T(8,128)(2,1)S(1)} %get-tuple-element.203), channel_id=1, source_target_pairs={{0,2},{1,3},{2,0},{3,1},{4,6},{5,7},{6,4},{7,5},{8,10},{9,11},{10,... | collective-permute-start | bytes 393224 | tf_op jit(solution)/shard_map/ppermute | solution.py:999
  121.6 10.2 %collective-permute-start.10 = (bf16[16,4096]{1,0:T(8,128)(2,1)S(1)}, bf16[16,4096]{1,0:T(8,128)(2,1)S(1)}, u32[]{:S(2)}, u32[]{:S(2)}) collective-permute-start(bf16[16,4096]{1,0:T(8,128)(2,1)S(1)} %get-tuple-element.202), channel_id=1, source_target_pairs={{0,6},{1,7},{2,4},{3,5},{4,2},{5,3},{6,0},{7,1},{8,14},{9,15},{10,... | collective-permute-start | bytes 393224 | tf_op jit(solution)/shard_map/ppermute | solution.py:999
  121.7 15.7 %collective-permute-start.5 = (bf16[4,32,1024]{2,1,0:T(8,128)(2,1)}, bf16[4,32,1024]{2,1,0:T(8,128)(2,1)S(1)}, u32[]{:S(2)}, u32[]{:S(2)}) collective-permute-start(bf16[4,32,1024]{2,1,0:T(8,128)(2,1)} %get-tuple-element.138), channel_id=1, source_target_pairs={{1,0},{2,1},{3,2},{4,3},{5,4},{6,5},{7,6},{9,8},{10,9},{11,10},{12... | collective-permute-start | bytes 786440 | tf_op jit(solution)/shard_map/ppermute | solution.py:965
  123.0 14.4 %collective-permute-start.6 = (bf16[4,16,1024]{2,1,0:T(8,128)(2,1)}, bf16[4,16,1024]{2,1,0:T(8,128)(2,1)S(1)}, u32[]{:S(2)}, u32[]{:S(2)}) collective-permute-start(bf16[4,16,1024]{2,1,0:T(8,128)(2,1)} %get-tuple-element.139), channel_id=1, source_target_pairs={{0,1},{1,2},{2,3},{3,4},{4,5},{5,6},{6,7},{8,9},{9,10},{10,11},{11... | collective-permute-start | bytes 393224 | tf_op jit(solution)/shard_map/ppermute | solution.py:965
  133.0 13.6 %collective-permute-start.11 = (bf16[16,4096]{1,0:T(8,128)(2,1)S(1)}, bf16[16,4096]{1,0:T(8,128)(2,1)S(1)}, u32[]{:S(2)}, u32[]{:S(2)}) collective-permute-start(bf16[16,4096]{1,0:T(8,128)(2,1)S(1)} %add_convert_fusion.4), channel_id=1, source_target_pairs={{0,4},{1,5},{2,6},{3,7},{4,0},{5,1},{6,2},{7,3},{8,12},{9,13},{10,... | collective-permute-start | bytes 393224 | tf_op jit(solution)/shard_map/ppermute | solution.py:999
  135.8 11.4 %collective-permute-start.12 = (bf16[16,4096]{1,0:T(8,128)(2,1)S(1)}, bf16[16,4096]{1,0:T(8,128)(2,1)S(1)}, u32[]{:S(2)}, u32[]{:S(2)}) collective-permute-start(bf16[16,4096]{1,0:T(8,128)(2,1)S(1)} %add_convert_fusion.4), channel_id=1, source_target_pairs={{0,2},{1,3},{2,0},{3,1},{4,6},{5,7},{6,4},{7,5},{8,10},{9,11},{10,... | collective-permute-start | bytes 393224 | tf_op jit(solution)/shard_map/ppermute | solution.py:999
  137.4 9.8 %collective-permute-start.13 = (bf16[16,4096]{1,0:T(8,128)(2,1)S(1)}, bf16[16,4096]{1,0:T(8,128)(2,1)S(1)}, u32[]{:S(2)}, u32[]{:S(2)}) collective-permute-start(bf16[16,4096]{1,0:T(8,128)(2,1)S(1)} %add_convert_fusion.4), channel_id=1, source_target_pairs={{0,6},{1,7},{2,4},{3,5},{4,2},{5,3},{6,0},{7,1},{8,14},{9,15},{10,... | collective-permute-start | bytes 393224 | tf_op jit(solution)/shard_map/ppermute | solution.py:999
  137.5 0.6 copy-start.4
  137.5 0.7 copy-start.2
  147.2 2.8 %collective-permute-start.14 = (bf16[256,2176]{1,0:T(8,128)(2,1)S(1)}, bf16[256,2176]{1,0:T(8,128)(2,1)S(1)}, u32[]{:S(2)}, u32[]{:S(2)}) collective-permute-start(bf16[256,2176]{1,0:T(8,128)(2,1)S(1)} %get-tuple-element.168), channel_id=1, source_target_pairs={{0,1},{1,0},{2,3},{3,2},{4,5},{5,4},{6,7},{7,6},{8,9},{9,8},{10,11... | collective-permute-start | bytes 3342344 | tf_op jit(solution)/shard_map/ppermute | solution.py:999
  149.9 11.7 %copy-start.1 = (bf16[256,2176]{1,0:T(8,128)(2,1)}, bf16[256,2176]{1,0:T(8,128)(2,1)S(1)}, u32[]{:S(2)}) copy-start(bf16[256,2176]{1,0:T(8,128)(2,1)S(1)} %collective-permute-done.14) | copy-start | bytes 3342340
  150.0 11.6 %collective-permute-start.15 = (bf16[128,2176]{1,0:T(8,128)(2,1)S(1)}, bf16[128,2176]{1,0:T(8,128)(2,1)S(1)}, u32[]{:S(2)}, u32[]{:S(2)}) collective-permute-start(bf16[128,2176]{1,0:T(8,128)(2,1)S(1)} %add_convert_fusion.1), channel_id=1, source_target_pairs={{0,8},{1,17},{2,10},{3,19},{4,12},{5,21},{6,14},{7,23},{8,0},{9,25... | collective-permute-start | bytes 1671176 | tf_op jit(solution)/shard_map/ppermute | solution.py:999
  161.7 18.7 %copy-start.3 = (bf16[128,2176]{1,0:T(8,128)(2,1)}, bf16[128,2176]{1,0:T(8,128)(2,1)S(1)}, u32[]{:S(2)}) copy-start(bf16[128,2176]{1,0:T(8,128)(2,1)S(1)} %collective-permute-done.15) | copy-start | bytes 1671172
  161.9 6.6 %collective-permute-start.16 = (bf16[64,2176]{1,0:T(8,128)(2,1)S(1)}, bf16[64,2176]{1,0:T(8,128)(2,1)S(1)}, u32[]{:S(2)}, u32[]{:S(2)}) collective-permute-start(bf16[64,2176]{1,0:T(8,128)(2,1)S(1)} %add_convert_fusion.3), channel_id=1, source_target_pairs={{0,16},{1,9},{2,18},{3,11},{4,20},{5,13},{6,22},{7,15},{8,24},{9,1... | collective-permute-start | bytes 835592 | tf_op jit(solution)/shard_map/ppermute | solution.py:999
  168.7 12.3 %collective-permute-start.17 = (bf16[64,4096]{1,0:T(8,128)(2,1)S(1)}, bf16[64,4096]{1,0:T(8,128)(2,1)S(1)}, u32[]{:S(2)}, u32[]{:S(2)}) collective-permute-start(bf16[64,4096]{1,0:T(8,128)(2,1)S(1)} %maximum_select_fusion.4), channel_id=1, source_target_pairs={{0,16},{1,9},{2,18},{3,11},{4,20},{5,13},{6,22},{7,15},{8,24},{9,1... | collective-permute-start | bytes 1572872 | tf_op jit(solution)/shard_map/ppermute | solution.py:999
  170.3 5.4 %collective-permute-start.18 = (bf16[16,2176]{1,0:T(8,128)(2,1)S(1)}, bf16[16,2176]{1,0:T(8,128)(2,1)S(1)}, u32[]{:S(2)}, u32[]{:S(2)}) collective-permute-start(bf16[16,2176]{1,0:T(8,128)(2,1)S(1)} %get-tuple-element.207), channel_id=1, source_target_pairs={{0,4},{1,5},{2,6},{3,7},{4,0},{5,1},{6,2},{7,3},{8,12},{9,13},{10,... | collective-permute-start | bytes 208904 | tf_op jit(solution)/shard_map/ppermute | solution.py:999
  173.2 5.1 %collective-permute-start.19 = (bf16[16,2176]{1,0:T(8,128)(2,1)S(1)}, bf16[16,2176]{1,0:T(8,128)(2,1)S(1)}, u32[]{:S(2)}, u32[]{:S(2)}) collective-permute-start(bf16[16,2176]{1,0:T(8,128)(2,1)S(1)} %get-tuple-element.206), channel_id=1, source_target_pairs={{0,2},{1,3},{2,0},{3,1},{4,6},{5,7},{6,4},{7,5},{8,10},{9,11},{10,... | collective-permute-start | bytes 208904 | tf_op jit(solution)/shard_map/ppermute | solution.py:999
  174.2 6.1 %collective-permute-start.20 = (bf16[16,2176]{1,0:T(8,128)(2,1)S(1)}, bf16[16,2176]{1,0:T(8,128)(2,1)S(1)}, u32[]{:S(2)}, u32[]{:S(2)}) collective-permute-start(bf16[16,2176]{1,0:T(8,128)(2,1)S(1)} %get-tuple-element.205), channel_id=1, source_target_pairs={{0,6},{1,7},{2,4},{3,5},{4,2},{5,3},{6,0},{7,1},{8,14},{9,15},{10,... | collective-permute-start | bytes 208904 | tf_op jit(solution)/shard_map/ppermute | solution.py:999
  175.7 4.6 %copy-start.7 = (bf16[16,2176]{1,0:T(8,128)(2,1)}, bf16[16,2176]{1,0:T(8,128)(2,1)S(1)}, u32[]{:S(2)}) copy-start(bf16[16,2176]{1,0:T(8,128)(2,1)S(1)} %collective-permute-done.18) | copy-start | bytes 208900
  178.3 2.0 copy-start.9
  180.3 0.6 copy-start.11
  181.0 0.9 copy-start.8
  181.0 0.9 copy-start.10
  181.0 0.9 copy-start.12
  181.2 17.8 %collective-permute-start.21 = (bf16[128,4096]{1,0:T(8,128)(2,1)S(1)}, bf16[128,4096]{1,0:T(8,128)(2,1)S(1)}, u32[]{:S(2)}, u32[]{:S(2)}) collective-permute-start(bf16[128,4096]{1,0:T(8,128)(2,1)S(1)} %maximum_select_fusion.2), channel_id=1, source_target_pairs={{0,8},{1,17},{2,10},{3,19},{4,12},{5,21},{6,14},{7,23},{8,0},{9,25... | collective-permute-start | bytes 3145736 | tf_op jit(solution)/shard_map/ppermute | solution.py:999
  183.0 6.2 %collective-permute-start.24 = (bf16[16,2176]{1,0:T(8,128)(2,1)S(1)}, bf16[16,2176]{1,0:T(8,128)(2,1)S(1)}, u32[]{:S(2)}, u32[]{:S(2)}) collective-permute-start(bf16[16,2176]{1,0:T(8,128)(2,1)S(1)} %add_convert_fusion.8), channel_id=1, source_target_pairs={{0,4},{1,5},{2,6},{3,7},{4,0},{5,1},{6,2},{7,3},{8,12},{9,13},{10,... | collective-permute-start | bytes 208904 | tf_op jit(solution)/shard_map/ppermute | solution.py:999
  183.7 5.8 %collective-permute-start.23 = (bf16[16,2176]{1,0:T(8,128)(2,1)S(1)}, bf16[16,2176]{1,0:T(8,128)(2,1)S(1)}, u32[]{:S(2)}, u32[]{:S(2)}) collective-permute-start(bf16[16,2176]{1,0:T(8,128)(2,1)S(1)} %add_convert_fusion.8), channel_id=1, source_target_pairs={{0,2},{1,3},{2,0},{3,1},{4,6},{5,7},{6,4},{7,5},{8,10},{9,11},{10,... | collective-permute-start | bytes 208904 | tf_op jit(solution)/shard_map/ppermute | solution.py:999
  184.7 6.1 %collective-permute-start.22 = (bf16[16,2176]{1,0:T(8,128)(2,1)S(1)}, bf16[16,2176]{1,0:T(8,128)(2,1)S(1)}, u32[]{:S(2)}, u32[]{:S(2)}) collective-permute-start(bf16[16,2176]{1,0:T(8,128)(2,1)S(1)} %add_convert_fusion.8), channel_id=1, source_target_pairs={{0,6},{1,7},{2,4},{3,5},{4,2},{5,3},{6,0},{7,1},{8,14},{9,15},{10,... | collective-permute-start | bytes 208904 | tf_op jit(solution)/shard_map/ppermute | solution.py:999
  190.9 6.6 %collective-permute-start.25 = (bf16[64,2176]{1,0:T(8,128)(2,1)S(1)}, bf16[64,2176]{1,0:T(8,128)(2,1)S(1)}, u32[]{:S(2)}, u32[]{:S(2)}) collective-permute-start(bf16[64,2176]{1,0:T(8,128)(2,1)S(1)} %maximum_select_fusion.7), channel_id=1, source_target_pairs={{0,16},{1,9},{2,18},{3,11},{4,20},{5,13},{6,22},{7,15},{8,24},{9,1... | collective-permute-start | bytes 835592 | tf_op jit(solution)/shard_map/ppermute | solution.py:999
  199.6 4.2 %collective-permute-start.27 = (bf16[256,4096]{1,0:T(8,128)(2,1)S(1)}, bf16[256,4096]{1,0:T(8,128)(2,1)S(1)}, u32[]{:S(2)}, u32[]{:S(2)}) collective-permute-start(bf16[256,4096]{1,0:T(8,128)(2,1)S(1)} %maximum_select_fusion.mine_u.mine_d), channel_id=1, source_target_pairs={{0,1},{1,0},{2,3},{3,2},{4,5},{5,4},{6,7},{7,6},{8,9},{9,8},{10,11... | collective-permute-start | bytes 6291464 | tf_op jit(solution)/shard_map/ppermute | solution.py:999
  199.7 9.6 %collective-permute-start.26 = (bf16[128,2176]{1,0:T(8,128)(2,1)S(1)}, bf16[128,2176]{1,0:T(8,128)(2,1)S(1)}, u32[]{:S(2)}, u32[]{:S(2)}) collective-permute-start(bf16[128,2176]{1,0:T(8,128)(2,1)S(1)} %maximum_select_fusion.3), channel_id=1, source_target_pairs={{0,8},{1,17},{2,10},{3,19},{4,12},{5,21},{6,14},{7,23},{8,0},{9,25... | collective-permute-start | bytes 1671176 | tf_op jit(solution)/shard_map/ppermute | solution.py:999
  209.6 2.8 %collective-permute-start.28 = (bf16[256,2176]{1,0:T(8,128)(2,1)S(1)}, bf16[256,2176]{1,0:T(8,128)(2,1)S(1)}, u32[]{:S(2)}, u32[]{:S(2)}) collective-permute-start(bf16[256,2176]{1,0:T(8,128)(2,1)S(1)} %maximum_select_fusion.1.part_ref.mine_v), channel_id=1, source_target_pairs={{0,1},{1,0},{2,3},{3,2},{4,5},{5,4},{6,7},{7,6},{8,9},{9,8},{10,11... | collective-permute-start | bytes 3342344 | tf_op jit(solution)/shard_map/ppermute | solution.py:999

commit v2 on v1

--- a/solution.py
+++ b/solution.py
@@ -377,13 +377,11 @@
     memory = (dot(jnp.concatenate(sums, 0), ow_ref[...]) + ob_ref[...]).astype(bf16)
     mk = dot(memory, w_ref[:, D : 2 * D]).astype(bf16)
     mv = (dot(memory, w_ref[:, 2 * D :]) + qvb_ref[1:2]).astype(bf16)
-    both = jnp.concatenate([mk, mv], 1)
     for r in range(rows):
         here = slice(r * (16 + sp), (r + 1) * (16 + sp))
         memory_ref[r] = memory[here][16:]
-        spread = dot(expand_ref[...], both[here]).astype(bf16)
-        mkg_ref[r] = spread[:, :D]
-        mvg_ref[r] = spread[:, D:]
+        mkg_ref[r] = dot(expand_ref[...], mk[here]).astype(bf16)
+        mvg_ref[r] = dot(expand_ref[...], mv[here]).astype(bf16)
     for value, out, sem in zip((mkg_ref, mvg_ref, summary_ref, memory_ref, ps_ref), early_refs, range(5)):
         pltpu.make_async_copy(value, out, early_sem.at[sem]).start()
     for store in stores:
@@ -523,7 +521,7 @@
     n2t_s[D:] = jnp.ones((16, x_ref.shape[0]), bf16)
 
     tb = x_ref.shape[0]
-    chunk = min(512, tb)
+    chunk = min(256, tb)
 
     def gelu_rows(i, few):
         half = slice((i % 2) * wide, (i % 2 + 1) * wide)
@@ -541,12 +539,13 @@
 
         for r0 in range(0, tb, chunk):
             rows = slice(r0, r0 + chunk)
+            some(2)
             if j < tiles:
                 cols = slice(j * wide, (j + 1) * wide)
                 up_s[j % 2][rows] = dot(n2_s[rows], uw_ref[:, cols]) + ub_ref[:, cols]
-                some(3)
+                some(1)
                 da_s[j % 2][rows] = dot_nt(c_ref[rows], dw_ref[cols, :]).astype(bf16)
-            some(3)
+            some(1)
             if j >= 2 and j % 2:
                 i = j - 2
                 both = slice((i - 1) * wide, (i + 1) * wide)
@@ -1339,7 +1338,7 @@
 
     ff_sum = Running(exchange, ff_keep, ff_send)
 
-    cut = groups * 3 // 8
+    cut = groups * 2 // 8
     parts = [(0, cut), (cut, groups)] if cut else [(0, groups)]
     dqs, dks, dvs, dms = [], [], [], []
     for g0, g1 in parts:

time: 216 us -> 215 us (level)
  no operation moved by 1% of the time
where the time goes in v2:
time: 215 us; the launch traced here: 214 us
  Pallas kernels  129 us (60%)
  starting transfers between devices  39.9 us (19%)
  waiting for transfers between devices  30.5 us (14%)
  other arithmetic  9.95 us (5%)
  local copies, waits for them, and re-layouts  4.08 us (2%)
    pallas_call x1, Pallas kernels, local(): pl.pallas_call(functools.partial(ff_kernel, tiles), grid=(tokens // tb,),...  41.8 us
    ppermute x24, starting transfers between devices, send(): return lax.ppermute(part, ('dp', 'tm'), pairs)  30.7 us
    ppermute x24, waiting for transfers between devices, send(): return lax.ppermute(part, ('dp', 'tm'), pairs)  30.5 us
    pallas_call x2, Pallas kernels, local(): pl.pallas_call(functools.partial(attend_back_kernel, g0, g1), grid=(rows,...  18.7 us
    pallas_call x1, Pallas kernels, local(): pl.pallas_call(functools.partial(memory_kernel, groups, total, utts), gri...  16.5 us
    pallas_call x1, Pallas kernels, local(): pl.pallas_call(functools.partial(memory_back_kernel, parts), grid=(1,), i...  10 us
    pallas_call x1, Pallas kernels, local(): pl.pallas_call(functools.partial(own_frames_kernel, len(dqs)), grid=(rows...  9.97 us
    pallas_call x1, Pallas kernels, local(): pl.pallas_call(own_kernel, grid=(rows,), in_specs=[row_spec((t, D)), cons...  9.34 us
  transfers between devices with their start and end apart: 29, of which 15 were waited for; matrix products, arithmetic and copies ran while one was open for 2% of the time, Pallas kernels for 32%

profile of v2, /device:TPU:0, one launch (start us, length us, event | category | flops | bytes accessed | tf_op | source)
XLA Modules:
  0.0 214.5 jit_solution(9296013311672796568)
XLA Ops:
  0.6 1.0 slice.8
  1.7 2.4 %collective-permute-start = (bf16[4,96,512]{2,1,0:T(8,128)(2,1)S(1)}, bf16[4,96,512]{2,1,0:T(8,128)(2,1)S(1)}, u32[]{:S(2)}, u32[]{:S(2)}) collective-permute-start(bf16[4,96,512]{2,1,0:T(8,128)(2,1)S(1)} %slice.8), channel_id=1, source_target_pairs={{0,1},{1,2},{2,3},{3,4},{4,5},{5,6},{6,7},{8,9},{9,10},{10,11},{11... | collective-permute-start | bytes 1179656 | tf_op jit(solution)/shard_map/ppermute | solution.py:964
  4.1 0.8 slice.9
  4.9 1.3 collective-permute-start.1
  6.2 9.3 %own.1 = (bf16[4,512,512]{2,1,0:T(8,128)(2,1)}, bf16[4,624,512]{2,1,0:T(8,128)(2,1)}, bf16[4,624,512]{2,1,0:T(8,128)(2,1)}, bf16[4,512,512]{2,1,0:T(8,128)(2,1)}...) custom-call(bf16[4,512,512]{2,1,0:T(8,128)(2,1)} %bitcast.23, f32[2,512]{1,0:T(2,128)} %refs_8_.2, ...), custom_call_target="tpu_custom_call" | custom-call | flops 1000000 | bytes 100000 | tf_op jit(solution)/shard_map/own/pallas_call | solution.py:1145
  15.6 0.6 copy-done.13
  16.3 16.5 %attend.1 = (bf16[4,624,512]{2,1,0:T(8,128)(2,1)}, bf16[4,624,512]{2,1,0:T(8,128)(2,1)}, bf16[4,128,512]{2,1,0:T(8,128)(2,1)}, bf16[4,128,512]{2,1,0:T(8,128)(2,...) custom-call(s32[2]{0:T(128)} %len_ref.1, ...), custom_call_target="tpu_custom_call", output_to_operand_aliasing={{0}: (13, {}), {1}: (14, {})} | custom-call | flops 1000000 | bytes 100000 | tf_op jit(solution)/shard_map/attend/pallas_call | solution.py:1182
  32.8 41.8 %feed_forward.1 = (bf16[2048,512]{1,0:T(8,128)(2,1)}, bf16[2048,512]{1,0:T(8,128)(2,1)}, bf16[2048,512]{1,0:T(8,128)(2,1)}, bf16[256,4096]{1,0:T(8,128)(2,1)}, b...) custom-call(s32[1]{0:T(128)} %bitcast.bit_ref.side_ref, ...), custom_call_target="tpu_custom_call" | custom-call | flops 1000000 | bytes 100000 | tf_op jit(solution)/shard_map/feed_forward/pallas_call | solution.py:1264
  74.6 3.3 %collective-permute-start.2 = (bf16[256,4096]{1,0:T(8,128)(2,1)}, bf16[256,4096]{1,0:T(8,128)(2,1)}, u32[]{:S(2)}, u32[]{:S(2)}) collective-permute-start(bf16[256,4096]{1,0:T(8,128)(2,1)} %get-tuple-element.120), channel_id=1, source_target_pairs={{0,1},{1,0},{2,3},{3,2},{4,5},{5,4},{6,7},{7,6},{8,9},{9,8},{10,11... | collective-permute-start | bytes 6291464 | tf_op jit(solution)/shard_map/ppermute | solution.py:998
  77.9 7.2 %attend_back.2 = (bf16[4,128,512]{2,1,0:T(8,128)(2,1)}, bf16[4,176,512]{2,1,0:T(8,128)(2,1)}, bf16[4,176,512]{2,1,0:T(8,128)(2,1)}, bf16[4,32,1024]{2,1,0:T(8,128)(2,1)}, bf16[4,16,1024]{2,1,0:T(8,128)(2,1)}) custom-call(bf16[4,512,512]{2,1,0:T(8,128)(2,1)} %get-tuple-element.110.q_ref, bf16[4,624,512]{2,1,0:T(8,128)(2,1)} %get-tuple-element.113.kext_ref.refs_13_, ...), custom_call_target="tpu_custom_call" | custom-call | flops 1000000 | bytes 100000 | tf_op jit(solution)/shard_map/attend_back/pallas_call | solution.py:1349
  85.2 1.5 add_convert_fusion
  86.7 1.6 collective-permute-start.3
  88.3 1.3 collective-permute-start.4
  89.6 11.5 %attend_back.3 = (bf16[4,384,512]{2,1,0:T(8,128)(2,1)}, bf16[4,432,512]{2,1,0:T(8,128)(2,1)}, bf16[4,432,512]{2,1,0:T(8,128)(2,1)}, bf16[4,96,1024]{2,1,0:T(8,128)(2,1)}, bf16[4,16,1024]{2,1,0:T(8,128)(2,1)}) custom-call(bf16[4,512,512]{2,1,0:T(8,128)(2,1)} %get-tuple-element.110.q_ref, bf16[4,624,512]{2,1,0:T(8,128)(2,1)} %get-tuple-element.113.kext_ref.refs_13_, ...), custom_call_target="tpu_custom_call" | custom-call | flops 1000000 | bytes 100000 | tf_op jit(solution)/shard_map/attend_back/pallas_call | solution.py:1349
  101.1 0.6 collective-permute-done.3
  101.6 1.6 add_convert_fusion.2
  103.3 1.6 collective-permute-start.7
  104.8 10.0 %memory_back.1 = (bf16[4,512,512]{2,1,0:T(8,128)(2,1)}, bf16[4,512,512]{2,1,0:T(8,128)(2,1)}, bf16[4,32,1024]{2,1,0:T(8,128)(2,1)}, bf16[4,16,1024]{2,1,0:T(8,12...) custom-call(bf16[4,32,1024]{2,1,0:T(8,128)(2,1)} %get-tuple-element.124.refs_0_, ...), custom_call_target="tpu_custom_call" | custom-call | flops 1000000 | bytes 100000 | tf_op jit(solution)/shard_map/memory_back/pallas_call | solution.py:1387
  114.9 1.8 add_convert_fusion.5
  116.6 2.8 %collective-permute-start.8 = (bf16[16,4096]{1,0:T(8,128)(2,1)S(1)}, bf16[16,4096]{1,0:T(8,128)(2,1)S(1)}, u32[]{:S(2)}, u32[]{:S(2)}) collective-permute-start(bf16[16,4096]{1,0:T(8,128)(2,1)S(1)} %get-tuple-element.204), channel_id=1, source_target_pairs={{0,4},{1,5},{2,6},{3,7},{4,0},{5,1},{6,2},{7,3},{8,12},{9,13},{10,... | collective-permute-start | bytes 393224 | tf_op jit(solution)/shard_map/ppermute | solution.py:998
  119.5 1.6 collective-permute-start.9
  121.1 1.3 collective-permute-start.5
  122.4 3.0 %collective-permute-start.6 = (bf16[4,16,1024]{2,1,0:T(8,128)(2,1)}, bf16[4,16,1024]{2,1,0:T(8,128)(2,1)S(1)}, u32[]{:S(2)}, u32[]{:S(2)}) collective-permute-start(bf16[4,16,1024]{2,1,0:T(8,128)(2,1)} %get-tuple-element.139), channel_id=1, source_target_pairs={{0,1},{1,2},{2,3},{3,4},{4,5},{5,6},{6,7},{8,9},{9,10},{10,11},{11... | collective-permute-start | bytes 393224 | tf_op jit(solution)/shard_map/ppermute | solution.py:964
  125.4 5.7 %query_weights.1 = (f32[512,512]{1,0:T(8,128)}, f32[8,512]{1,0:T(8,128)}) custom-call(bf16[4,512,512]{2,1,0:T(8,128)(2,1)} %get-tuple-element.144.nt_ref, f32[4,32,512]{2,1,0:T(8,128)} %get-tuple-element.145.ns_ref, bf16[4,128,512]{2,1,0:T(8,128)(2,1)} %get-tuple-element.119.refs_0_, bf16[4,384,512]{2,1,0:T(8,128)(2,1)} %get-tuple-element.123.refs_1_, ...), custom_call_target="tpu_custom_call" | custom-call | flops 1000000 | bytes 100000 | tf_op jit(solution)/shard_map/query_weights/pallas_call | solution.py:1444
  131.2 1.2 add_convert_fusion.4
  132.4 3.1 %collective-permute-start.11 = (bf16[16,4096]{1,0:T(8,128)(2,1)S(1)}, bf16[16,4096]{1,0:T(8,128)(2,1)S(1)}, u32[]{:S(2)}, u32[]{:S(2)}) collective-permute-start(bf16[16,4096]{1,0:T(8,128)(2,1)S(1)} %add_convert_fusion.4), channel_id=1, source_target_pairs={{0,4},{1,5},{2,6},{3,7},{4,0},{5,1},{6,2},{7,3},{8,12},{9,13},{10,... | collective-permute-start | bytes 393224 | tf_op jit(solution)/shard_map/ppermute | solution.py:998
  135.5 1.3 collective-permute-start.12
  136.8 0.2 collective-permute-start.13
  137.1 0.6 copy-done.4
  137.8 8.4 %key_weights.1 = (bf16[256,2176]{1,0:T(8,128)(2,1)S(1)}, bf16[256,2176]{1,0:T(8,128)(2,1)S(1)}) custom-call(bf16[4,512,512]{2,1,0:T(8,128)(2,1)} %get-tuple-element.144.nt_ref, bf16[4,512,512]{2,1,0:T(8,128)(2,1)} %get-tuple-element.136.dk_ref.refs_2_, bf16[4,512,512]{2,1,0:T(8,128)(2,1)} %get-tuple-element.137.dv_ref.refs_3_, ...), custom_call_target="tpu_custom_call" | custom-call | flops 1000000 | bytes 100000 | tf_op jit(solution)/shard_map/key_weights/pallas_call | solution.py:1456
  146.2 0.5 collective-permute-done.12
  146.7 2.8 %collective-permute-done.14 = bf16[256,2176]{1,0:T(8,128)(2,1)S(1)} collective-permute-done((bf16[256,2176]{1,0:T(8,128)(2,1)S(1)}, bf16[256,2176]{1,0:T(8,128)(2,1)S(1)}, u32[]{:S(2)}, u32[]{:S(2)}) %collective-permute-start.14) | collective-permute-done | bytes 1114144 | tf_op jit(solution)/shard_map/ppermute | solution.py:998
  149.6 1.5 collective-permute-start.15
  151.0 10.0 %own_frames.1 = bf16[4,512,512]{2,1,0:T(8,128)(2,1)} custom-call(bf16[4,512,512]{2,1,0:T(8,128)(2,1)} %bitcast.25, bf16[4,128,512]{2,1,0:T(8,128)(2,1)} %get-tuple-element.119.refs_0_, bf16[4,384,512]{2,1,0:T(8,128)(2,1)} %get-tuple-element.123.refs_1_, bf16[4,512,512]{2,1,0:T(8,128)(2,1)} %get-tuple-element.136.dk_ref.refs_2_, ...), custom_call_target="tpu_custom_call" | custom-call | flops 1000000 | bytes 100000 | tf_op jit(solution)/shard_map/own_frames/pallas_call | solution.py:1522
  161.2 0.9 collective-permute-start.16
  162.2 5.7 %collective-permute-done.16 = bf16[64,2176]{1,0:T(8,128)(2,1)S(1)} collective-permute-done((bf16[64,2176]{1,0:T(8,128)(2,1)S(1)}, bf16[64,2176]{1,0:T(8,128)(2,1)S(1)}, u32[]{:S(2)}, u32[]{:S(2)}) %collective-permute-start.16) | collective-permute-done | bytes 278560 | tf_op jit(solution)/shard_map/ppermute | solution.py:998
  168.0 0.9 collective-permute-start.17
  169.0 1.2 add_convert_fusion.9
  170.2 2.9 %collective-permute-start.18 = (bf16[16,2176]{1,0:T(8,128)(2,1)S(1)}, bf16[16,2176]{1,0:T(8,128)(2,1)S(1)}, u32[]{:S(2)}, u32[]{:S(2)}) collective-permute-start(bf16[16,2176]{1,0:T(8,128)(2,1)S(1)} %get-tuple-element.207), channel_id=1, source_target_pairs={{0,4},{1,5},{2,6},{3,7},{4,0},{5,1},{6,2},{7,3},{8,12},{9,13},{10,... | collective-permute-start | bytes 208904 | tf_op jit(solution)/shard_map/ppermute | solution.py:998
  173.1 0.8 collective-permute-start.19
  173.9 0.8 collective-permute-start.20
  174.6 1.1 collective-permute-done.18
  175.7 2.4 %collective-permute-done.19 = bf16[16,2176]{1,0:T(8,128)(2,1)S(1)} collective-permute-done((bf16[16,2176]{1,0:T(8,128)(2,1)S(1)}, bf16[16,2176]{1,0:T(8,128)(2,1)S(1)}, u32[]{:S(2)}, u32[]{:S(2)}) %collective-permute-start.19) | collective-permute-done | bytes 69664 | tf_op jit(solution)/shard_map/ppermute | solution.py:998
  178.0 1.9 collective-permute-done.20
  180.0 0.6 copy-done.11
  180.9 0.7 collective-permute-start.21
  181.6 1.1 add_convert_fusion.8
  182.6 0.7 collective-permute-start.24
  183.3 0.8 collective-permute-start.23
  184.1 2.9 %collective-permute-start.22 = (bf16[16,2176]{1,0:T(8,128)(2,1)S(1)}, bf16[16,2176]{1,0:T(8,128)(2,1)S(1)}, u32[]{:S(2)}, u32[]{:S(2)}) collective-permute-start(bf16[16,2176]{1,0:T(8,128)(2,1)S(1)} %add_convert_fusion.8), channel_id=1, source_target_pairs={{0,6},{1,7},{2,4},{3,5},{4,2},{5,3},{6,0},{7,1},{8,14},{9,15},{10,... | collective-permute-start | bytes 208904 | tf_op jit(solution)/shard_map/ppermute | solution.py:998
  187.1 1.5 collective-permute-done.24
  188.5 0.4 collective-permute-done.23
  188.9 1.3 collective-permute-done.22
  190.3 1.3 collective-permute-start.25
  191.7 5.3 %collective-permute-done.25 = bf16[64,2176]{1,0:T(8,128)(2,1)S(1)} collective-permute-done((bf16[64,2176]{1,0:T(8,128)(2,1)S(1)}, bf16[64,2176]{1,0:T(8,128)(2,1)S(1)}, u32[]{:S(2)}, u32[]{:S(2)}) %collective-permute-start.25) | collective-permute-done | bytes 278560 | tf_op jit(solution)/shard_map/ppermute | solution.py:998
  196.9 1.8 collective-permute-done.21
  198.7 0.5 maximum_select_fusion.mine_u.mine_d
  199.4 0.7 collective-permute-start.26
  200.0 3.4 %collective-permute-done.27.other_u.other_d = bf16[256,4096]{1,0:T(8,128)(2,1)S(1)} collective-permute-done((bf16[256,4096]{1,0:T(8,128)(2,1)S(1)}, bf16[256,4096]{1,0:T(8,128)(2,1)S(1)}, u32[]{:S(2)}, u32[]{:S(2)}) %collective-permute-start.27) | collective-permute-done | bytes 2097184 | tf_op jit(solution)/shard_map/ppermute | solution.py:998
  203.4 4.0 %unpack_feed_forward.1 = (f32[512,2048]{1,0:T(8,128)}, f32[2048,512]{1,0:T(8,128)}) custom-call(s32[1]{0:T(128)} %bitcast.bit_ref.side_ref, bf16[256,4096]{1,0:T(8,128)(2,1)S(1)} %maximum_select_fusion.mine_u.mine_d, bf16[256,4096]{1,0:T(8,128)(2,1)S(1)} %collective-permute-done.27.other_u.other_d, bf16[256,4096]{1,0:T(8,128)(2,1)S(1)} %maximum_select_fusion.mine_u.mine_d, ...), custom_call_target="tpu_custom_call" | custom-call | flops 1000000 | bytes 100000 | tf_op jit(solution)/shard_map/unpack_feed_forward/pallas_call | solution.py:1554
  207.5 1.5 collective-permute-done.26
  209.3 2.1 %unpack_own.1 = (f32[512,1536]{1,0:T(8,128)}, f32[512,512]{1,0:T(8,128)}) custom-call(s32[1]{0:T(128)} %bitcast.bit_ref.side_ref, bf16[256,2176]{1,0:T(8,128)(2,1)S(1)} %maximum_select_fusion.1.part_ref.mine_v), custom_call_target="tpu_custom_call" | custom-call | flops 1000000 | bytes 100000 | tf_op jit(solution)/shard_map/unpack_own/pallas_call | solution.py:1577
  211.4 0.6 collective-permute-done.28.part_ref.other_v
  212.0 2.3 %unpack_rest.1 = (f32[512,1536]{1,0:T(8,128)}, f32[512,512]{1,0:T(8,128)}, f32[2,512]{1,0:T(2,128)}, f32[2,512]{1,0:T(2,128)}, f32[2,512]{1,0:T(2,128)}, /*index...) custom-call(s32[1]{0:T(128)S(6)} %sub.3.side_ref, ...), custom_call_target="tpu_custom_call", output_to_operand_aliasing={{0}: (4, {}), {1}: (5, {})} | custom-call | flops 1000000 | bytes 100000 | tf_op jit(solution)/shard_map/unpack_rest/pallas_call | solution.py:1589
  (52 shorter events, 1.6 us)
Async XLA Ops:
  1.7 13.9 %collective-permute-start = (bf16[4,96,512]{2,1,0:T(8,128)(2,1)S(1)}, bf16[4,96,512]{2,1,0:T(8,128)(2,1)S(1)}, u32[]{:S(2)}, u32[]{:S(2)}) collective-permute-start(bf16[4,96,512]{2,1,0:T(8,128)(2,1)S(1)} %slice.8), channel_id=1, source_target_pairs={{0,1},{1,2},{2,3},{3,4},{4,5},{5,6},{6,7},{8,9},{9,10},{10,11},{11... | collective-permute-start | bytes 1179656 | tf_op jit(solution)/shard_map/ppermute | solution.py:964
  4.9 10.6 %collective-permute-start.1 = (bf16[4,16,512]{2,1,0:T(8,128)(2,1)S(1)}, bf16[4,16,512]{2,1,0:T(8,128)(2,1)S(1)}, u32[]{:S(2)}, u32[]{:S(2)}) collective-permute-start(bf16[4,16,512]{2,1,0:T(8,128)(2,1)S(1)} %slice.9), channel_id=1, source_target_pairs={{1,0},{2,1},{3,2},{4,3},{5,4},{6,5},{7,6},{9,8},{10,9},{11,10},{12... | collective-permute-start | bytes 196616 | tf_op jit(solution)/shard_map/ppermute | solution.py:964
  15.6 0.6 copy-start.13
  15.6 0.7 copy-start.5
  74.6 10.6 %collective-permute-start.2 = (bf16[256,4096]{1,0:T(8,128)(2,1)}, bf16[256,4096]{1,0:T(8,128)(2,1)}, u32[]{:S(2)}, u32[]{:S(2)}) collective-permute-start(bf16[256,4096]{1,0:T(8,128)(2,1)} %get-tuple-element.120), channel_id=1, source_target_pairs={{0,1},{1,0},{2,3},{3,2},{4,5},{5,4},{6,7},{7,6},{8,9},{9,8},{10,11... | collective-permute-start | bytes 6291464 | tf_op jit(solution)/shard_map/ppermute | solution.py:998
  77.9 7.2 %copy-start = (bf16[256,4096]{1,0:T(8,128)(2,1)S(1)}, bf16[256,4096]{1,0:T(8,128)(2,1)}, u32[]{:S(2)}) copy-start(bf16[256,4096]{1,0:T(8,128)(2,1)} %get-tuple-element.130) | copy-start | bytes 6291460
  85.1 3.1 %copy-start.14 = (bf16[4,16,1024]{2,1,0:T(8,128)(2,1)S(1)}, bf16[4,16,1024]{2,1,0:T(8,128)(2,1)}, u32[]{:S(2)}) copy-start(bf16[4,16,1024]{2,1,0:T(8,128)(2,1)} %get-tuple-element.133) | copy-start | bytes 393220
  86.7 15.0 %collective-permute-start.3 = (bf16[128,4096]{1,0:T(8,128)(2,1)S(1)}, bf16[128,4096]{1,0:T(8,128)(2,1)}, u32[]{:S(2)}, u32[]{:S(2)}) collective-permute-start(bf16[128,4096]{1,0:T(8,128)(2,1)S(1)} %add_convert_fusion), channel_id=1, source_target_pairs={{0,8},{1,17},{2,10},{3,19},{4,12},{5,21},{6,14},{7,23},{8,0},{9,25... | collective-permute-start | bytes 3145736 | tf_op jit(solution)/shard_map/ppermute | solution.py:998
  88.3 13.4 %collective-permute-start.4 = (bf16[4,16,1024]{2,1,0:T(8,128)(2,1)S(1)}, bf16[4,16,1024]{2,1,0:T(8,128)(2,1)S(1)}, u32[]{:S(2)}, u32[]{:S(2)}) collective-permute-start(bf16[4,16,1024]{2,1,0:T(8,128)(2,1)S(1)} %copy-done.14), channel_id=1, source_target_pairs={{1,0},{2,1},{3,2},{4,3},{5,4},{6,5},{7,6},{9,8},{10,9},{11,10},{12... | collective-permute-start | bytes 393224 | tf_op jit(solution)/shard_map/ppermute | solution.py:964
  101.6 3.2 %copy-start.6 = (bf16[4,16,1024]{2,1,0:T(8,128)(2,1)}, bf16[4,16,1024]{2,1,0:T(8,128)(2,1)S(1)}, u32[]{:S(2)}) copy-start(bf16[4,16,1024]{2,1,0:T(8,128)(2,1)S(1)} %collective-permute-done.4.refs_6_) | copy-start | bytes 393220
  103.3 11.6 %collective-permute-start.7 = (bf16[64,4096]{1,0:T(8,128)(2,1)S(1)}, bf16[64,4096]{1,0:T(8,128)(2,1)S(1)}, u32[]{:S(2)}, u32[]{:S(2)}) collective-permute-start(bf16[64,4096]{1,0:T(8,128)(2,1)S(1)} %add_convert_fusion.2), channel_id=1, source_target_pairs={{0,16},{1,9},{2,18},{3,11},{4,20},{5,13},{6,22},{7,15},{8,24},{9,1... | collective-permute-start | bytes 1572872 | tf_op jit(solution)/shard_map/ppermute | solution.py:998
  116.6 14.5 %collective-permute-start.8 = (bf16[16,4096]{1,0:T(8,128)(2,1)S(1)}, bf16[16,4096]{1,0:T(8,128)(2,1)S(1)}, u32[]{:S(2)}, u32[]{:S(2)}) collective-permute-start(bf16[16,4096]{1,0:T(8,128)(2,1)S(1)} %get-tuple-element.204), channel_id=1, source_target_pairs={{0,4},{1,5},{2,6},{3,7},{4,0},{5,1},{6,2},{7,3},{8,12},{9,13},{10,... | collective-permute-start | bytes 393224 | tf_op jit(solution)/shard_map/ppermute | solution.py:998
  119.5 11.7 %collective-permute-start.9 = (bf16[16,4096]{1,0:T(8,128)(2,1)S(1)}, bf16[16,4096]{1,0:T(8,128)(2,1)S(1)}, u32[]{:S(2)}, u32[]{:S(2)}) collective-permute-start(bf16[16,4096]{1,0:T(8,128)(2,1)S(1)} %get-tuple-element.203), channel_id=1, source_target_pairs={{0,2},{1,3},{2,0},{3,1},{4,6},{5,7},{6,4},{7,5},{8,10},{9,11},{10,... | collective-permute-start | bytes 393224 | tf_op jit(solution)/shard_map/ppermute | solution.py:998
  121.1 10.1 %collective-permute-start.10 = (bf16[16,4096]{1,0:T(8,128)(2,1)S(1)}, bf16[16,4096]{1,0:T(8,128)(2,1)S(1)}, u32[]{:S(2)}, u32[]{:S(2)}) collective-permute-start(bf16[16,4096]{1,0:T(8,128)(2,1)S(1)} %get-tuple-element.202), channel_id=1, source_target_pairs={{0,6},{1,7},{2,4},{3,5},{4,2},{5,3},{6,0},{7,1},{8,14},{9,15},{10,... | collective-permute-start | bytes 393224 | tf_op jit(solution)/shard_map/ppermute | solution.py:998
  121.1 16.0 %collective-permute-start.5 = (bf16[4,32,1024]{2,1,0:T(8,128)(2,1)}, bf16[4,32,1024]{2,1,0:T(8,128)(2,1)S(1)}, u32[]{:S(2)}, u32[]{:S(2)}) collective-permute-start(bf16[4,32,1024]{2,1,0:T(8,128)(2,1)} %get-tuple-element.138), channel_id=1, source_target_pairs={{1,0},{2,1},{3,2},{4,3},{5,4},{6,5},{7,6},{9,8},{10,9},{11,10},{12... | collective-permute-start | bytes 786440 | tf_op jit(solution)/shard_map/ppermute | solution.py:964
  122.4 14.7 %collective-permute-start.6 = (bf16[4,16,1024]{2,1,0:T(8,128)(2,1)}, bf16[4,16,1024]{2,1,0:T(8,128)(2,1)S(1)}, u32[]{:S(2)}, u32[]{:S(2)}) collective-permute-start(bf16[4,16,1024]{2,1,0:T(8,128)(2,1)} %get-tuple-element.139), channel_id=1, source_target_pairs={{0,1},{1,2},{2,3},{3,4},{4,5},{5,6},{6,7},{8,9},{9,10},{10,11},{11... | collective-permute-start | bytes 393224 | tf_op jit(solution)/shard_map/ppermute | solution.py:964
  132.4 13.8 %collective-permute-start.11 = (bf16[16,4096]{1,0:T(8,128)(2,1)S(1)}, bf16[16,4096]{1,0:T(8,128)(2,1)S(1)}, u32[]{:S(2)}, u32[]{:S(2)}) collective-permute-start(bf16[16,4096]{1,0:T(8,128)(2,1)S(1)} %add_convert_fusion.4), channel_id=1, source_target_pairs={{0,4},{1,5},{2,6},{3,7},{4,0},{5,1},{6,2},{7,3},{8,12},{9,13},{10,... | collective-permute-start | bytes 393224 | tf_op jit(solution)/shard_map/ppermute | solution.py:998
  135.5 11.2 %collective-permute-start.12 = (bf16[16,4096]{1,0:T(8,128)(2,1)S(1)}, bf16[16,4096]{1,0:T(8,128)(2,1)S(1)}, u32[]{:S(2)}, u32[]{:S(2)}) collective-permute-start(bf16[16,4096]{1,0:T(8,128)(2,1)S(1)} %add_convert_fusion.4), channel_id=1, source_target_pairs={{0,2},{1,3},{2,0},{3,1},{4,6},{5,7},{6,4},{7,5},{8,10},{9,11},{10,... | collective-permute-start | bytes 393224 | tf_op jit(solution)/shard_map/ppermute | solution.py:998
  136.8 9.9 %collective-permute-start.13 = (bf16[16,4096]{1,0:T(8,128)(2,1)S(1)}, bf16[16,4096]{1,0:T(8,128)(2,1)S(1)}, u32[]{:S(2)}, u32[]{:S(2)}) collective-permute-start(bf16[16,4096]{1,0:T(8,128)(2,1)S(1)} %add_convert_fusion.4), channel_id=1, source_target_pairs={{0,6},{1,7},{2,4},{3,5},{4,2},{5,3},{6,0},{7,1},{8,14},{9,15},{10,... | collective-permute-start | bytes 393224 | tf_op jit(solution)/shard_map/ppermute | solution.py:998
  137.1 0.7 copy-start.4
  137.1 0.7 copy-start.2
  146.7 2.8 %collective-permute-start.14 = (bf16[256,2176]{1,0:T(8,128)(2,1)S(1)}, bf16[256,2176]{1,0:T(8,128)(2,1)S(1)}, u32[]{:S(2)}, u32[]{:S(2)}) collective-permute-start(bf16[256,2176]{1,0:T(8,128)(2,1)S(1)} %get-tuple-element.168), channel_id=1, source_target_pairs={{0,1},{1,0},{2,3},{3,2},{4,5},{5,4},{6,7},{7,6},{8,9},{9,8},{10,11... | collective-permute-start | bytes 3342344 | tf_op jit(solution)/shard_map/ppermute | solution.py:998
  149.5 11.6 %copy-start.1 = (bf16[256,2176]{1,0:T(8,128)(2,1)}, bf16[256,2176]{1,0:T(8,128)(2,1)S(1)}, u32[]{:S(2)}) copy-start(bf16[256,2176]{1,0:T(8,128)(2,1)S(1)} %collective-permute-done.14) | copy-start | bytes 3342340
  149.6 11.4 %collective-permute-start.15 = (bf16[128,2176]{1,0:T(8,128)(2,1)S(1)}, bf16[128,2176]{1,0:T(8,128)(2,1)S(1)}, u32[]{:S(2)}, u32[]{:S(2)}) collective-permute-start(bf16[128,2176]{1,0:T(8,128)(2,1)S(1)} %add_convert_fusion.1), channel_id=1, source_target_pairs={{0,8},{1,17},{2,10},{3,19},{4,12},{5,21},{6,14},{7,23},{8,0},{9,25... | collective-permute-start | bytes 1671176 | tf_op jit(solution)/shard_map/ppermute | solution.py:998
  161.0 18.9 %copy-start.3 = (bf16[128,2176]{1,0:T(8,128)(2,1)}, bf16[128,2176]{1,0:T(8,128)(2,1)S(1)}, u32[]{:S(2)}) copy-start(bf16[128,2176]{1,0:T(8,128)(2,1)S(1)} %collective-permute-done.15) | copy-start | bytes 1671172
  161.2 6.6 %collective-permute-start.16 = (bf16[64,2176]{1,0:T(8,128)(2,1)S(1)}, bf16[64,2176]{1,0:T(8,128)(2,1)S(1)}, u32[]{:S(2)}, u32[]{:S(2)}) collective-permute-start(bf16[64,2176]{1,0:T(8,128)(2,1)S(1)} %add_convert_fusion.3), channel_id=1, source_target_pairs={{0,16},{1,9},{2,18},{3,11},{4,20},{5,13},{6,22},{7,15},{8,24},{9,1... | collective-permute-start | bytes 835592 | tf_op jit(solution)/shard_map/ppermute | solution.py:998
  168.0 12.6 %collective-permute-start.17 = (bf16[64,4096]{1,0:T(8,128)(2,1)S(1)}, bf16[64,4096]{1,0:T(8,128)(2,1)S(1)}, u32[]{:S(2)}, u32[]{:S(2)}) collective-permute-start(bf16[64,4096]{1,0:T(8,128)(2,1)S(1)} %maximum_select_fusion.4), channel_id=1, source_target_pairs={{0,16},{1,9},{2,18},{3,11},{4,20},{5,13},{6,22},{7,15},{8,24},{9,1... | collective-permute-start | bytes 1572872 | tf_op jit(solution)/shard_map/ppermute | solution.py:998
  170.2 5.5 %collective-permute-start.18 = (bf16[16,2176]{1,0:T(8,128)(2,1)S(1)}, bf16[16,2176]{1,0:T(8,128)(2,1)S(1)}, u32[]{:S(2)}, u32[]{:S(2)}) collective-permute-start(bf16[16,2176]{1,0:T(8,128)(2,1)S(1)} %get-tuple-element.207), channel_id=1, source_target_pairs={{0,4},{1,5},{2,6},{3,7},{4,0},{5,1},{6,2},{7,3},{8,12},{9,13},{10,... | collective-permute-start | bytes 208904 | tf_op jit(solution)/shard_map/ppermute | solution.py:998
  173.1 5.0 %collective-permute-start.19 = (bf16[16,2176]{1,0:T(8,128)(2,1)S(1)}, bf16[16,2176]{1,0:T(8,128)(2,1)S(1)}, u32[]{:S(2)}, u32[]{:S(2)}) collective-permute-start(bf16[16,2176]{1,0:T(8,128)(2,1)S(1)} %get-tuple-element.206), channel_id=1, source_target_pairs={{0,2},{1,3},{2,0},{3,1},{4,6},{5,7},{6,4},{7,5},{8,10},{9,11},{10,... | collective-permute-start | bytes 208904 | tf_op jit(solution)/shard_map/ppermute | solution.py:998
  173.9 6.1 %collective-permute-start.20 = (bf16[16,2176]{1,0:T(8,128)(2,1)S(1)}, bf16[16,2176]{1,0:T(8,128)(2,1)S(1)}, u32[]{:S(2)}, u32[]{:S(2)}) collective-permute-start(bf16[16,2176]{1,0:T(8,128)(2,1)S(1)} %get-tuple-element.205), channel_id=1, source_target_pairs={{0,6},{1,7},{2,4},{3,5},{4,2},{5,3},{6,0},{7,1},{8,14},{9,15},{10,... | collective-permute-start | bytes 208904 | tf_op jit(solution)/shard_map/ppermute | solution.py:998
  175.7 4.3 %copy-start.7 = (bf16[16,2176]{1,0:T(8,128)(2,1)}, bf16[16,2176]{1,0:T(8,128)(2,1)S(1)}, u32[]{:S(2)}) copy-start(bf16[16,2176]{1,0:T(8,128)(2,1)S(1)} %collective-permute-done.18) | copy-start | bytes 208900
  178.0 1.9 copy-start.9
  180.0 0.6 copy-start.11
  180.6 0.9 copy-start.8
  180.6 0.9 copy-start.10
  180.6 0.9 copy-start.12
  180.9 17.8 %collective-permute-start.21 = (bf16[128,4096]{1,0:T(8,128)(2,1)S(1)}, bf16[128,4096]{1,0:T(8,128)(2,1)S(1)}, u32[]{:S(2)}, u32[]{:S(2)}) collective-permute-start(bf16[128,4096]{1,0:T(8,128)(2,1)S(1)} %maximum_select_fusion.2), channel_id=1, source_target_pairs={{0,8},{1,17},{2,10},{3,19},{4,12},{5,21},{6,14},{7,23},{8,0},{9,25... | collective-permute-start | bytes 3145736 | tf_op jit(solution)/shard_map/ppermute | solution.py:998
  182.6 5.9 %collective-permute-start.24 = (bf16[16,2176]{1,0:T(8,128)(2,1)S(1)}, bf16[16,2176]{1,0:T(8,128)(2,1)S(1)}, u32[]{:S(2)}, u32[]{:S(2)}) collective-permute-start(bf16[16,2176]{1,0:T(8,128)(2,1)S(1)} %add_convert_fusion.8), channel_id=1, source_target_pairs={{0,4},{1,5},{2,6},{3,7},{4,0},{5,1},{6,2},{7,3},{8,12},{9,13},{10,... | collective-permute-start | bytes 208904 | tf_op jit(solution)/shard_map/ppermute | solution.py:998
  183.3 5.6 %collective-permute-start.23 = (bf16[16,2176]{1,0:T(8,128)(2,1)S(1)}, bf16[16,2176]{1,0:T(8,128)(2,1)S(1)}, u32[]{:S(2)}, u32[]{:S(2)}) collective-permute-start(bf16[16,2176]{1,0:T(8,128)(2,1)S(1)} %add_convert_fusion.8), channel_id=1, source_target_pairs={{0,2},{1,3},{2,0},{3,1},{4,6},{5,7},{6,4},{7,5},{8,10},{9,11},{10,... | collective-permute-start | bytes 208904 | tf_op jit(solution)/shard_map/ppermute | solution.py:998
  184.1 6.1 %collective-permute-start.22 = (bf16[16,2176]{1,0:T(8,128)(2,1)S(1)}, bf16[16,2176]{1,0:T(8,128)(2,1)S(1)}, u32[]{:S(2)}, u32[]{:S(2)}) collective-permute-start(bf16[16,2176]{1,0:T(8,128)(2,1)S(1)} %add_convert_fusion.8), channel_id=1, source_target_pairs={{0,6},{1,7},{2,4},{3,5},{4,2},{5,3},{6,0},{7,1},{8,14},{9,15},{10,... | collective-permute-start | bytes 208904 | tf_op jit(solution)/shard_map/ppermute | solution.py:998
  190.3 6.6 %collective-permute-start.25 = (bf16[64,2176]{1,0:T(8,128)(2,1)S(1)}, bf16[64,2176]{1,0:T(8,128)(2,1)S(1)}, u32[]{:S(2)}, u32[]{:S(2)}) collective-permute-start(bf16[64,2176]{1,0:T(8,128)(2,1)S(1)} %maximum_select_fusion.7), channel_id=1, source_target_pairs={{0,16},{1,9},{2,18},{3,11},{4,20},{5,13},{6,22},{7,15},{8,24},{9,1... | collective-permute-start | bytes 835592 | tf_op jit(solution)/shard_map/ppermute | solution.py:998
  199.2 4.2 %collective-permute-start.27 = (bf16[256,4096]{1,0:T(8,128)(2,1)S(1)}, bf16[256,4096]{1,0:T(8,128)(2,1)S(1)}, u32[]{:S(2)}, u32[]{:S(2)}) collective-permute-start(bf16[256,4096]{1,0:T(8,128)(2,1)S(1)} %maximum_select_fusion.mine_u.mine_d), channel_id=1, source_target_pairs={{0,1},{1,0},{2,3},{3,2},{4,5},{5,4},{6,7},{7,6},{8,9},{9,8},{10,11... | collective-permute-start | bytes 6291464 | tf_op jit(solution)/shard_map/ppermute | solution.py:998
  199.4 9.6 %collective-permute-start.26 = (bf16[128,2176]{1,0:T(8,128)(2,1)S(1)}, bf16[128,2176]{1,0:T(8,128)(2,1)S(1)}, u32[]{:S(2)}, u32[]{:S(2)}) collective-permute-start(bf16[128,2176]{1,0:T(8,128)(2,1)S(1)} %maximum_select_fusion.3), channel_id=1, source_target_pairs={{0,8},{1,17},{2,10},{3,19},{4,12},{5,21},{6,14},{7,23},{8,0},{9,25... | collective-permute-start | bytes 1671176 | tf_op jit(solution)/shard_map/ppermute | solution.py:998
  209.2 2.8 %collective-permute-start.28 = (bf16[256,2176]{1,0:T(8,128)(2,1)S(1)}, bf16[256,2176]{1,0:T(8,128)(2,1)S(1)}, u32[]{:S(2)}, u32[]{:S(2)}) collective-permute-start(bf16[256,2176]{1,0:T(8,128)(2,1)S(1)} %maximum_select_fusion.1.part_ref.mine_v), channel_id=1, source_target_pairs={{0,1},{1,0},{2,3},{3,2},{4,5},{5,4},{6,7},{7,6},{8,9},{9,8},{10,11... | collective-permute-start | bytes 3342344 | tf_op jit(solution)/shard_map/ppermute | solution.py:998
